TPU v7x, 32 devices: a whole 2x2x4 slice. The times are simulated.
32 devices in a mesh: tok: 8 (over y, x, core), exp: 4 (over z).
Axes of the slice: x: 2, y: 2, z: 4, core: 2. Of those that a mesh axis runs over, the one named last changes fastest.
Arguments:
- tokens: bfloat16 [128, 6144], P('tok', 'exp'), may hold values from -6 to 6
- route_ids: int32 [128, 2], P('tok'), may hold values from 0 to 3, all different within a row; in each aligned block of 16 rows (0 to 15, 16 to 31, ...) at most 12 rows name the same one
- gate_codes: int32 [128, 2], P('tok'), may hold values from 1 to 255
- merge_labels: int32 [4], replicated, may hold values from 0 to 1, as said below
- freq_counts: int32 [4], replicated, may hold values from 1024 to 4096
- w_gate: bfloat16 [32768, 6144], P(('tok', 'exp')), may hold values from -0.078125 to 0.078125
- w_up: bfloat16 [32768, 6144], P(('tok', 'exp')), may hold values from -0.078125 to 0.078125
- w_down: bfloat16 [32768, 6144], P('tok', 'exp'), may hold values from -0.0625 to 0.0625
Outputs:
- initial_out: bfloat16 [128, 6144], P('tok', 'exp')
- merged_out: bfloat16 [128, 6144], P('tok', 'exp')
Inputs may be any that keep to these rules, and one draw needn't show every extreme that they name: `route_ids`: the 2 ids of a row differ. Among the 16 rows of one token shard no expert is named more than 12 times, a bound that some block reaches. `merge_labels`: experts with equal labels form one merge group; every group has exactly two experts.
All inputs are finite; a program needn't handle non-finite values.
Results may differ from a plain program's by a relative error of at most 0.0085.
Values may be sent and summed in bfloat16 or wider, within the bound.
No kernel may reach another device: no remote copies, remote signals or barrier semaphores. Data moves between devices by JAX's collectives and lax.ppermute only.
A program may use at most 256 MiB of HBM per device.

v0:
```python
import jax
import jax.numpy as jnp
from jax import lax
from jax.sharding import PartitionSpec as P

EXPERTS = 4
TOP = 2
CAP = 12


def passed_along(value, axis, by):
    devices = lax.axis_size(axis)
    return lax.ppermute(value, axis, [(i, (i + by) % devices) for i in range(devices)])


def local(tokens, route_ids, gate_codes, merge_labels, freq_counts, w_gate, w_up, w_down):
    n_tok = lax.axis_size("tok")
    span = n_tok // EXPERTS
    expert = lax.axis_index("tok") // span
    tok_dev = tokens.shape[0]
    width = tokens.shape[1]
    flat = route_ids.reshape(-1)
    labels_idx = jnp.arange(EXPERTS, dtype=jnp.int32)
    picked = (flat[:, None] == labels_idx[None, :]).astype(jnp.int32)
    before = jnp.cumsum(picked, axis=0) - picked
    slot = jnp.sum(before * picked, axis=1)
    places = jnp.arange(CAP, dtype=jnp.int32)
    landing = picked.T[:, None, :] * (slot[None, None, :] == places[None, :, None]).astype(
        jnp.int32
    )
    landing = landing.reshape(EXPERTS, CAP, tok_dev, TOP)
    scale = gate_codes.astype(jnp.float32) / 256.0
    place_map = jnp.sum(landing, axis=3).astype(jnp.bfloat16)
    weighted = jnp.sum(landing.astype(jnp.float32) * scale[None, None, :, :], axis=3)
    packed = jnp.einsum(
        "ecn,nd->ecd", place_map, tokens, preferred_element_type=jnp.float32
    ).astype(jnp.bfloat16)
    copies = jnp.repeat(packed, span, axis=0)
    arrived = lax.all_to_all(copies, "tok", split_axis=0, concat_axis=0, tiled=True)
    rows_part = arrived.reshape(n_tok * CAP, width)
    rows = lax.all_gather(rows_part, "exp", axis=1, tiled=True)

    def project(gate_w, up_w, down_w):
        gate = jnp.einsum("sd,fd->sf", rows, gate_w, preferred_element_type=jnp.float32)
        upper = jnp.einsum("sd,fd->sf", rows, up_w, preferred_element_type=jnp.float32)
        hidden = (jax.nn.silu(gate) * upper).astype(jnp.bfloat16)
        units = lax.all_gather(hidden, "exp", axis=1, tiled=True)
        return jnp.dot(units, down_w, preferred_element_type=jnp.float32)

    first = project(w_gate, w_up, w_down)
    freq = freq_counts.astype(jnp.float32)
    own_label = jnp.sum(jnp.where(labels_idx == expert, merge_labels, 0))
    member = jnp.where(merge_labels == own_label, freq, jnp.float32(0.0))
    coef = member / jnp.sum(member)

    def weight_of(source):
        return jnp.sum(jnp.where(labels_idx == source, coef, jnp.float32(0.0)))

    own_weight = weight_of(expert)
    accums = (
        own_weight * w_gate.astype(jnp.float32),
        own_weight * w_up.astype(jnp.float32),
        own_weight * w_down.astype(jnp.float32),
    )
    for offset in range(1, EXPERTS):
        peers = passed_along((w_gate, w_up, w_down), "tok", offset * span)
        factor = weight_of((expert - offset) % EXPERTS)
        accums = (
            accums[0] + factor * peers[0].astype(jnp.float32),
            accums[1] + factor * peers[1].astype(jnp.float32),
            accums[2] + factor * peers[2].astype(jnp.float32),
        )
    second = project(
        accums[0].astype(jnp.bfloat16),
        accums[1].astype(jnp.bfloat16),
        accums[2].astype(jnp.bfloat16),
    )
    stacked = jnp.stack(
        [first.reshape(n_tok, CAP, width), second.reshape(n_tok, CAP, width)], axis=0
    )
    backs = lax.all_to_all(
        stacked.astype(jnp.bfloat16), "tok", split_axis=1, concat_axis=1, tiled=True
    ).astype(stacked.dtype)
    totals = jnp.sum(backs.reshape(2, EXPERTS, span, CAP, width), axis=2)
    final = jnp.einsum(
        "ecn,xecd->xnd",
        weighted,
        totals,
        precision=lax.Precision.HIGHEST,
        preferred_element_type=jnp.float32,
    )
    return (final[0].astype(jnp.bfloat16), final[1].astype(jnp.bfloat16))


def solution(mesh):
    return jax.shard_map(
        local,
        mesh=mesh,
        in_specs=(
            P("tok", "exp"),
            P("tok", None),
            P("tok", None),
            P(),
            P(),
            P(("tok", "exp"), None),
            P(("tok", "exp"), None),
            P("tok", "exp"),
        ),
        out_specs=(P("tok", "exp"), P("tok", "exp")),
        check_vma=False,
    )
```

profile of v0, /device:TPU:0, one launch (start us, length us, event | category | flops | bytes accessed | tf_op | source)
XLA Modules:
  0.0 1811.9 jit_solution(13832626158747803228)
XLA Ops:
  7.2 0.0 copy-start
  7.2 0.0 all-gather.2.cloned.1.call-start
  7.2 3.0 collective-permute-start
  10.2 1.0 collective-permute-start.2
  11.2 1.9 collective-permute-start.1
  13.2 0.6 collective-permute-start.3
  13.8 2.3 collective-permute-start.5
  16.1 266.5 %collective-permute-done = bf16[1024,6144]{1,0:T(8,128)(2,1)S(1)} collective-permute-done((bf16[1024,6144]{1,0:T(8,128)(2,1)}, bf16[1024,6144]{1,0:T(8,128)(2,1)S(1)}, u32[]{:S(2)}, u32[]{:S(2)}) %collective-permute-start) | collective-permute-done | bytes 12582944 | tf_op jit(solution)/shard_map/ppermute | solution.py:13
  282.6 4.5 copy-done.4
  287.1 2.0 collective-permute-start.4
  289.1 0.8 copy.25
  289.9 0.1 eq.85
  290.0 262.9 %collective-permute-done.2 = bf16[1024,6144]{1,0:T(8,128)(2,1)} collective-permute-done((bf16[1024,6144]{1,0:T(8,128)(2,1)}, bf16[1024,6144]{1,0:T(8,128)(2,1)}, u32[]{:S(2)}, u32[]{:S(2)}) %collective-permute-start.2) | collective-permute-done | bytes 12582944 | tf_op jit(solution)/shard_map/ppermute | solution.py:13
  552.9 1.5 collective-permute-start.6
  554.4 0.0 collective-permute-done.1
  554.4 1.6 collective-permute-start.8
  556.0 266.0 %collective-permute-done.3 = bf16[1024,6144]{1,0:T(8,128)(2,1)} collective-permute-done((bf16[1024,6144]{1,0:T(8,128)(2,1)}, bf16[1024,6144]{1,0:T(8,128)(2,1)}, u32[]{:S(2)}, u32[]{:S(2)}) %collective-permute-start.3) | collective-permute-done | bytes 12582944 | tf_op jit(solution)/shard_map/ppermute | solution.py:13
  822.0 2.0 collective-permute-start.7
  824.1 0.1 fusion.13
  824.1 0.1 reduce_window_sum.11
  824.2 0.2 select_reduce_fusion
  824.4 0.1 eq.89
  824.5 0.1 copy.26
  824.6 0.7 fusion.14
  825.3 0.0 copy-done
  825.3 0.2 convolution_convert_fusion.1
  825.5 808.9 %all_to_all.10 = bf16[8,12,1536]{2,1,0:T(8,128)(2,1)S(1)} all-to-all(bf16[8,12,1536]{2,1,0:T(8,128)(2,1)S(1)} %bitcast.34), channel_id=1, replica_groups=mesh['tok'=8,'exp'=4] {'tok'}, dimensions={0} | all-to-all | bytes 589824 | tf_op jit(solution)/shard_map/all_to_all | solution.py:39
  1634.4 0.8 reshape.75
  1635.2 0.0 all-gather.2.cloned.1.call-update
  1635.3 1.3 fusion.15
  1636.6 1.9 fusion.20
  1638.5 2.6 fusion.16
  1641.1 26.5 %all-gather.2.cloned.1.call-done = bf16[96,6144]{1,0:T(8,128)(2,1)} async-done(((bf16[96,1536]{1,0:T(8,128)(2,1)}), bf16[96,6144]{1,0:T(8,128)(2,1)}) %all-gather.2.cloned.1.call-update) | async-done | bytes 1179664 | tf_op jit(solution)/shard_map/all_gather | solution.py:41
  1667.6 9.1 fusion.21
  1676.7 0.0 copy-done.2
  1676.7 0.0 slice-start.2
  1676.7 8.7 fusion.6
  1685.4 18.3 %all_gather.10 = bf16[96,4096]{1,0:T(8,128)(2,1)S(1)} all-gather(bf16[96,1024]{1,0:T(8,128)(2,1)S(1)} %fusion.6), channel_id=1, replica_groups=mesh['tok'=8,'exp'=4] {'exp'}, dimensions={1}, use_global_device_ids=true | all-gather | bytes 983040 | tf_op jit(solution)/shard_map/all_gather | solution.py:47
  1703.7 0.0 slice-done
  1703.7 0.0 slice-done.1
  1703.7 0.0 slice-done.2
  1703.7 2.1 convolution_convert_fusion
  1705.9 0.1 stack_reshape.8
  1705.9 21.5 %fusion = f32[96,1024]{1,0:T(8,128)S(1)} fusion(bf16[96,6144]{1,0:T(8,128)(2,1)S(1)} %copy-done.2, bf16[1024,6144]{1,0:T(8,128)(2,1)} %collective-permute-done.2, bf16[1024,6144]{1,0:T(8,128)(2,1)} %collective-permute-done.1, bf16[1024,6144]{1,0:T(8,128)(2,1)} %copy-done.4, bf16[1024,6144]{1,0:T(8,128)(2,1)} %param.13, f32[]{:T(128)} %get-tuple-element.3, ...), kind=kOutput, calls=%fused_computation.3 | convolution fusion | flops 1283457024 | bytes 51904528 | tf_op jit(solution)/shard_map/sd,fd->sf/dot_general | solution.py:44
  1727.5 0.0 collective-permute-done.5
  1727.5 0.0 collective-permute-done.4
  1727.5 21.6 %multiply_convert_fusion = bf16[96,1024]{1,0:T(8,128)(2,1)S(1)} fusion(f32[96,1024]{1,0:T(8,128)S(1)} %fusion, bf16[96,6144]{1,0:T(8,128)(2,1)S(1)} %copy-done.2, bf16[1024,6144]{1,0:T(8,128)(2,1)} %collective-permute-done.5, bf16[1024,6144]{1,0:T(8,128)(2,1)} %collective-permute-done.4, bf16[1024,6144]{1,0:T(8,128)(2,1)} %collective-permute-done.3, ...), kind=kOutput, calls=%fused_computation.17 | convolution fusion | flops 1284046848 | bytes 52101136 | tf_op jit(solution)/shard_map/sd,fd->sf/dot_general | solution.py:45
  1749.1 17.6 all_gather.11
  1766.7 0.0 collective-permute-done.6
  1766.7 0.0 collective-permute-done.8
  1766.7 0.0 collective-permute-done.7
  1766.7 0.0 copy-start.1
  1766.7 20.7 %fusion.3 = bf16[96,1536]{1,0:T(8,128)(2,1)S(1)} fusion(bf16[96,4096]{1,0:T(8,128)(2,1)S(1)} %all_gather.11, bf16[4096,1536]{1,0:T(8,128)(2,1)} %collective-permute-done.8, bf16[4096,1536]{1,0:T(8,128)(2,1)} %collective-permute-done.7, bf16[4096,1536]{1,0:T(8,128)(2,1)} %collective-permute-done.6, bf16[4096,1536]{1,0:T(8,128)(2,1)} %param.15, ...), kind=kOutput, calls=%fused_computation.7 | convolution fusion | flops 1283604480 | bytes 51413008 | tf_op jit(solution)/shard_map/dot_general | solution.py:48
  1787.4 0.1 stack_reshape.9
  1787.5 0.1 pad_maximum_fusion
  1787.6 1.4 copy.28
  1789.0 3.7 all-to-all-start.1
  1792.6 0.0 copy-done.3
  1792.7 0.1 copy.30
  1792.8 10.3 all-to-all-done.1
  1803.1 0.7 convert_reduce_fusion
  1803.8 0.7 fusion.5
  1804.5 0.6 slice_bitcast_fusion
  1805.1 0.0 copy-done.1
  (12 shorter events, 0.1 us)
Async XLA Ops:
  7.2 818.1 %copy-start = (bf16[16,1536]{1,0:T(8,128)(2,1)S(1)}, bf16[16,1536]{1,0:T(8,128)(2,1)}, u32[]{:S(2)}) copy-start(bf16[16,1536]{1,0:T(8,128)(2,1)} %param.8) | copy-start | bytes 147460
  7.2 1660.4 %all-gather.2.cloned.1.call-start = ((), (), s32[]{:S(2)}) async-start(), calls=%async_computation.2 | async-start | bytes 1474560 | tf_op jit(solution)/shard_map/all_gather | solution.py:41
  7.2 275.4 %collective-permute-start = (bf16[1024,6144]{1,0:T(8,128)(2,1)}, bf16[1024,6144]{1,0:T(8,128)(2,1)S(1)}, u32[]{:S(2)}, u32[]{:S(2)}) collective-permute-start(bf16[1024,6144]{1,0:T(8,128)(2,1)} %param.13), channel_id=1, source_target_pairs={{0,8},{4,12},{8,16},{12,20},{16,24},{20,28},{24,0},{28,4},{1,9},{5... | collective-permute-start | bytes 37748744 | tf_op jit(solution)/shard_map/ppermute | solution.py:13
  10.2 542.7 %collective-permute-start.2 = (bf16[1024,6144]{1,0:T(8,128)(2,1)}, bf16[1024,6144]{1,0:T(8,128)(2,1)}, u32[]{:S(2)}, u32[]{:S(2)}) collective-permute-start(bf16[1024,6144]{1,0:T(8,128)(2,1)} %param.13), channel_id=1, source_target_pairs={{0,24},{4,28},{8,0},{12,4},{16,8},{20,12},{24,16},{28,20},{1,25},{... | collective-permute-start | bytes 37748744 | tf_op jit(solution)/shard_map/ppermute | solution.py:13
  11.2 543.2 %collective-permute-start.1 = (bf16[1024,6144]{1,0:T(8,128)(2,1)}, bf16[1024,6144]{1,0:T(8,128)(2,1)}, u32[]{:S(2)}, u32[]{:S(2)}) collective-permute-start(bf16[1024,6144]{1,0:T(8,128)(2,1)} %param.13), channel_id=1, source_target_pairs={{0,16},{4,20},{8,24},{12,28},{16,0},{20,4},{24,8},{28,12},{1,17},{... | collective-permute-start | bytes 37748744 | tf_op jit(solution)/shard_map/ppermute | solution.py:13
  13.2 808.9 %collective-permute-start.3 = (bf16[1024,6144]{1,0:T(8,128)(2,1)}, bf16[1024,6144]{1,0:T(8,128)(2,1)}, u32[]{:S(2)}, u32[]{:S(2)}) collective-permute-start(bf16[1024,6144]{1,0:T(8,128)(2,1)} %param.14), channel_id=1, source_target_pairs={{0,8},{4,12},{8,16},{12,20},{16,24},{20,28},{24,0},{28,4},{1,9},{5... | collective-permute-start | bytes 37748744 | tf_op jit(solution)/shard_map/ppermute | solution.py:13
  13.8 1713.7 %collective-permute-start.5 = (bf16[1024,6144]{1,0:T(8,128)(2,1)}, bf16[1024,6144]{1,0:T(8,128)(2,1)}, u32[]{:S(2)}, u32[]{:S(2)}) collective-permute-start(bf16[1024,6144]{1,0:T(8,128)(2,1)} %param.14), channel_id=1, source_target_pairs={{0,24},{4,28},{8,0},{12,4},{16,8},{20,12},{24,16},{28,20},{1,25},{... | collective-permute-start | bytes 37748744 | tf_op jit(solution)/shard_map/ppermute | solution.py:13
  282.6 4.5 copy-start.4
  287.1 1440.4 %collective-permute-start.4 = (bf16[1024,6144]{1,0:T(8,128)(2,1)}, bf16[1024,6144]{1,0:T(8,128)(2,1)}, u32[]{:S(2)}, u32[]{:S(2)}) collective-permute-start(bf16[1024,6144]{1,0:T(8,128)(2,1)} %param.14), channel_id=1, source_target_pairs={{0,16},{4,20},{8,24},{12,28},{16,0},{20,4},{24,8},{28,12},{1,17},{... | collective-permute-start | bytes 37748744 | tf_op jit(solution)/shard_map/ppermute | solution.py:13
  552.9 1213.8 %collective-permute-start.6 = (bf16[4096,1536]{1,0:T(8,128)(2,1)}, bf16[4096,1536]{1,0:T(8,128)(2,1)}, u32[]{:S(2)}, u32[]{:S(2)}) collective-permute-start(bf16[4096,1536]{1,0:T(8,128)(2,1)} %param.15), channel_id=1, source_target_pairs={{0,8},{4,12},{8,16},{12,20},{16,24},{20,28},{24,0},{28,4},{1,9},{5... | collective-permute-start | bytes 37748744 | tf_op jit(solution)/shard_map/ppermute | solution.py:13
  554.4 1212.3 %collective-permute-start.8 = (bf16[4096,1536]{1,0:T(8,128)(2,1)}, bf16[4096,1536]{1,0:T(8,128)(2,1)}, u32[]{:S(2)}, u32[]{:S(2)}) collective-permute-start(bf16[4096,1536]{1,0:T(8,128)(2,1)} %param.15), channel_id=1, source_target_pairs={{0,24},{4,28},{8,0},{12,4},{16,8},{20,12},{24,16},{28,20},{1,25},{... | collective-permute-start | bytes 37748744 | tf_op jit(solution)/shard_map/ppermute | solution.py:13
  822.0 944.7 %collective-permute-start.7 = (bf16[4096,1536]{1,0:T(8,128)(2,1)}, bf16[4096,1536]{1,0:T(8,128)(2,1)}, u32[]{:S(2)}, u32[]{:S(2)}) collective-permute-start(bf16[4096,1536]{1,0:T(8,128)(2,1)} %param.15), channel_id=1, source_target_pairs={{0,16},{4,20},{8,24},{12,28},{16,0},{20,4},{24,8},{28,12},{1,17},{... | collective-permute-start | bytes 37748744 | tf_op jit(solution)/shard_map/ppermute | solution.py:13
  1667.6 9.1 copy-start.2
  1667.6 36.1 %slice-start = ((s8[12582912]{0:T(1024)(128)(4,1)}), s8[4194304]{0:T(1024)(128)(4,1)S(1)}, s32[]{:S(2)}) async-start(s8[12582912]{0:T(1024)(128)(4,1)} %bitcast.32), calls=%async_computation.3 | async-start | bytes 8388608
  1667.6 36.1 %slice-start.1 = ((s8[12582912]{0:T(1024)(128)(4,1)}), s8[4194304]{0:T(1024)(128)(4,1)S(1)}, s32[]{:S(2)}) async-start(s8[12582912]{0:T(1024)(128)(4,1)} %bitcast.32), calls=%async_computation.4 | async-start | bytes 8388608
  1676.7 27.0 %slice-start.2 = ((s8[12582912]{0:T(1024)(128)(4,1)}), s8[4194304]{0:T(1024)(128)(4,1)S(1)}, s32[]{:S(2)}) async-start(s8[12582912]{0:T(1024)(128)(4,1)} %bitcast.32), calls=%async_computation.5 | async-start | bytes 8388608
  1766.7 26.0 %copy-start.3 = (s32[16,2]{0,1:T(2,128)S(1)}, s32[16,2]{0,1:T(2,128)}, u32[]{:S(2)}) copy-start(s32[16,2]{0,1:T(2,128)} %param.10) | copy-start | bytes 388
  1766.7 38.4 %copy-start.1 = (bf16[16,1536]{1,0:T(8,128)(2,1)S(1)}, bf16[16,1536]{1,0:T(8,128)(2,1)}, u32[]{:S(2)}) copy-start(bf16[16,1536]{1,0:T(8,128)(2,1)} %param.8) | copy-start | bytes 147460
  1789.0 14.1 all-to-all-start.1
Sparse Core Ops, SparseCore 0:
  1635.3 32.2 all-gather.1
where the time goes:
time: 1810 us
  blocking collectives  845 us (47%)
  waiting for transfers between devices  832 us (46%)
  matrix products  84.6 us (5%)
  starting transfers between devices  19.7 us (1%)
    all_to_all x1, blocking collectives, local(): lax.all_to_all(copies, 'tok', split_axis=0, concat_axis=0, tiled=True)  809 us
    ppermute x9, waiting for transfers between devices, passed_along(): lax.ppermute(value, axis, [(i, (i + by) % devices) for i in range(devices)])  795 us
  transfers between devices with their start and end apart: 11, of which 5 were waited for; matrix products, arithmetic and copies ran while one was open for 4% of the time, Pallas kernels for 0%

commit v1 on v0

v1 whole, which is shorter than its diff:
```python
import functools

import jax
import jax.numpy as jnp
from jax import lax
from jax.experimental import pallas as pl
from jax.experimental.pallas import tpu as pltpu
from jax.sharding import PartitionSpec as P

EXPERTS = 4
TOP = 2
CAP = 12
LANES = 128
UNITS = 256
VMEM_LIMIT = 16 << 20
F32 = jnp.float32
BF16 = jnp.bfloat16
NT = (((1,), (1,)), ((), ()))
IN_VMEM = pl.BlockSpec(memory_space=pltpu.VMEM)
IN_SMEM = pl.BlockSpec(memory_space=pltpu.SMEM)


def swapped(value, axis, by):
    devices = lax.axis_size(axis)
    return lax.ppermute(value, axis, [(i, i ^ by) for i in range(devices)])


def column(table, index):
    lane = lax.broadcasted_iota(jnp.int32, table.shape, 1)
    return jnp.sum(jnp.where(lane == index, table, 0.0), axis=1, keepdims=True)


def silu(v):
    return v / (1.0 + jnp.exp(-v))


def project_kernel(place, x, meta, gate_w, up_w, slots, acts, *, shard, n_exp):
    z, expert = place[0], place[1]
    tokens = x.shape[0]
    depth = x.shape[1] // n_exp
    units = gate_w.shape[0]
    step = min(UNITS, units)
    table = meta[...].astype(F32).T
    line = lax.broadcasted_iota(jnp.int32, table.shape, 0)
    slot = jnp.sum(jnp.where(line == expert, table, 0.0), axis=0, keepdims=True)
    token = lax.broadcasted_iota(jnp.int32, (1, tokens), 1)
    target = jnp.where(slot < 0, -1, (token // shard) * CAP + slot.astype(jnp.int32))
    rows = slots.shape[0]
    pick = (lax.broadcasted_iota(jnp.int32, (rows, tokens), 0) == target).astype(F32).astype(BF16)
    for first in range(0, units, step):
        sums = []
        for weight in (gate_w, up_w):
            total = None
            for k in range(n_exp):
                at = pl.multiple_of((z ^ k) * depth, LANES)
                part = lax.dot_general(
                    weight[first:first + step, pl.ds(at, depth)],
                    x[:, k * depth:(k + 1) * depth],
                    NT,
                    preferred_element_type=F32,
                )
                total = part if total is None else total + part
            sums.append(total)
        gate, upper = sums
        acts[0, first:first + step, :] = gate.astype(BF16)
        acts[1, first:first + step, :] = upper.astype(BF16)
        hidden = (silu(gate) * upper).T.astype(BF16)
        slots[:, first:first + step] = jnp.dot(
            pick, hidden, preferred_element_type=F32
        ).astype(BF16)


def merge_kernel(coefs, own, peer, hidden, *, flip):
    tokens = own.shape[2]
    i = lax.broadcasted_iota(jnp.int32, (tokens, tokens), 0)
    j = lax.broadcasted_iota(jnp.int32, (tokens, tokens), 1)
    order = ((i ^ flip) == j).astype(F32).astype(BF16)
    mixed = []
    for which in range(2):
        theirs = jnp.dot(peer[which], order, preferred_element_type=F32)
        mixed.append(coefs[0] * own[which].astype(F32) + coefs[1] * theirs)
    hidden[...] = (silu(mixed[0]) * mixed[1]).T.astype(BF16)


def down_kernel(place, scale, meta, *refs, shard, packed):
    pieces, weight, out = refs[:-2], refs[-2], refs[-1]
    z, expert, other = place[0], place[1], place[2]
    n_exp = len(pieces)
    depth = weight.shape[0] // n_exp
    table = meta[...].astype(F32)
    tokens = table.shape[0]
    if packed:
        slot = column(table, expert)
        token = lax.broadcasted_iota(jnp.int32, (tokens, 1), 0)
        target = jnp.where(slot < 0, -1, (token // shard) * CAP + slot.astype(jnp.int32))
        rows = pieces[0].shape[0]
        spread = (lax.broadcasted_iota(jnp.int32, (tokens, rows), 1) == target).astype(F32).astype(BF16)
        factor = column(table, EXPERTS + expert)
    else:
        factor = (column(table, EXPERTS + expert) + column(table, EXPERTS + other)) * scale[0]
    total = None
    for k in range(n_exp):
        at = pl.multiple_of((z ^ k) * depth, 16)
        hidden = pieces[k][...]
        if packed:
            hidden = jnp.dot(spread, hidden, preferred_element_type=F32).astype(BF16)
        part = jnp.dot(hidden, weight[pl.ds(at, depth), :], preferred_element_type=F32)
        total = part if total is None else total + part
    out[...] = (total * factor).astype(out.dtype)


def params():
    return pltpu.CompilerParams(vmem_limit_bytes=VMEM_LIMIT)


def spread(value):
    devices = lax.axis_size("exp")
    return (value,) + tuple(swapped(value, "exp", k) for k in range(1, devices))


def exchange(pairing, coefs, slots, acts, *, shard):
    n_tok = lax.axis_size("tok")
    span = n_tok // EXPERTS
    units, all_tokens = acts.shape[1], acts.shape[2]
    with jax.named_scope("peer"):
        peer = swapped(acts, "tok", pairing * span)
    with jax.named_scope("spread_first"):
        first = spread(slots)
    hidden = pl.pallas_call(
        functools.partial(merge_kernel, flip=pairing * span // 2 * shard),
        in_specs=[IN_SMEM, IN_VMEM, IN_VMEM],
        out_specs=IN_VMEM,
        out_shape=jax.ShapeDtypeStruct((all_tokens, units), BF16),
        compiler_params=params(),
        name="merge",
    )(coefs, acts, peer)
    with jax.named_scope("spread_second"):
        second = spread(hidden)
    return first, second


def local(tokens, route_ids, gate_codes, merge_labels, freq_counts, w_gate, w_up, w_down):
    n_tok = lax.axis_size("tok")
    n_exp = lax.axis_size("exp")
    span = n_tok // EXPERTS
    t = lax.axis_index("tok")
    z = lax.axis_index("exp")
    expert = t // span
    shard = tokens.shape[0]
    all_tokens = n_tok * shard
    units = w_gate.shape[0]
    width = w_down.shape[1]
    experts = jnp.arange(EXPERTS, dtype=jnp.int32)
    flat = route_ids.reshape(-1)
    picked = flat[:, None] == experts[None, :]
    earlier = jnp.arange(shard * TOP)[:, None] > jnp.arange(shard * TOP)[None, :]
    before = jnp.sum(
        (earlier[:, :, None] & picked[None, :, :]).astype(F32), axis=1
    )
    slot = jnp.max(jnp.where(picked, before, -1.0).reshape(shard, TOP, EXPERTS), axis=1)
    scale = jnp.sum(
        jnp.where(
            route_ids[:, :, None] == experts[None, None, :],
            gate_codes.astype(F32)[:, :, None] / 256.0,
            0.0,
        ),
        axis=1,
    )
    notes = jnp.concatenate(
        [slot, scale, jnp.zeros((shard, LANES - 2 * EXPERTS), F32)], axis=1
    ).astype(BF16)
    mate = jnp.sum(
        jnp.where((merge_labels == merge_labels[0]) & (experts > 0), experts, 0)
    )
    freq = freq_counts.astype(F32)
    mine = jnp.sum(jnp.where(experts == expert, freq, 0.0))
    theirs = jnp.sum(jnp.where(experts == (expert ^ mate), freq, 0.0))
    coefs = jnp.stack([mine, theirs]) / (mine + theirs)
    place = jnp.stack([z, expert, expert ^ mate]).astype(jnp.int32)

    with jax.named_scope("gather_tokens"):
        row = jnp.concatenate(
            [tokens] + [swapped(tokens, "exp", k) for k in range(1, n_exp)] + [notes], axis=1
        )
        half = jnp.concatenate(
            [row] + [swapped(row, "tok", j) for j in range(2, n_tok, 2)], axis=0
        )
        rows = jnp.concatenate([half, swapped(half, "tok", 1)], axis=0)
        x = rows[:, :-LANES]
        meta = rows[:, -LANES:]

    slots, acts = pl.pallas_call(
        functools.partial(project_kernel, shard=shard, n_exp=n_exp),
        in_specs=[IN_SMEM] + [IN_VMEM] * 4,
        out_specs=[IN_VMEM, IN_VMEM],
        out_shape=[
            jax.ShapeDtypeStruct((n_tok * CAP, units), BF16),
            jax.ShapeDtypeStruct((2, units, all_tokens), BF16),
        ],
        compiler_params=params(),
        name="project",
    )(place, x, meta, w_gate, w_up)
    first, second = lax.switch(
        mate - 1,
        [functools.partial(exchange, pairing, shard=shard) for pairing in range(1, EXPERTS)],
        coefs,
        slots,
        acts,
    )

    def down(pieces, packed):
        return pl.pallas_call(
            functools.partial(down_kernel, shard=shard, packed=packed),
            in_specs=[IN_SMEM, IN_SMEM] + [IN_VMEM] * (len(pieces) + 2),
            out_specs=IN_VMEM,
            out_shape=jax.ShapeDtypeStruct((all_tokens, width), BF16),
            compiler_params=params(),
            name="down",
        )(place, coefs, meta, *pieces, w_down)

    outs = []
    for pieces, packed in ((first, True), (second, False)):
        part = down(pieces, packed)
        middle = all_tokens // 2
        with jax.named_scope("cores"):
            both = part[:middle].astype(F32) + swapped(part[middle:], "tok", 1).astype(F32)
        with jax.named_scope("chips"):
            total = both[:shard]
            sent = both.astype(BF16)
            for i in range(1, n_tok // 2):
                total = total + swapped(sent[i * shard:(i + 1) * shard], "tok", 2 * i).astype(F32)
        outs.append(total.astype(BF16))
    return tuple(outs)


def solution(mesh):
    return jax.shard_map(
        local,
        mesh=mesh,
        in_specs=(
            P("tok", "exp"),
            P("tok", None),
            P("tok", None),
            P(),
            P(),
            P(("tok", "exp"), None),
            P(("tok", "exp"), None),
            P("tok", "exp"),
        ),
        out_specs=(P("tok", "exp"), P("tok", "exp")),
        check_vma=False,
    )
```

time: 1810 us -> 130 us (0.07)
  blocking collectives: 845 us -> 0 us
  waiting for transfers between devices: 832 us -> 59.3 us
  matrix products: 84.6 us -> 0 us
    all_to_all x1 -> x0, blocking collectives: 809 us -> none  [local(): lax.all_to_all(copies, 'tok', split_axis=0, concat_axis=0, tiled=True)]
    ppermute x9 -> x22, waiting for transfers between devices: 795 us -> 59.3 us  [swapped(): return lax.ppermute(value, axis, [(i, i ^ by) for i in range(devices)])]
    dot_general x8 -> x0, matrix products: 84.6 us -> none  [the longest x2 30.6 us: project(): jnp.einsum('sd,fd->sf', rows, gate_w, preferred_element_type=jnp.float32)]
    all_gather x2 -> x0, blocking collectives: 35.8 us -> none  [project(): units = lax.all_gather(hidden, 'exp', axis=1, tiled=True)]
    all_gather x1 -> x0, waiting for transfers between devices: 26.5 us -> none  [local(): rows = lax.all_gather(rows_part, 'exp', axis=1, tiled=True)]
  transfers between devices with their start and end apart: 11 -> 22, of which waited for: 5 -> 8; matrix products, arithmetic and copies ran while one was open for 4% -> 6% of each run, Pallas kernels for 0% -> 4%
where the time goes in v1:
time: 130 us; the launch traced here: 129 us
  waiting for transfers between devices  59.3 us (46%)
  starting transfers between devices  27.1 us (21%)
  Pallas kernels  16.4 us (13%)
  local copies, waits for them, and re-layouts  16 us (12%)
  other arithmetic  7.02 us (5%)
  between operations  3.36 us (3%)
    ppermute x22, waiting for transfers between devices, swapped(): return lax.ppermute(value, axis, [(i, i ^ by) for i in range(devices)])  59.3 us
    ppermute x22, starting transfers between devices, swapped(): return lax.ppermute(value, axis, [(i, i ^ by) for i in range(devices)])  27.1 us
    unnamed x11, local copies, waits for them, and re-layouts  14.6 us
    pallas_call x1, Pallas kernels, local(): pl.pallas_call(functools.partial(project_kernel, shard=shard, n_exp=n_exp...  8.1 us
    pallas_call x2, Pallas kernels, down(): pl.pallas_call(functools.partial(down_kernel, shard=shard, packed=packed)...  6.53 us
  transfers between devices with their start and end apart: 22, of which 8 were waited for; matrix products, arithmetic and copies ran while one was open for 6% of the time, Pallas kernels for 4%

profile of v1, /device:TPU:0, one launch (start us, length us, event | category | flops | bytes accessed | tf_op | source)
XLA Modules:
  0.0 129.4 jit_solution(6193636506009156041)
XLA Ops:
  0.6 3.1 %collective-permute-start.21 = (bf16[16,1536]{1,0:T(8,128)(2,1)}, bf16[16,1536]{1,0:T(8,128)(2,1)S(1)}, u32[]{:S(2)}, u32[]{:S(2)}) collective-permute-start(bf16[16,1536]{1,0:T(8,128)(2,1)} %param.11), channel_id=1, source_target_pairs={{0,1},{1,0},{2,3},{3,2},{4,5},{5,4},{6,7},{7,6},{8,9},{9,8},{10,11... | collective-permute-start | bytes 147464 | tf_op jit(solution)/shard_map/gather_tokens/ppermute | solution.py:25
  3.7 2.6 %collective-permute-start.22 = (bf16[16,1536]{1,0:T(8,128)(2,1)}, bf16[16,1536]{1,0:T(8,128)(2,1)S(1)}, u32[]{:S(2)}, u32[]{:S(2)}) collective-permute-start(bf16[16,1536]{1,0:T(8,128)(2,1)} %param.11), channel_id=1, source_target_pairs={{0,2},{1,3},{2,0},{3,1},{4,6},{5,7},{6,4},{7,5},{8,10},{9,11},{10,... | collective-permute-start | bytes 147464 | tf_op jit(solution)/shard_map/gather_tokens/ppermute | solution.py:25
  6.3 0.0 collective-permute-start.23
  6.3 1.9 %fusion.8 = s32[]{:T(128)} fusion(s32[4]{0:T(128)} %param.14, s32[]{:T(128)} %bitcast.9), kind=kLoop, calls=%fused_computation.30 | loop fusion | flops 19 | bytes 24 | tf_op jit(solution)/shard_map/reduce_sum | solution.py:172
  8.3 0.8 copy.16
  9.0 0.1 eq.60
  9.1 0.1 convert_reduce_fusion
  9.2 0.1 copy.18
  9.3 0.7 convert_multiply_fusion
  10.0 0.1 copy.19
  10.8 0.1 select_reduce_fusion
  10.9 1.3 %fusion.6 = (f32[]{:T(128)}, f32[]{:T(128)}) fusion(s32[4]{0:T(128)} %param.15, s32[]{:T(128)} %select_n.25, s32[]{:T(128)} %xor.4), kind=kLoop, calls=%fused_computation.26 | loop fusion | flops 26 | bytes 32 | tf_op jit(solution)/shard_map/reduce_sum | solution.py:176
  13.4 0.1 pad_add_fusion.place
  13.5 1.3 maximum_divide_fusion.scale
  15.4 0.0 collective-permute-done.21
  15.5 0.0 collective-permute-done.22
  15.5 0.9 concatenate.13
  16.4 1.7 %collective-permute-start.24 = (bf16[16,6272]{1,0:T(8,128)(2,1)S(1)}, bf16[16,6272]{1,0:T(8,128)(2,1)S(1)}, u32[]{:S(2)}, u32[]{:S(2)}) collective-permute-start(bf16[16,6272]{1,0:T(8,128)(2,1)S(1)} %concatenate.13), channel_id=1, source_target_pairs={{0,8},{4,12},{8,0},{12,4},{16,24},{20,28},{24,16},{28,20},{1,9},{5... | collective-permute-start | bytes 602120 | tf_op jit(solution)/shard_map/gather_tokens/ppermute | solution.py:25
  18.1 1.5 %collective-permute-start.25 = (bf16[16,6272]{1,0:T(8,128)(2,1)S(1)}, bf16[16,6272]{1,0:T(8,128)(2,1)S(1)}, u32[]{:S(2)}, u32[]{:S(2)}) collective-permute-start(bf16[16,6272]{1,0:T(8,128)(2,1)S(1)} %concatenate.13), channel_id=1, source_target_pairs={{0,16},{4,20},{8,24},{12,28},{16,0},{20,4},{24,8},{28,12},{1,17},{... | collective-permute-start | bytes 602120 | tf_op jit(solution)/shard_map/gather_tokens/ppermute | solution.py:25
  19.6 0.3 collective-permute-start.26
  19.9 4.4 %collective-permute-done.24 = bf16[16,6272]{1,0:T(8,128)(2,1)S(1)} collective-permute-done((bf16[16,6272]{1,0:T(8,128)(2,1)S(1)}, bf16[16,6272]{1,0:T(8,128)(2,1)S(1)}, u32[]{:S(2)}, u32[]{:S(2)}) %collective-permute-start.24) | collective-permute-done | bytes 200736 | tf_op jit(solution)/shard_map/gather_tokens/ppermute | solution.py:25
  24.3 3.8 %collective-permute-done.25 = bf16[16,6272]{1,0:T(8,128)(2,1)S(1)} collective-permute-done((bf16[16,6272]{1,0:T(8,128)(2,1)S(1)}, bf16[16,6272]{1,0:T(8,128)(2,1)S(1)}, u32[]{:S(2)}, u32[]{:S(2)}) %collective-permute-start.25) | collective-permute-done | bytes 200736 | tf_op jit(solution)/shard_map/gather_tokens/ppermute | solution.py:25
  28.1 0.0 collective-permute-done.26
  28.1 0.1 pad_maximum_fusion
  28.2 0.1 collective-permute-start.27
  28.3 2.2 %collective-permute-done.27 = bf16[64,6272]{1,0:T(8,128)(2,1)S(1)} collective-permute-done((bf16[64,6272]{1,0:T(8,128)(2,1)S(1)}, bf16[64,6272]{1,0:T(8,128)(2,1)S(1)}, u32[]{:S(2)}, u32[]{:S(2)}) %collective-permute-start.27) | collective-permute-done | bytes 802848 | tf_op jit(solution)/shard_map/gather_tokens/ppermute | solution.py:25
  30.5 0.1 constant_dynamic-update-slice_fusion
  30.6 0.2 slice.61.x
  30.8 0.0 copy-start.1
  30.8 4.6 %copy-done.1 = bf16[1024,6144]{1,0:T(8,128)(2,1)S(1)} copy-done((bf16[1024,6144]{1,0:T(8,128)(2,1)S(1)}, bf16[1024,6144]{1,0:T(8,128)(2,1)}, u32[]{:S(2)}) %copy-start.1) | copy-done | bytes 12582936
  35.4 4.6 %copy-done.2 = bf16[1024,6144]{1,0:T(8,128)(2,1)S(1)} copy-done((bf16[1024,6144]{1,0:T(8,128)(2,1)S(1)}, bf16[1024,6144]{1,0:T(8,128)(2,1)}, u32[]{:S(2)}) %copy-start.2) | copy-done | bytes 12582936
  40.0 8.1 %project.1 = (bf16[96,1024]{1,0:T(8,128)(2,1)S(1)}, bf16[2,1024,128]{2,1,0:T(8,128)(2,1)S(1)}) custom-call(s32[3]{0:T(128)S(1)} %pad_add_fusion.place, bf16[128,6144]{1,0:T(8,128)(2,1)S(1)} %slice.61.x, bf16[128,128]{1,0:T(8,128)(2,1)S(1)} %slice.60.meta, bf16[1024,6144]{1,0:T(8,128)(2,1)S(1)} %copy-done.1, bf16[1024,6144]{1,0:T(8,128)(2,1)S(1)} %copy-done.2), custom_call_target="tpu_custom_call" | custom-call | tf_op jit(solution)/shard_map/project/pallas_call | solution.py:192
  48.1 58.1 %conditional.1 = (bf16[96,1024]{1,0:T(8,128)(2,1)}, bf16[96,1024]{1,0:T(8,128)(2,1)}, bf16[96,1024]{1,0:T(8,128)(2,1)}, bf16[128,1024]{1,0:T(8,128)(2,1)}, bf16[...) conditional(s32[]{:T(128)} %clamp.3, ...), branch_computations={%region_6.7_spmd, %region_7.8_spmd, %region_8.9_spmd} | conditional | bytes 7602512 | solution.py:203
  48.1 1.5 %collective-permute-start.17 = (bf16[2,1024,128]{2,1,0:T(8,128)(2,1)S(1)}, bf16[2,1024,128]{2,1,0:T(8,128)(2,1)S(1)}, u32[]{:S(2)}, u32[]{:S(2)}) collective-permute-start(bf16[2,1024,128]{2,1,0:T(8,128)(2,1)S(1)} %get-tuple-element.26.own), channel_id=1, source_target_pairs={{0,24},{4,28},{8,16},{12,20},{16,8},{20,12},{24,0},{28,4},{1,25},{... | collective-permute-start | bytes 1572872 | tf_op jit(solution)/shard_map/cond/branch_2_fun/peer/ppermute | solution.py:25
  49.6 0.6 collective-permute-start.14
  50.2 12.8 %collective-permute-done.17.peer = bf16[2,1024,128]{2,1,0:T(8,128)(2,1)S(1)} collective-permute-done((bf16[2,1024,128]{2,1,0:T(8,128)(2,1)S(1)}, bf16[2,1024,128]{2,1,0:T(8,128)(2,1)S(1)}, u32[]{:S(2)}, u32[]{:S(2)}) %collective-permute-start.17) | collective-permute-done | bytes 524320 | tf_op jit(solution)/shard_map/cond/branch_2_fun/peer/ppermute | solution.py:25
  63.0 1.7 %merge.5 = bf16[128,1024]{1,0:T(8,128)(2,1)} custom-call(f32[2]{0:T(128)S(1)} %get-tuple-element.25.coefs, bf16[2,1024,128]{2,1,0:T(8,128)(2,1)S(1)} %get-tuple-element.26.own, bf16[2,1024,128]{2,1,0:T(8,128)(2,1)S(1)} %collective-permute-done.17.peer), custom_call_target="tpu_custom_call" | custom-call | tf_op jit(solution)/shard_map/cond/branch_2_fun/merge/pallas_call | solution.py:129
  64.8 0.6 collective-permute-start.18
  65.4 3.5 %collective-permute-start.19 = (bf16[128,1024]{1,0:T(8,128)(2,1)}, bf16[128,1024]{1,0:T(8,128)(2,1)}, u32[]{:S(2)}, u32[]{:S(2)}) collective-permute-start(bf16[128,1024]{1,0:T(8,128)(2,1)} %merge.5), channel_id=1, source_target_pairs={{0,2},{1,3},{2,0},{3,1},{4,6},{5,7},{6,4},{7,5},{8,10},{9,11},{10,... | collective-permute-start | bytes 786440 | tf_op jit(solution)/shard_map/cond/branch_2_fun/spread_second/ppermute | solution.py:25
  68.9 0.3 collective-permute-start.20
  69.2 1.2 collective-permute-start.15
  70.4 0.0 collective-permute-done.14
  70.4 2.4 %collective-permute-start.16 = (bf16[96,1024]{1,0:T(8,128)(2,1)S(1)}, bf16[96,1024]{1,0:T(8,128)(2,1)}, u32[]{:S(2)}, u32[]{:S(2)}) collective-permute-start(bf16[96,1024]{1,0:T(8,128)(2,1)S(1)} %get-tuple-element.24), channel_id=1, source_target_pairs={{0,3},{1,2},{2,1},{3,0},{4,7},{5,6},{6,5},{7,4},{8,11},{9,10},{10,... | collective-permute-start | bytes 589832 | tf_op jit(solution)/shard_map/cond/branch_2_fun/spread_first/ppermute | solution.py:25
  72.7 33.2 %collective-permute-done.15 = bf16[96,1024]{1,0:T(8,128)(2,1)} collective-permute-done((bf16[96,1024]{1,0:T(8,128)(2,1)S(1)}, bf16[96,1024]{1,0:T(8,128)(2,1)}, u32[]{:S(2)}, u32[]{:S(2)}) %collective-permute-start.15) | collective-permute-done | bytes 196640 | tf_op jit(solution)/shard_map/cond/branch_2_fun/spread_first/ppermute | solution.py:25
  106.0 0.0 collective-permute-done.16
  106.0 0.0 collective-permute-done.18
  106.0 0.0 collective-permute-done.19
  106.2 0.0 copy-start
  106.2 4.6 %copy-done = bf16[4096,1536]{1,0:T(8,128)(2,1)S(1)} copy-done((bf16[4096,1536]{1,0:T(8,128)(2,1)S(1)}, bf16[4096,1536]{1,0:T(8,128)(2,1)}, u32[]{:S(2)}) %copy-start) | copy-done | bytes 12582936
  110.8 3.0 %down.3 = bf16[128,1536]{1,0:T(8,128)(2,1)S(1)} custom-call(s32[3]{0:T(128)S(1)} %pad_add_fusion.place, f32[2]{0:T(128)S(1)} %maximum_divide_fusion.scale, bf16[128,128]{1,0:T(8,128)(2,1)S(1)} %slice.60.meta, bf16[128,1024]{1,0:T(8,128)(2,1)} %get-tuple-element.43.refs_0_, bf16[128,1024]{1,0:T(8,128)(2,1)} %get-tuple-element.44.refs_1_, ...), custom_call_target="tpu_custom_call" | custom-call | tf_op jit(solution)/shard_map/down/pallas_call | solution.py:212
  113.8 0.1 collective-permute-start.32
  113.9 3.5 %down.2 = bf16[128,1536]{1,0:T(8,128)(2,1)S(1)} custom-call(s32[3]{0:T(128)S(1)} %pad_add_fusion.place, f32[2]{0:T(128)S(1)} %maximum_divide_fusion.scale, bf16[128,128]{1,0:T(8,128)(2,1)S(1)} %slice.60.meta, bf16[96,1024]{1,0:T(8,128)(2,1)S(1)} %get-tuple-element.38.refs_0_, bf16[96,1024]{1,0:T(8,128)(2,1)} %get-tuple-element.40.refs_1_, ...), custom_call_target="tpu_custom_call" | custom-call | tf_op jit(solution)/shard_map/down/pallas_call | solution.py:212
  117.4 0.6 collective-permute-start.28
  118.1 1.2 collective-permute-start.33
  119.3 0.8 collective-permute-start.34
  120.1 1.5 %collective-permute-start.35 = (bf16[16,1536]{1,0:T(8,128)(2,1)S(1)}, bf16[16,1536]{1,0:T(8,128)(2,1)S(1)}, u32[]{:S(2)}, u32[]{:S(2)}) collective-permute-start(bf16[16,1536]{1,0:T(8,128)(2,1)S(1)} %get-tuple-element.56), channel_id=1, source_target_pairs={{0,24},{4,28},{8,16},{12,20},{16,8},{20,12},{24,0},{28,4},{1,25},{... | collective-permute-start | bytes 147464 | tf_op jit(solution)/shard_map/chips/ppermute | solution.py:25
  121.7 1.2 collective-permute-start.29
  122.9 0.8 collective-permute-start.30
  123.8 1.5 %collective-permute-start.31 = (bf16[16,1536]{1,0:T(8,128)(2,1)S(1)}, bf16[16,1536]{1,0:T(8,128)(2,1)S(1)}, u32[]{:S(2)}, u32[]{:S(2)}) collective-permute-start(bf16[16,1536]{1,0:T(8,128)(2,1)S(1)} %get-tuple-element.59), channel_id=1, source_target_pairs={{0,24},{4,28},{8,16},{12,20},{16,8},{20,12},{24,0},{28,4},{1,25},{... | collective-permute-start | bytes 147464 | tf_op jit(solution)/shard_map/chips/ppermute | solution.py:25
  125.3 0.2 collective-permute-done.35
  125.5 0.6 fusion.2
  126.1 1.0 collective-permute-done.30
  127.1 1.6 %collective-permute-done.31 = bf16[16,1536]{1,0:T(8,128)(2,1)S(1)} collective-permute-done((bf16[16,1536]{1,0:T(8,128)(2,1)S(1)}, bf16[16,1536]{1,0:T(8,128)(2,1)S(1)}, u32[]{:S(2)}, u32[]{:S(2)}) %collective-permute-start.31) | collective-permute-done | bytes 49184 | tf_op jit(solution)/shard_map/chips/ppermute | solution.py:25
  128.8 0.6 fusion.5
  (22 shorter events, 0.3 us)
Async XLA Ops:
  0.6 14.8 %collective-permute-start.21 = (bf16[16,1536]{1,0:T(8,128)(2,1)}, bf16[16,1536]{1,0:T(8,128)(2,1)S(1)}, u32[]{:S(2)}, u32[]{:S(2)}) collective-permute-start(bf16[16,1536]{1,0:T(8,128)(2,1)} %param.11), channel_id=1, source_target_pairs={{0,1},{1,0},{2,3},{3,2},{4,5},{5,4},{6,7},{7,6},{8,9},{9,8},{10,11... | collective-permute-start | bytes 147464 | tf_op jit(solution)/shard_map/gather_tokens/ppermute | solution.py:25
  3.7 11.7 %collective-permute-start.22 = (bf16[16,1536]{1,0:T(8,128)(2,1)}, bf16[16,1536]{1,0:T(8,128)(2,1)S(1)}, u32[]{:S(2)}, u32[]{:S(2)}) collective-permute-start(bf16[16,1536]{1,0:T(8,128)(2,1)} %param.11), channel_id=1, source_target_pairs={{0,2},{1,3},{2,0},{3,1},{4,6},{5,7},{6,4},{7,5},{8,10},{9,11},{10,... | collective-permute-start | bytes 147464 | tf_op jit(solution)/shard_map/gather_tokens/ppermute | solution.py:25
  6.3 9.2 %collective-permute-start.23 = (bf16[16,1536]{1,0:T(8,128)(2,1)}, bf16[16,1536]{1,0:T(8,128)(2,1)S(1)}, u32[]{:S(2)}, u32[]{:S(2)}) collective-permute-start(bf16[16,1536]{1,0:T(8,128)(2,1)} %param.11), channel_id=1, source_target_pairs={{0,3},{1,2},{2,1},{3,0},{4,7},{5,6},{6,5},{7,4},{8,11},{9,10},{10,... | collective-permute-start | bytes 147464 | tf_op jit(solution)/shard_map/gather_tokens/ppermute | solution.py:25
  16.4 7.9 %collective-permute-start.24 = (bf16[16,6272]{1,0:T(8,128)(2,1)S(1)}, bf16[16,6272]{1,0:T(8,128)(2,1)S(1)}, u32[]{:S(2)}, u32[]{:S(2)}) collective-permute-start(bf16[16,6272]{1,0:T(8,128)(2,1)S(1)} %concatenate.13), channel_id=1, source_target_pairs={{0,8},{4,12},{8,0},{12,4},{16,24},{20,28},{24,16},{28,20},{1,9},{5... | collective-permute-start | bytes 602120 | tf_op jit(solution)/shard_map/gather_tokens/ppermute | solution.py:25
  18.1 10.0 %collective-permute-start.25 = (bf16[16,6272]{1,0:T(8,128)(2,1)S(1)}, bf16[16,6272]{1,0:T(8,128)(2,1)S(1)}, u32[]{:S(2)}, u32[]{:S(2)}) collective-permute-start(bf16[16,6272]{1,0:T(8,128)(2,1)S(1)} %concatenate.13), channel_id=1, source_target_pairs={{0,16},{4,20},{8,24},{12,28},{16,0},{20,4},{24,8},{28,12},{1,17},{... | collective-permute-start | bytes 602120 | tf_op jit(solution)/shard_map/gather_tokens/ppermute | solution.py:25
  19.6 8.5 %collective-permute-start.26 = (bf16[16,6272]{1,0:T(8,128)(2,1)S(1)}, bf16[16,6272]{1,0:T(8,128)(2,1)S(1)}, u32[]{:S(2)}, u32[]{:S(2)}) collective-permute-start(bf16[16,6272]{1,0:T(8,128)(2,1)S(1)} %concatenate.13), channel_id=1, source_target_pairs={{0,24},{4,28},{8,16},{12,20},{16,8},{20,12},{24,0},{28,4},{1,25},{... | collective-permute-start | bytes 602120 | tf_op jit(solution)/shard_map/gather_tokens/ppermute | solution.py:25
  28.2 2.4 %collective-permute-start.27 = (bf16[64,6272]{1,0:T(8,128)(2,1)S(1)}, bf16[64,6272]{1,0:T(8,128)(2,1)S(1)}, u32[]{:S(2)}, u32[]{:S(2)}) collective-permute-start(bf16[64,6272]{1,0:T(8,128)(2,1)S(1)} %pad_maximum_fusion), channel_id=1, source_target_pairs={{0,4},{4,0},{8,12},{12,8},{16,20},{20,16},{24,28},{28,24},{1,5},{5... | collective-permute-start | bytes 2408456 | tf_op jit(solution)/shard_map/gather_tokens/ppermute | solution.py:25
  30.8 4.6 %copy-start.1 = (bf16[1024,6144]{1,0:T(8,128)(2,1)S(1)}, bf16[1024,6144]{1,0:T(8,128)(2,1)}, u32[]{:S(2)}) copy-start(bf16[1024,6144]{1,0:T(8,128)(2,1)} %gate_w.1) | copy-start | bytes 37748740
  35.4 4.6 %copy-start.2 = (bf16[1024,6144]{1,0:T(8,128)(2,1)S(1)}, bf16[1024,6144]{1,0:T(8,128)(2,1)}, u32[]{:S(2)}) copy-start(bf16[1024,6144]{1,0:T(8,128)(2,1)} %up_w.1) | copy-start | bytes 37748740
  48.1 14.9 %collective-permute-start.17 = (bf16[2,1024,128]{2,1,0:T(8,128)(2,1)S(1)}, bf16[2,1024,128]{2,1,0:T(8,128)(2,1)S(1)}, u32[]{:S(2)}, u32[]{:S(2)}) collective-permute-start(bf16[2,1024,128]{2,1,0:T(8,128)(2,1)S(1)} %get-tuple-element.26.own), channel_id=1, source_target_pairs={{0,24},{4,28},{8,16},{12,20},{16,8},{20,12},{24,0},{28,4},{1,25},{... | collective-permute-start | bytes 1572872 | tf_op jit(solution)/shard_map/cond/branch_2_fun/peer/ppermute | solution.py:25
  49.6 20.7 %collective-permute-start.14 = (bf16[96,1024]{1,0:T(8,128)(2,1)S(1)}, bf16[96,1024]{1,0:T(8,128)(2,1)}, u32[]{:S(2)}, u32[]{:S(2)}) collective-permute-start(bf16[96,1024]{1,0:T(8,128)(2,1)S(1)} %get-tuple-element.24), channel_id=1, source_target_pairs={{0,1},{1,0},{2,3},{3,2},{4,5},{5,4},{6,7},{7,6},{8,9},{9,8},{10,11... | collective-permute-start | bytes 589832 | tf_op jit(solution)/shard_map/cond/branch_2_fun/spread_first/ppermute | solution.py:25
  64.8 41.2 %collective-permute-start.18 = (bf16[128,1024]{1,0:T(8,128)(2,1)}, bf16[128,1024]{1,0:T(8,128)(2,1)}, u32[]{:S(2)}, u32[]{:S(2)}) collective-permute-start(bf16[128,1024]{1,0:T(8,128)(2,1)} %merge.5), channel_id=1, source_target_pairs={{0,1},{1,0},{2,3},{3,2},{4,5},{5,4},{6,7},{7,6},{8,9},{9,8},{10,11... | collective-permute-start | bytes 786440 | tf_op jit(solution)/shard_map/cond/branch_2_fun/spread_second/ppermute | solution.py:25
  65.4 40.6 %collective-permute-start.19 = (bf16[128,1024]{1,0:T(8,128)(2,1)}, bf16[128,1024]{1,0:T(8,128)(2,1)}, u32[]{:S(2)}, u32[]{:S(2)}) collective-permute-start(bf16[128,1024]{1,0:T(8,128)(2,1)} %merge.5), channel_id=1, source_target_pairs={{0,2},{1,3},{2,0},{3,1},{4,6},{5,7},{6,4},{7,5},{8,10},{9,11},{10,... | collective-permute-start | bytes 786440 | tf_op jit(solution)/shard_map/cond/branch_2_fun/spread_second/ppermute | solution.py:25
  68.9 37.1 %collective-permute-start.20 = (bf16[128,1024]{1,0:T(8,128)(2,1)}, bf16[128,1024]{1,0:T(8,128)(2,1)}, u32[]{:S(2)}, u32[]{:S(2)}) collective-permute-start(bf16[128,1024]{1,0:T(8,128)(2,1)} %merge.5), channel_id=1, source_target_pairs={{0,3},{1,2},{2,1},{3,0},{4,7},{5,6},{6,5},{7,4},{8,11},{9,10},{10,... | collective-permute-start | bytes 786440 | tf_op jit(solution)/shard_map/cond/branch_2_fun/spread_second/ppermute | solution.py:25
  69.2 36.8 %collective-permute-start.15 = (bf16[96,1024]{1,0:T(8,128)(2,1)S(1)}, bf16[96,1024]{1,0:T(8,128)(2,1)}, u32[]{:S(2)}, u32[]{:S(2)}) collective-permute-start(bf16[96,1024]{1,0:T(8,128)(2,1)S(1)} %get-tuple-element.24), channel_id=1, source_target_pairs={{0,2},{1,3},{2,0},{3,1},{4,6},{5,7},{6,4},{7,5},{8,10},{9,11},{10,... | collective-permute-start | bytes 589832 | tf_op jit(solution)/shard_map/cond/branch_2_fun/spread_first/ppermute | solution.py:25
  70.4 35.6 %collective-permute-start.16 = (bf16[96,1024]{1,0:T(8,128)(2,1)S(1)}, bf16[96,1024]{1,0:T(8,128)(2,1)}, u32[]{:S(2)}, u32[]{:S(2)}) collective-permute-start(bf16[96,1024]{1,0:T(8,128)(2,1)S(1)} %get-tuple-element.24), channel_id=1, source_target_pairs={{0,3},{1,2},{2,1},{3,0},{4,7},{5,6},{6,5},{7,4},{8,11},{9,10},{10,... | collective-permute-start | bytes 589832 | tf_op jit(solution)/shard_map/cond/branch_2_fun/spread_first/ppermute | solution.py:25
  106.2 4.6 %copy-start = (bf16[4096,1536]{1,0:T(8,128)(2,1)S(1)}, bf16[4096,1536]{1,0:T(8,128)(2,1)}, u32[]{:S(2)}) copy-start(bf16[4096,1536]{1,0:T(8,128)(2,1)} %refs_4_.3) | copy-start | bytes 37748740
  113.8 4.2 %collective-permute-start.32 = (bf16[64,1536]{1,0:T(8,128)(2,1)S(1)}, bf16[64,1536]{1,0:T(8,128)(2,1)S(1)}, u32[]{:S(2)}, u32[]{:S(2)}) collective-permute-start(bf16[64,1536]{1,0:T(8,128)(2,1)S(1)} %slice.69), channel_id=1, source_target_pairs={{0,4},{4,0},{8,12},{12,8},{16,20},{20,16},{24,28},{28,24},{1,5},{5... | collective-permute-start | bytes 589832 | tf_op jit(solution)/shard_map/cores/ppermute | solution.py:25
  117.4 4.2 %collective-permute-start.28 = (bf16[64,1536]{1,0:T(8,128)(2,1)S(1)}, bf16[64,1536]{1,0:T(8,128)(2,1)S(1)}, u32[]{:S(2)}, u32[]{:S(2)}) collective-permute-start(bf16[64,1536]{1,0:T(8,128)(2,1)S(1)} %slice.63), channel_id=1, source_target_pairs={{0,4},{4,0},{8,12},{12,8},{16,20},{20,16},{24,28},{28,24},{1,5},{5... | collective-permute-start | bytes 589832 | tf_op jit(solution)/shard_map/cores/ppermute | solution.py:25
  118.1 5.7 %collective-permute-start.33 = (bf16[16,1536]{1,0:T(8,128)(2,1)S(1)}, bf16[16,1536]{1,0:T(8,128)(2,1)S(1)}, u32[]{:S(2)}, u32[]{:S(2)}) collective-permute-start(bf16[16,1536]{1,0:T(8,128)(2,1)S(1)} %get-tuple-element.55), channel_id=1, source_target_pairs={{0,8},{4,12},{8,0},{12,4},{16,24},{20,28},{24,16},{28,20},{1,9},{5... | collective-permute-start | bytes 147464 | tf_op jit(solution)/shard_map/chips/ppermute | solution.py:25
  119.3 5.9 %collective-permute-start.34 = (bf16[16,1536]{1,0:T(8,128)(2,1)S(1)}, bf16[16,1536]{1,0:T(8,128)(2,1)S(1)}, u32[]{:S(2)}, u32[]{:S(2)}) collective-permute-start(bf16[16,1536]{1,0:T(8,128)(2,1)S(1)} %get-tuple-element.57), channel_id=1, source_target_pairs={{0,16},{4,20},{8,24},{12,28},{16,0},{20,4},{24,8},{28,12},{1,17},{... | collective-permute-start | bytes 147464 | tf_op jit(solution)/shard_map/chips/ppermute | solution.py:25
  120.1 5.4 %collective-permute-start.35 = (bf16[16,1536]{1,0:T(8,128)(2,1)S(1)}, bf16[16,1536]{1,0:T(8,128)(2,1)S(1)}, u32[]{:S(2)}, u32[]{:S(2)}) collective-permute-start(bf16[16,1536]{1,0:T(8,128)(2,1)S(1)} %get-tuple-element.56), channel_id=1, source_target_pairs={{0,24},{4,28},{8,16},{12,20},{16,8},{20,12},{24,0},{28,4},{1,25},{... | collective-permute-start | bytes 147464 | tf_op jit(solution)/shard_map/chips/ppermute | solution.py:25
  121.7 4.4 %collective-permute-start.29 = (bf16[16,1536]{1,0:T(8,128)(2,1)S(1)}, bf16[16,1536]{1,0:T(8,128)(2,1)S(1)}, u32[]{:S(2)}, u32[]{:S(2)}) collective-permute-start(bf16[16,1536]{1,0:T(8,128)(2,1)S(1)} %get-tuple-element.58), channel_id=1, source_target_pairs={{0,8},{4,12},{8,0},{12,4},{16,24},{20,28},{24,16},{28,20},{1,9},{5... | collective-permute-start | bytes 147464 | tf_op jit(solution)/shard_map/chips/ppermute | solution.py:25
  122.9 4.2 %collective-permute-start.30 = (bf16[16,1536]{1,0:T(8,128)(2,1)S(1)}, bf16[16,1536]{1,0:T(8,128)(2,1)S(1)}, u32[]{:S(2)}, u32[]{:S(2)}) collective-permute-start(bf16[16,1536]{1,0:T(8,128)(2,1)S(1)} %get-tuple-element.60), channel_id=1, source_target_pairs={{0,16},{4,20},{8,24},{12,28},{16,0},{20,4},{24,8},{28,12},{1,17},{... | collective-permute-start | bytes 147464 | tf_op jit(solution)/shard_map/chips/ppermute | solution.py:25
  123.8 5.0 %collective-permute-start.31 = (bf16[16,1536]{1,0:T(8,128)(2,1)S(1)}, bf16[16,1536]{1,0:T(8,128)(2,1)S(1)}, u32[]{:S(2)}, u32[]{:S(2)}) collective-permute-start(bf16[16,1536]{1,0:T(8,128)(2,1)S(1)} %get-tuple-element.59), channel_id=1, source_target_pairs={{0,24},{4,28},{8,16},{12,20},{16,8},{20,12},{24,0},{28,4},{1,25},{... | collective-permute-start | bytes 147464 | tf_op jit(solution)/shard_map/chips/ppermute | solution.py:25

commit v2 on v0

v2 whole, which is shorter than its diff:
```python
import functools

import jax
import jax.numpy as jnp
from jax import lax
from jax.experimental import pallas as pl
from jax.experimental.pallas import tpu as pltpu
from jax.sharding import PartitionSpec as P

EXPERTS = 4
TOP = 2
CAP = 12
LANES = 128
VMEM_LIMIT = 6 << 20
LOADS = 4
F32 = jnp.float32
BF16 = jnp.bfloat16
NT = (((1,), (1,)), ((), ()))
IN_VMEM = pl.BlockSpec(memory_space=pltpu.VMEM)
IN_SMEM = pl.BlockSpec(memory_space=pltpu.SMEM)
IN_HBM = pl.BlockSpec(memory_space=pltpu.HBM)
ANYWHERE = pl.BlockSpec(memory_space=pl.ANY)


def swapped(value, axis, by):
    devices = lax.axis_size(axis)
    return lax.ppermute(value, axis, [(i, i ^ by) for i in range(devices)])


def iota(shape, dim):
    return lax.broadcasted_iota(jnp.int32, shape, dim)


def one_hot(mask):
    return mask.astype(F32).astype(BF16)


def token_flip(tokens, by):
    shape = (tokens, tokens)
    return one_hot((iota(shape, 0) ^ by) == iota(shape, 1))


def silu(v):
    return v / (1.0 + jnp.exp(-v))


def mate_of(labels):
    mate = 0
    for i in range(1, EXPERTS):
        mate = mate + jnp.where(labels[i] == labels[0], i, 0)
    return mate


def notes_kernel(ids, codes, *refs):
    notes = refs[-1]
    shard = ids.shape[1]
    shape = (LANES, shard)
    line = iota(shape, 0)
    picked = jnp.zeros(shape, F32)
    scale = jnp.zeros(shape, F32)
    for k in range(TOP):
        own = ids[k:k + 1, :]
        picked = picked + (own == line).astype(F32)
        weight = codes[k:k + 1, :].astype(F32) / 256.0
        scale = scale + jnp.where(own == line - EXPERTS, weight, 0.0)
    square = (shard, shard)
    earlier = (iota(square, 0) < iota(square, 1)).astype(F32)
    same = (iota(square, 0) == iota(square, 1)).astype(F32)
    slot = jnp.dot(picked, earlier, preferred_element_type=F32)
    slot = jnp.where(picked > 0.0, slot, -1.0)
    table = jnp.where(line < EXPERTS, slot, scale)
    notes[...] = lax.dot_general(same, table, NT, preferred_element_type=F32).astype(BF16)


def load_kernel(place, *refs, ks):
    weights, (blocks, done, sems) = refs[:2], refs[-3:]
    rows = blocks.shape[2] // LOADS
    depth = blocks.shape[3]
    copies = []
    for i, k in enumerate(ks):
        columns = pl.ds(pl.multiple_of((place[0] ^ k) * depth, LANES), depth)
        for w, weight in enumerate(weights):
            for p in range(LOADS):
                part = pl.ds(p * rows, rows)
                copies.append(
                    pltpu.make_async_copy(
                        weight.at[part, columns], blocks.at[w, i, part], sems.at[w, i, p]
                    )
                )
    for copy in copies:
        copy.start()
    for copy in copies:
        copy.wait()
    done[...] = jnp.zeros(done.shape, F32)


def product(place, blocks, x, j, w):
    size = blocks.shape[2] // EXPERTS
    depth = blocks.shape[3]
    rows = pl.ds(pl.multiple_of((place[1] ^ j) * size, 16), size)
    total = None
    for i in range(blocks.shape[1]):
        part = lax.dot_general(
            blocks[w, i, rows], x[:, i * depth:(i + 1) * depth], NT, preferred_element_type=F32
        )
        total = part if total is None else total + part
    return total


def project_first_kernel(place, x, blocks, *refs):
    sums = refs[-1]
    for j in range(EXPERTS):
        for w in range(2):
            sums[j, w] = product(place, blocks, x, j, w)


def picks(notes, expert, rows, shard):
    table = notes[...].astype(F32).T
    slot = jnp.sum(jnp.where(iota(table.shape, 0) == expert, table, 0.0), axis=0, keepdims=True)
    tokens = slot.shape[1]
    first = (iota((1, tokens), 1) // shard) * CAP
    target = jnp.where(slot < 0.0, -1, first + slot.astype(jnp.int32))
    return one_hot(iota((rows, tokens), 0) == target)


def project_sent_kernel(place, x, notes, sums, blocks, slots, *sent, shard):
    size = blocks.shape[2] // EXPERTS
    pick = picks(notes, place[1], slots.shape[0], shard)
    for j in range(1, EXPERTS):
        gate = product(place, blocks, x, j, 0) + sums[j, 0]
        upper = product(place, blocks, x, j, 1) + sums[j, 1]
        sent[j - 1][0] = gate.astype(BF16)
        sent[j - 1][1] = upper.astype(BF16)
        hidden = (silu(gate) * upper).T.astype(BF16)
        slots[:, (j - 1) * size:j * size] = jnp.dot(
            pick, hidden, preferred_element_type=F32
        ).astype(BF16)


def project_own_kernel(place, x, notes, sums, blocks, others, slots, own, *, shard):
    size = blocks.shape[2] // EXPERTS
    pick = picks(notes, place[1], slots.shape[0], shard)
    gate = product(place, blocks, x, 0, 0) + sums[0, 0]
    upper = product(place, blocks, x, 0, 1) + sums[0, 1]
    own[0] = gate
    own[1] = upper
    hidden = (silu(gate) * upper).T.astype(BF16)
    slots[:, :size] = jnp.dot(pick, hidden, preferred_element_type=F32).astype(BF16)
    slots[:, size:] = others[...]


def merge_kernel(place, labels, freq, own, *refs, flips):
    peers, hidden = refs[:EXPERTS - 1], refs[-1]
    expert = place[1]
    mate = mate_of(labels)
    tokens = own.shape[2]
    parts = [own]
    counts = [jnp.full((1, 1), freq[expert], jnp.int32).astype(F32)]
    for j, peer in enumerate(peers, 1):
        order = token_flip(tokens, flips[j - 1])
        parts.append([jnp.dot(peer[i], order, preferred_element_type=F32) for i in range(2)])
        counts.append(jnp.full((1, 1), freq[expert ^ j], jnp.int32).astype(F32))
    for group in range(2):
        member = []
        for j in range(EXPERTS):
            same = jnp.logical_or(j == 0, mate == j)
            member.append(jnp.where(same if group == 0 else jnp.logical_not(same), counts[j], 0.0))
        whole = member[0] + member[1] + member[2] + member[3]
        gate, upper = [
            sum((member[j] / whole) * parts[j][i] for j in range(EXPERTS)) for i in range(2)
        ]
        hidden[group] = (silu(gate) * upper).T.astype(BF16)


def route_kernel(labels, *refs, count):
    pieces, sent = refs[:count], refs[1 - EXPERTS:]
    mate = mate_of(labels)
    for j, to in enumerate(sent, 1):
        group = jnp.where(mate == j, 0, 1)
        for i in range(count):
            to[i] = pieces[i][group]


def times_weight(place, weight, hidden, ks, n_exp, factor, store):
    z, expert = place[0], place[1]
    depth = weight.shape[0] // n_exp
    size = depth // EXPERTS
    width = weight.shape[1]
    step = min(256, width)
    for n in range(0, width, step):
        total = None
        for i, k in enumerate(ks):
            for j in range(EXPERTS):
                at = pl.multiple_of((z ^ k) * depth + (expert ^ j) * size, 16)
                part = jnp.dot(
                    hidden[:, (i * EXPERTS + j) * size:(i * EXPERTS + j + 1) * size],
                    weight[pl.ds(at, size), n:n + step],
                    preferred_element_type=F32,
                )
                total = part if total is None else total + part
        store(n, step, total * factor)


def first_down_kernel(place, notes, *refs, shard, n_exp, line):
    weight, *pieces = refs[:-2]
    out, hidden = refs[-2:]
    z, expert = place[0], place[1]
    depth = weight.shape[0] // n_exp
    ks = list(range(n_exp))
    inner = None
    if line:
        inner = jnp.logical_or(z == 1, z == 2)
        ks = [0, 1, jnp.where(inner, 3, 2), jnp.where(inner, 2, 3)]
        pieces = [[pieces[0]], [pieces[1]], [pieces[2], pieces[4]], [pieces[3], pieces[5]]]
    else:
        pieces = [[piece] for piece in pieces[:n_exp]]
    table = notes[...].astype(F32)
    tokens = table.shape[0]
    lane = iota(table.shape, 1)
    slot = jnp.sum(jnp.where(lane == expert, table, 0.0), axis=1, keepdims=True)
    factor = jnp.sum(jnp.where(lane == EXPERTS + expert, table, 0.0), axis=1, keepdims=True)
    first = (iota((tokens, 1), 0) // shard) * CAP
    target = jnp.where(slot < 0.0, -1, first + slot.astype(jnp.int32))
    spread = one_hot(iota((tokens, pieces[0][0].shape[0]), 1) == target)
    for i, found in enumerate(pieces):
        piece = found[0][...]
        if len(found) > 1:
            piece = jnp.where(inner, piece, found[1][...])
        hidden[:, i * depth:(i + 1) * depth] = jnp.dot(
            spread, piece, preferred_element_type=F32
        ).astype(BF16)

    def store(n, step, total):
        out[:, n:n + step] = total

    times_weight(place, weight, hidden, ks, n_exp, factor, store)


def second_down_kernel(place, labels, freq, notes, weight, initial, *refs, flips, n_exp, shard):
    own, refs = refs[:n_exp], refs[n_exp:]
    peers, (keep, sent, hidden) = refs[:-3], refs[-3:]
    expert = place[1]
    size = weight.shape[0] // n_exp // EXPERTS
    table = notes[...].astype(F32)
    tokens = table.shape[0]
    mate = mate_of(labels)
    lane = iota(table.shape, 1)
    mine = jnp.logical_or(lane == EXPERTS + expert, lane == EXPERTS + (expert ^ mate))
    factor = jnp.sum(jnp.where(mine, table, 0.0), axis=1, keepdims=True)
    chosen = jnp.full((1, 1), freq[expert], jnp.int32).astype(F32)
    other = jnp.full((1, 1), freq[expert ^ mate], jnp.int32).astype(F32)
    factor = factor * (chosen / (chosen + other))
    for j in range(1, EXPERTS):
        order = token_flip(tokens, flips[j - 1])
        found = []
        for part in peers[j - 1::EXPERTS - 1]:
            found += [part[i] for i in range(part.shape[0])]
        for k in range(n_exp):
            at = (k * EXPERTS + j) * size
            hidden[:, at:at + size] = jnp.dot(
                order, found[k], preferred_element_type=F32
            ).astype(BF16)
    for k in range(n_exp):
        hidden[:, k * EXPERTS * size:(k * EXPERTS + 1) * size] = own[k][0]
    middle = tokens // 2

    def put(index, n, step, total):
        for c in range(middle // shard):
            rows = slice(c * shard, (c + 1) * shard)
            keep[c, index, :, n:n + step] = total[rows]
            rows = slice(middle + c * shard, middle + (c + 1) * shard)
            sent[c, index, :, n:n + step] = total[rows].astype(BF16)

    def store(n, step, total):
        put(0, n, step, initial[:, n:n + step])
        put(1, n, step, total)

    times_weight(place, weight, hidden, range(n_exp), n_exp, factor, store)


def cores_kernel(keep, theirs, own, *sent):
    own[...] = keep[0] + theirs[0].astype(F32)
    for c, to in enumerate(sent, 1):
        to[...] = (keep[c] + theirs[c].astype(F32)).astype(BF16)


def finish_kernel(own, *refs):
    parts, outs = refs[:-2], refs[-2:]
    for i, out in enumerate(outs):
        total = own[i]
        for part in parts:
            total = total + part[i].astype(F32)
        out[...] = total.astype(BF16)


def local(tokens, route_ids, gate_codes, merge_labels, freq_counts, w_gate, w_up, w_down):
    n_tok = lax.axis_size("tok")
    n_exp = lax.axis_size("exp")
    span = n_tok // EXPERTS
    z = lax.axis_index("exp")
    expert = lax.axis_index("tok") // span
    shard, depth = tokens.shape
    all_tokens = n_tok * shard
    units = w_gate.shape[0]
    size = units // EXPERTS
    width = w_down.shape[1]
    half = n_exp // 2
    flips = tuple(j * span // 2 * shard for j in range(1, EXPERTS))
    others = range(1, EXPERTS)
    gate_w = pltpu.with_memory_space_constraint(w_gate, pltpu.HBM)
    up_w = pltpu.with_memory_space_constraint(w_up, pltpu.HBM)
    place = jnp.stack([z, expert]).astype(jnp.int32)
    shape = jax.ShapeDtypeStruct

    small = pl.CostEstimate(flops=1, bytes_accessed=1, transcendentals=0)
    limit = VMEM_LIMIT if all_tokens <= LANES else 2 * VMEM_LIMIT

    def call(kernel, name, out_shape, *args, scratch=(), smem=0, unused=0, hbm=0, cost=True):
        specs = [IN_SMEM] * smem + [IN_HBM] * hbm
        specs += [IN_VMEM] * (len(args) - len(specs) - unused) + [ANYWHERE] * unused
        return pl.pallas_call(
            kernel,
            in_specs=specs,
            out_specs=[IN_VMEM] * len(out_shape) if isinstance(out_shape, list) else IN_VMEM,
            out_shape=out_shape,
            scratch_shapes=scratch,
            compiler_params=pltpu.CompilerParams(vmem_limit_bytes=limit),
            cost_estimate=small if cost else None,
            name=name,
        )(*args)

    def load(ks, *after):
        return call(
            functools.partial(load_kernel, ks=ks),
            "load",
            [pltpu.VMEM((2, len(ks), units, depth), BF16), shape((8, LANES), F32)],
            place,
            gate_w,
            up_w,
            *after,
            scratch=[pltpu.SemaphoreType.DMA((2, len(ks), LOADS))],
            smem=1,
            hbm=2,
            unused=len(after),
            cost=False,
        )

    near_w, near_done = load(range(half))
    notes = call(
        notes_kernel, "notes", shape((shard, LANES), BF16), route_ids.T, gate_codes.T, near_done, unused=1
    )

    with jax.named_scope("gather_tokens"):
        rows = [tokens] + [swapped(tokens, "exp", k) for k in range(1, n_exp)]
        near = jnp.concatenate([notes] + rows[:half], axis=1)
        far = jnp.concatenate(rows[half:], axis=1)

        def chips(row):
            return [row] + [swapped(row, "tok", j) for j in range(2, n_tok, 2)]

        def cores(parts):
            rows = jnp.concatenate(parts, axis=0)
            return jnp.concatenate([rows, swapped(rows, "tok", 1)], axis=0), rows

        near = chips(near)
        near[1], far = lax.optimization_barrier((near[1], far))
        far = chips(far)
        near, near_rows = cores(near)
        far_w, far_done = load(range(half, n_exp), near_rows)
        far, _ = cores(far)
        table = near[:, :LANES]
        near = near[:, LANES:]

    sums = call(
        project_first_kernel,
        "project_first",
        shape((EXPERTS, 2, size, all_tokens), F32),
        place,
        near,
        near_w,
        far_done,
        smem=1,
        unused=1,
        cost=False,
    )
    others_slots, *sent = call(
        functools.partial(project_sent_kernel, shard=shard),
        "project_sent",
        [shape((n_tok * CAP, units - size), BF16)]
        + [shape((2, size, all_tokens), BF16) for _ in others],
        place,
        far,
        table,
        sums,
        far_w,
        smem=1,
        cost=False,
    )
    with jax.named_scope("peers"):
        peers = [swapped(sent[j - 1], "tok", j * span) for j in others]
    slots, own = call(
        functools.partial(project_own_kernel, shard=shard),
        "project_own",
        [shape((n_tok * CAP, units), BF16), shape((2, size, all_tokens), F32)],
        place,
        far,
        table,
        sums,
        far_w,
        others_slots,
        smem=1,
        cost=False,
    )
    line = n_exp == 4
    middle = ((1, 2), (2, 1))
    ends = ((1, 0), (2, 3))
    with jax.named_scope("spread_first"):
        if line:
            early = [swapped(slots, "exp", 1), lax.ppermute(slots, "exp", middle)]
        else:
            early = [swapped(slots, "exp", k) for k in range(1, n_exp)]
    merged = call(
        functools.partial(merge_kernel, flips=flips),
        "merge",
        shape((2, all_tokens, size), BF16),
        place,
        merge_labels,
        freq_counts,
        own,
        *peers,
        smem=3,
    )
    with jax.named_scope("spread_second"):
        second = [merged] + [swapped(merged, "exp", k) for k in range(1, n_exp)]
    with jax.named_scope("spread_first"):
        first = [slots] + early
        later = []
        if line:
            later = [lax.ppermute(early[0], "exp", middle), lax.ppermute(early[1], "exp", ends)]
            later[0], second[1] = lax.optimization_barrier((later[0], second[1]))
            first += later + [lax.ppermute(later[0], "exp", ends)]

    def grouped(pieces, *after):
        out = call(
            functools.partial(route_kernel, count=len(pieces)),
            "route",
            [shape((len(pieces), all_tokens, size), BF16) for _ in others],
            merge_labels,
            *pieces,
            *after,
            smem=1,
            unused=len(after),
        )
        with jax.named_scope("groups"):
            return out, [swapped(out[j - 1], "tok", j * span) for j in others]

    own_out, groups = grouped(second[:1], second[1])
    far_out, more = grouped(second[1:], *groups)
    initial = call(
        functools.partial(first_down_kernel, shard=shard, n_exp=n_exp, line=line),
        "first_down",
        shape((all_tokens, width), F32),
        place,
        table,
        w_down,
        *first,
        far_out[0],
        scratch=[pltpu.VMEM((all_tokens, n_exp * units), BF16)],
        smem=1,
        unused=1,
        cost=False,
    )
    ends = (n_tok // 2, 2, shard, width)
    keep, sent = call(
        functools.partial(second_down_kernel, flips=flips, n_exp=n_exp, shard=shard),
        "second_down",
        [shape(ends, F32), shape(ends, BF16)],
        place,
        merge_labels,
        freq_counts,
        table,
        w_down,
        initial,
        *second,
        *groups,
        *more,
        scratch=[pltpu.VMEM((all_tokens, n_exp * units), BF16)],
        smem=3,
        cost=False,
    )
    with jax.named_scope("cores"):
        theirs = swapped(sent, "tok", 1)
    piece = (2, shard, width)
    own, *sent = call(
        cores_kernel,
        "cores",
        [shape(piece, F32)] + [shape(piece, BF16) for _ in range(1, n_tok // 2)],
        keep,
        theirs,
    )
    with jax.named_scope("chips"):
        parts = [swapped(value, "tok", 2 * c) for c, value in enumerate(sent, 1)]
    return tuple(
        call(finish_kernel, "finish", [shape((shard, width), BF16)] * 2, own, *parts)
    )


def solution(mesh):
    return jax.shard_map(
        local,
        mesh=mesh,
        in_specs=(
            P("tok", "exp"),
            P("tok", None),
            P("tok", None),
            P(),
            P(),
            P(("tok", "exp"), None),
            P(("tok", "exp"), None),
            P("tok", "exp"),
        ),
        out_specs=(P("tok", "exp"), P("tok", "exp")),
        check_vma=False,
    )
```

time: 1810 us -> 96.3 us (0.05)
  blocking collectives: 845 us -> 0 us
  waiting for transfers between devices: 832 us -> 26.5 us
  matrix products: 84.6 us -> 0 us
  Pallas kernels: 0 us -> 28.7 us
  starting transfers between devices: 19.7 us -> 39.4 us
    all_to_all x1 -> x0, blocking collectives: 809 us -> none  [local(): lax.all_to_all(copies, 'tok', split_axis=0, concat_axis=0, tiled=True)]
    ppermute x9 -> x32, waiting for transfers between devices: 795 us -> 26.5 us  [the longest x28 23.8 us: swapped(): return lax.ppermute(value, axis, [(i, i ^ by) for i in range(devices)])]
    dot_general x8 -> x0, matrix products: 84.6 us -> none  [the longest x2 30.6 us: project(): jnp.einsum('sd,fd->sf', rows, gate_w, preferred_element_type=jnp.float32)]
    all_gather x2 -> x0, blocking collectives: 35.8 us -> none  [project(): units = lax.all_gather(hidden, 'exp', axis=1, tiled=True)]
    pallas_call x0 -> x13, Pallas kernels: none -> 28.7 us  [call(): pl.pallas_call(kernel, in_specs=specs, out_specs=[IN_VMEM] * len(out_shap...]
    all_gather x1 -> x0, waiting for transfers between devices: 26.5 us -> none  [local(): rows = lax.all_gather(rows_part, 'exp', axis=1, tiled=True)]
    ppermute x9 -> x32, starting transfers between devices: 16 us -> 39.4 us  [the longest x28 35.3 us: swapped(): return lax.ppermute(value, axis, [(i, i ^ by) for i in range(devices)])]
  transfers between devices with their start and end apart: 11 -> 32, of which waited for: 5 -> 13; matrix products, arithmetic and copies ran while one was open for 4% -> 0% of each run, Pallas kernels for 0% -> 20%
where the time goes in v2:
time: 96.3 us; the launch traced here: 96.1 us
  starting transfers between devices  39.4 us (41%)
  Pallas kernels  28.7 us (30%)
  waiting for transfers between devices  26.5 us (28%)
  between operations  1.02 us (1%)
    ppermute x28, starting transfers between devices, swapped(): return lax.ppermute(value, axis, [(i, i ^ by) for i in range(devices)])  35.3 us
    pallas_call x13, Pallas kernels, call(): pl.pallas_call(kernel, in_specs=specs, out_specs=[IN_VMEM] * len(out_shap...  28.7 us
    ppermute x28, waiting for transfers between devices, swapped(): return lax.ppermute(value, axis, [(i, i ^ by) for i in range(devices)])  23.8 us
    ppermute x1, waiting for transfers between devices, local(): first += later + [lax.ppermute(later[0], 'exp', ends)]  2.66 us
  transfers between devices with their start and end apart: 32, of which 13 were waited for; matrix products, arithmetic and copies ran while one was open for 0% of the time, Pallas kernels for 20%

profile of v2, /device:TPU:0, one launch (start us, length us, event | category | flops | bytes accessed | tf_op | source)
XLA Modules:
  0.0 96.1 jit_solution(4927961999819146364)
XLA Ops:
  0.6 3.1 %collective-permute-start = (bf16[16,1536]{1,0:T(8,128)(2,1)}, bf16[16,1536]{1,0:T(8,128)(2,1)S(1)}, u32[]{:S(2)}, u32[]{:S(2)}) collective-permute-start(bf16[16,1536]{1,0:T(8,128)(2,1)} %param.8), channel_id=1, source_target_pairs={{0,1},{1,0},{2,3},{3,2},{4,5},{5,4},{6,7},{7,6},{8,9},{9,8},{10,11... | collective-permute-start | bytes 147464 | tf_op jit(solution)/shard_map/gather_tokens/ppermute | solution.py:27
  3.7 2.5 %collective-permute-start.3 = (bf16[16,1536]{1,0:T(8,128)(2,1)}, bf16[16,1536]{1,0:T(8,128)(2,1)S(1)}, u32[]{:S(2)}, u32[]{:S(2)}) collective-permute-start(bf16[16,1536]{1,0:T(8,128)(2,1)} %param.8), channel_id=1, source_target_pairs={{0,3},{1,2},{2,1},{3,0},{4,7},{5,6},{6,5},{7,4},{8,11},{9,10},{10,... | collective-permute-start | bytes 147464 | tf_op jit(solution)/shard_map/gather_tokens/ppermute | solution.py:27
  6.2 0.1 collective-permute-start.2
  6.3 0.1 pad_add_fusion.place
  6.4 5.3 %load.2 = (bf16[2,2,1024,1536]{3,2,1,0:T(8,128)(2,1)S(1)}, f32[8,128]{1,0:T(8,128)S(1)}) custom-call(s32[2]{0:T(128)S(1)} %pad_add_fusion.place, bf16[1024,6144]{1,0:T(8,128)(2,1)} %refs_0_.4, bf16[1024,6144]{1,0:T(8,128)(2,1)} %refs_1_.3), custom_call_target="tpu_custom_call" | custom-call | tf_op jit(solution)/shard_map/load/pallas_call | solution.py:321
  11.7 0.2 notes.1
  12.0 1.6 %collective-permute-start.4 = (bf16[16,3200]{1,0:T(8,128)(2,1)S(1)}, bf16[16,3200]{1,0:T(8,128)(2,1)S(1)}, u32[]{:S(2)}, u32[]{:S(2)}) collective-permute-start(bf16[16,3200]{1,0:T(8,128)(2,1)S(1)} %get-tuple-element.54), channel_id=1, source_target_pairs={{0,16},{4,20},{8,24},{12,28},{16,0},{20,4},{24,8},{28,12},{1,17},{... | collective-permute-start | bytes 307208 | tf_op jit(solution)/shard_map/gather_tokens/ppermute | solution.py:27
  13.6 1.5 %collective-permute-start.1 = (bf16[16,3200]{1,0:T(8,128)(2,1)S(1)}, bf16[16,3200]{1,0:T(8,128)(2,1)S(1)}, u32[]{:S(2)}, u32[]{:S(2)}) collective-permute-start(bf16[16,3200]{1,0:T(8,128)(2,1)S(1)} %get-tuple-element.54), channel_id=1, source_target_pairs={{0,8},{4,12},{8,0},{12,4},{16,24},{20,28},{24,16},{28,20},{1,9},{5... | collective-permute-start | bytes 307208 | tf_op jit(solution)/shard_map/gather_tokens/ppermute | solution.py:27
  15.1 0.5 collective-permute-start.5
  15.6 2.9 %collective-permute-done.1 = bf16[16,3200]{1,0:T(8,128)(2,1)S(1)} collective-permute-done((bf16[16,3200]{1,0:T(8,128)(2,1)S(1)}, bf16[16,3200]{1,0:T(8,128)(2,1)S(1)}, u32[]{:S(2)}, u32[]{:S(2)}) %collective-permute-start.1) | collective-permute-done | bytes 102432 | tf_op jit(solution)/shard_map/gather_tokens/ppermute | solution.py:27
  18.5 1.5 %collective-permute-start.9 = (bf16[16,3072]{1,0:T(8,128)(2,1)S(1)}, bf16[16,3072]{1,0:T(8,128)(2,1)S(1)}, u32[]{:S(2)}, u32[]{:S(2)}) collective-permute-start(bf16[16,3072]{1,0:T(8,128)(2,1)S(1)} %pad_maximum_fusion.3), channel_id=1, source_target_pairs={{0,24},{4,28},{8,16},{12,20},{16,8},{20,12},{24,0},{28,4},{1,25},{... | collective-permute-start | bytes 294920 | tf_op jit(solution)/shard_map/gather_tokens/ppermute | solution.py:27
  20.0 1.4 %collective-permute-start.8 = (bf16[16,3072]{1,0:T(8,128)(2,1)S(1)}, bf16[16,3072]{1,0:T(8,128)(2,1)S(1)}, u32[]{:S(2)}, u32[]{:S(2)}) collective-permute-start(bf16[16,3072]{1,0:T(8,128)(2,1)S(1)} %pad_maximum_fusion.3), channel_id=1, source_target_pairs={{0,16},{4,20},{8,24},{12,28},{16,0},{20,4},{24,8},{28,12},{1,17},{... | collective-permute-start | bytes 294920 | tf_op jit(solution)/shard_map/gather_tokens/ppermute | solution.py:27
  21.5 0.6 collective-permute-start.7
  22.1 0.1 collective-permute-start.6
  22.2 5.3 %load.3 = (bf16[2,2,1024,1536]{3,2,1,0:T(8,128)(2,1)S(1)}, f32[8,128]{1,0:T(8,128)S(1)}) custom-call(s32[2]{0:T(128)S(1)} %pad_add_fusion.place, bf16[1024,6144]{1,0:T(8,128)(2,1)} %refs_0_.4, bf16[1024,6144]{1,0:T(8,128)(2,1)} %refs_1_.3, bf16[64,3200]{1,0:T(8,128)(2,1)S(1)} %pad_maximum_fusion.refs_2_), custom_call_target="tpu_custom_call" | custom-call | tf_op jit(solution)/shard_map/gather_tokens/load/pallas_call | solution.py:321
  27.6 0.6 collective-permute-start.10
  28.3 0.1 slice.9.x
  28.4 3.9 %project_first.1.sums = f32[4,2,256,128]{3,2,1,0:T(8,128)S(1)} custom-call(s32[2]{0:T(128)S(1)} %pad_add_fusion.place, bf16[128,3072]{1,0:T(8,128)(2,1)S(1)} %slice.9.x, bf16[2,2,1024,1536]{3,2,1,0:T(8,128)(2,1)S(1)} %get-tuple-element.31.blocks, f32[8,128]{1,0:T(8,128)S(1)} %get-tuple-element.32.refs_0_), custom_call_target="tpu_custom_call" | custom-call | tf_op jit(solution)/shard_map/project_first/pallas_call | solution.py:321
  32.3 0.0 copy-start
  32.4 0.0 copy-start.1
  32.4 0.0 slice-start
  32.4 0.0 slice-start.1
  32.4 3.9 %project_sent.1 = (bf16[96,768]{1,0:T(8,128)(2,1)S(1)}, bf16[2,256,128]{2,1,0:T(8,128)(2,1)S(1)}, bf16[2,256,128]{2,1,0:T(8,128)(2,1)S(1)}, bf16[2,256,128]{2,1,0:T(8,128)(2,1)S(1)}) custom-call(s32[2]{0:T(128)S(1)} %pad_add_fusion.place, bf16[128,3072]{1,0:T(8,128)(2,1)S(1)} %constant_dynamic-update-slice_fusion.5.x, bf16[128,128]{1,0:T(8,128)(2,1)S(1)} %slice.8.notes, ...), custom_call_target="tpu_custom_call" | custom-call | tf_op jit(solution)/shard_map/project_sent/pallas_call | solution.py:321
  36.3 0.0 slice-start.2
  36.3 1.7 %project_own.1 = (bf16[96,1024]{1,0:T(8,128)(2,1)S(1)}, f32[2,256,128]{2,1,0:T(8,128)S(1)}) custom-call(s32[2]{0:T(128)S(1)} %pad_add_fusion.place, bf16[128,3072]{1,0:T(8,128)(2,1)S(1)} %constant_dynamic-update-slice_fusion.5.x, bf16[128,128]{1,0:T(8,128)(2,1)S(1)} %slice.8.notes, f32[4,2,256,128]{3,2,1,0:T(8,128)S(1)} %project_first.1.sums, ...), custom_call_target="tpu_custom_call" | custom-call | tf_op jit(solution)/shard_map/project_own/pallas_call | solution.py:321
  38.0 1.6 %collective-permute-start.11 = (bf16[96,1024]{1,0:T(8,128)(2,1)S(1)}, bf16[96,1024]{1,0:T(8,128)(2,1)S(1)}, u32[]{:S(2)}, u32[]{:S(2)}) collective-permute-start(bf16[96,1024]{1,0:T(8,128)(2,1)S(1)} %get-tuple-element.35.refs_1_), channel_id=1, source_target_pairs={{0,1},{1,0},{2,3},{3,2},{4,5},{5,4},{6,7},{7,6},{8,9},{9,8},{10,11... | collective-permute-start | bytes 589832 | tf_op jit(solution)/shard_map/spread_first/ppermute | solution.py:27
  39.7 1.4 %collective-permute-start.14 = (bf16[2,256,128]{2,1,0:T(8,128)(2,1)S(1)}, bf16[2,256,128]{2,1,0:T(8,128)(2,1)S(1)}, u32[]{:S(2)}, u32[]{:S(2)}) collective-permute-start(bf16[2,256,128]{2,1,0:T(8,128)(2,1)S(1)} %get-tuple-element.37), channel_id=1, source_target_pairs={{0,8},{4,12},{8,0},{12,4},{16,24},{20,28},{24,16},{28,20},{1,9},{5... | collective-permute-start | bytes 393224 | tf_op jit(solution)/shard_map/peers/ppermute | solution.py:27
  41.1 0.6 collective-permute-start.15
  41.7 1.4 %collective-permute-start.16 = (bf16[2,256,128]{2,1,0:T(8,128)(2,1)S(1)}, bf16[2,256,128]{2,1,0:T(8,128)(2,1)S(1)}, u32[]{:S(2)}, u32[]{:S(2)}) collective-permute-start(bf16[2,256,128]{2,1,0:T(8,128)(2,1)S(1)} %get-tuple-element.39), channel_id=1, source_target_pairs={{0,24},{4,28},{8,16},{12,20},{16,8},{20,12},{24,0},{28,4},{1,25},{... | collective-permute-start | bytes 393224 | tf_op jit(solution)/shard_map/peers/ppermute | solution.py:27
  43.2 1.8 %collective-permute-done.11.refs_2_ = bf16[96,1024]{1,0:T(8,128)(2,1)S(1)} collective-permute-done((bf16[96,1024]{1,0:T(8,128)(2,1)S(1)}, bf16[96,1024]{1,0:T(8,128)(2,1)S(1)}, u32[]{:S(2)}, u32[]{:S(2)}) %collective-permute-start.11) | collective-permute-done | bytes 196640 | tf_op jit(solution)/shard_map/spread_first/ppermute | solution.py:27
  44.9 0.7 collective-permute-start.13
  45.6 0.7 collective-permute-start.12
  46.3 2.5 %collective-permute-done.15.refs_1_ = bf16[2,256,128]{2,1,0:T(8,128)(2,1)S(1)} collective-permute-done((bf16[2,256,128]{2,1,0:T(8,128)(2,1)S(1)}, bf16[2,256,128]{2,1,0:T(8,128)(2,1)S(1)}, u32[]{:S(2)}, u32[]{:S(2)}) %collective-permute-start.15) | collective-permute-done | bytes 131104 | tf_op jit(solution)/shard_map/peers/ppermute | solution.py:27
  48.8 1.0 %merge.1.refs_0_ = bf16[2,128,256]{2,1,0:T(8,128)(2,1)S(1)} custom-call(s32[2]{0:T(128)S(1)} %pad_add_fusion.place, s32[4]{0:T(128)S(1)} %copy-done, s32[4]{0:T(128)S(1)} %copy-done.1, f32[2,256,128]{2,1,0:T(8,128)S(1)} %get-tuple-element.36.own, bf16[2,256,128]{2,1,0:T(8,128)(2,1)S(1)} %collective-permute-done.14.refs_0_, ...), custom_call_target="tpu_custom_call" | custom-call | flops 1 | bytes 1 | tf_op jit(solution)/shard_map/merge/pallas_call | solution.py:321
  49.8 3.7 %collective-permute-start.17 = (bf16[2,128,256]{2,1,0:T(8,128)(2,1)S(1)}, bf16[2,128,256]{2,1,0:T(8,128)(2,1)S(1)}, u32[]{:S(2)}, u32[]{:S(2)}) collective-permute-start(bf16[2,128,256]{2,1,0:T(8,128)(2,1)S(1)} %merge.1.refs_0_), channel_id=1, source_target_pairs={{0,1},{1,0},{2,3},{3,2},{4,5},{5,4},{6,7},{7,6},{8,9},{9,8},{10,11... | collective-permute-start | bytes 393224 | tf_op jit(solution)/shard_map/spread_second/ppermute | solution.py:27
  53.4 2.5 %collective-permute-start.21 = (bf16[2,128,256]{2,1,0:T(8,128)(2,1)S(1)}, bf16[2,128,256]{2,1,0:T(8,128)(2,1)S(1)}, u32[]{:S(2)}, u32[]{:S(2)}) collective-permute-start(bf16[2,128,256]{2,1,0:T(8,128)(2,1)S(1)} %merge.1.refs_0_), channel_id=1, source_target_pairs={{0,3},{1,2},{2,1},{3,0},{4,7},{5,6},{6,5},{7,4},{8,11},{9,10},{10,... | collective-permute-start | bytes 393224 | tf_op jit(solution)/shard_map/spread_second/ppermute | solution.py:27
  55.9 1.4 %collective-permute-done.17.refs_1_.refs_0_ = bf16[2,128,256]{2,1,0:T(8,128)(2,1)S(1)} collective-permute-done((bf16[2,128,256]{2,1,0:T(8,128)(2,1)S(1)}, bf16[2,128,256]{2,1,0:T(8,128)(2,1)S(1)}, u32[]{:S(2)}, u32[]{:S(2)}) %collective-permute-start.17) | collective-permute-done | bytes 131104 | tf_op jit(solution)/shard_map/spread_second/ppermute | solution.py:27
  57.3 0.6 route.2
  57.9 1.5 %collective-permute-start.22 = (bf16[1,128,256]{2,1,0:T(8,128)(2,1)S(1)}, bf16[1,128,256]{2,1,0:T(8,128)(2,1)S(1)}, u32[]{:S(2)}, u32[]{:S(2)}) collective-permute-start(bf16[1,128,256]{2,1,0:T(8,128)(2,1)S(1)} %get-tuple-element.42), channel_id=1, source_target_pairs={{0,8},{4,12},{8,0},{12,4},{16,24},{20,28},{24,16},{28,20},{1,9},{5... | collective-permute-start | bytes 196616 | tf_op jit(solution)/shard_map/groups/ppermute | solution.py:27
  59.4 0.6 collective-permute-start.23
  60.0 1.4 %collective-permute-start.24 = (bf16[1,128,256]{2,1,0:T(8,128)(2,1)S(1)}, bf16[1,128,256]{2,1,0:T(8,128)(2,1)S(1)}, u32[]{:S(2)}, u32[]{:S(2)}) collective-permute-start(bf16[1,128,256]{2,1,0:T(8,128)(2,1)S(1)} %get-tuple-element.44), channel_id=1, source_target_pairs={{0,24},{4,28},{8,16},{12,20},{16,8},{20,12},{24,0},{28,4},{1,25},{... | collective-permute-start | bytes 196616 | tf_op jit(solution)/shard_map/groups/ppermute | solution.py:27
  61.5 0.8 collective-permute-done.21.refs_2_.refs_3_
  62.2 1.3 %collective-permute-start.18 = (bf16[96,1024]{1,0:T(8,128)(2,1)S(1)}, bf16[96,1024]{1,0:T(8,128)(2,1)S(1)}, u32[]{:S(2)}, u32[]{:S(2)}) collective-permute-start(bf16[96,1024]{1,0:T(8,128)(2,1)S(1)} %collective-permute-done.12.refs_3_), channel_id=1, source_target_pairs={{1,0},{2,3},{5,4},{6,7},{9,8},{10,11},{13,12},{14,15},{17,16},{18,... | collective-permute-start | bytes 589832 | tf_op jit(solution)/shard_map/spread_first/ppermute | solution.py:439
  63.5 5.9 %collective-permute-done.20.refs_1_.refs_2_ = bf16[2,128,256]{2,1,0:T(8,128)(2,1)S(1)} collective-permute-done((bf16[2,128,256]{2,1,0:T(8,128)(2,1)S(1)}, bf16[2,128,256]{2,1,0:T(8,128)(2,1)S(1)}, u32[]{:S(2)}, u32[]{:S(2)}) %collective-permute-start.20) | collective-permute-done | bytes 131104 | tf_op jit(solution)/shard_map/spread_second/ppermute | solution.py:27
  69.4 1.5 %collective-permute-start.19 = (bf16[96,1024]{1,0:T(8,128)(2,1)S(1)}, bf16[96,1024]{1,0:T(8,128)(2,1)S(1)}, u32[]{:S(2)}, u32[]{:S(2)}) collective-permute-start(bf16[96,1024]{1,0:T(8,128)(2,1)S(1)} %collective-permute-done.13.refs_4_), channel_id=1, source_target_pairs={{1,0},{2,3},{5,4},{6,7},{9,8},{10,11},{13,12},{14,15},{17,16},{18,... | collective-permute-start | bytes 589832 | tf_op jit(solution)/shard_map/spread_first/ppermute | solution.py:441
  70.9 0.6 route.3
  71.5 1.5 %collective-permute-start.26 = (bf16[3,128,256]{2,1,0:T(8,128)(2,1)S(1)}, bf16[3,128,256]{2,1,0:T(8,128)(2,1)S(1)}, u32[]{:S(2)}, u32[]{:S(2)}) collective-permute-start(bf16[3,128,256]{2,1,0:T(8,128)(2,1)S(1)} %get-tuple-element.46), channel_id=1, source_target_pairs={{0,16},{4,20},{8,24},{12,28},{16,0},{20,4},{24,8},{28,12},{1,17},{... | collective-permute-start | bytes 589832 | tf_op jit(solution)/shard_map/groups/ppermute | solution.py:27
  73.0 1.4 %collective-permute-start.27 = (bf16[3,128,256]{2,1,0:T(8,128)(2,1)S(1)}, bf16[3,128,256]{2,1,0:T(8,128)(2,1)S(1)}, u32[]{:S(2)}, u32[]{:S(2)}) collective-permute-start(bf16[3,128,256]{2,1,0:T(8,128)(2,1)S(1)} %get-tuple-element.47), channel_id=1, source_target_pairs={{0,24},{4,28},{8,16},{12,20},{16,8},{20,12},{24,0},{28,4},{1,25},{... | collective-permute-start | bytes 589832 | tf_op jit(solution)/shard_map/groups/ppermute | solution.py:27
  74.4 0.6 collective-permute-start.25
  75.0 2.7 %collective-permute-done.19.refs_6_ = bf16[96,1024]{1,0:T(8,128)(2,1)S(1)} collective-permute-done((bf16[96,1024]{1,0:T(8,128)(2,1)S(1)}, bf16[96,1024]{1,0:T(8,128)(2,1)S(1)}, u32[]{:S(2)}, u32[]{:S(2)}) %collective-permute-start.19) | collective-permute-done | bytes 196640 | tf_op jit(solution)/shard_map/spread_first/ppermute | solution.py:441
  77.7 2.8 %first_down.1.initial = f32[128,1536]{1,0:T(8,128)S(1)} custom-call(s32[2]{0:T(128)S(1)} %pad_add_fusion.place, bf16[128,128]{1,0:T(8,128)(2,1)S(1)} %slice.8.notes, bf16[4096,1536]{1,0:T(8,128)(2,1)S(1)} %bitcast.5, bf16[96,1024]{1,0:T(8,128)(2,1)S(1)} %get-tuple-element.35.refs_1_, bf16[96,1024]{1,0:T(8,128)(2,1)S(1)} %collective-permute-done.11.refs_2_, ...), custom_call_target="tpu_custom_call" | custom-call | tf_op jit(solution)/shard_map/first_down/pallas_call | solution.py:321
  80.5 0.6 collective-permute-done.26.refs_8_
  81.1 0.4 collective-permute-done.27.refs_9_
  81.5 1.2 %collective-permute-done.25.refs_7_ = bf16[3,128,256]{2,1,0:T(8,128)(2,1)S(1)} collective-permute-done((bf16[3,128,256]{2,1,0:T(8,128)(2,1)S(1)}, bf16[3,128,256]{2,1,0:T(8,128)(2,1)S(1)}, u32[]{:S(2)}, u32[]{:S(2)}) %collective-permute-start.25) | collective-permute-done | bytes 196640 | tf_op jit(solution)/shard_map/groups/ppermute | solution.py:27
  82.6 2.6 %second_down.1 = (f32[4,2,16,1536]{3,2,1,0:T(8,128)S(1)}, bf16[4,2,16,1536]{3,2,1,0:T(8,128)(2,1)S(1)}) custom-call(s32[2]{0:T(128)S(1)} %pad_add_fusion.place, s32[4]{0:T(128)S(1)} %copy-done, s32[4]{0:T(128)S(1)} %copy-done.1, bf16[128,128]{1,0:T(8,128)(2,1)S(1)} %slice.8.notes, bf16[4096,1536]{1,0:T(8,128)(2,1)S(1)} %bitcast.5, ...), custom_call_target="tpu_custom_call" | custom-call | tf_op jit(solution)/shard_map/second_down/pallas_call | solution.py:321
  85.3 0.1 collective-permute-start.28
  85.4 1.7 %collective-permute-done.28.theirs = bf16[4,2,16,1536]{3,2,1,0:T(8,128)(2,1)S(1)} collective-permute-done((bf16[4,2,16,1536]{3,2,1,0:T(8,128)(2,1)S(1)}, bf16[4,2,16,1536]{3,2,1,0:T(8,128)(2,1)S(1)}, u32[]{:S(2)}, u32[]{:S(2)}) %collective-permute-start.28) | collective-permute-done | bytes 393248 | tf_op jit(solution)/shard_map/cores/ppermute | solution.py:27
  87.1 0.1 cores.1
  87.2 1.5 %collective-permute-start.29 = (bf16[2,16,1536]{2,1,0:T(8,128)(2,1)S(1)}, bf16[2,16,1536]{2,1,0:T(8,128)(2,1)S(1)}, u32[]{:S(2)}, u32[]{:S(2)}) collective-permute-start(bf16[2,16,1536]{2,1,0:T(8,128)(2,1)S(1)} %get-tuple-element.51), channel_id=1, source_target_pairs={{0,8},{4,12},{8,0},{12,4},{16,24},{20,28},{24,16},{28,20},{1,9},{5... | collective-permute-start | bytes 294920 | tf_op jit(solution)/shard_map/chips/ppermute | solution.py:27
  88.7 0.6 collective-permute-start.30
  89.3 1.4 %collective-permute-start.31 = (bf16[2,16,1536]{2,1,0:T(8,128)(2,1)S(1)}, bf16[2,16,1536]{2,1,0:T(8,128)(2,1)S(1)}, u32[]{:S(2)}, u32[]{:S(2)}) collective-permute-start(bf16[2,16,1536]{2,1,0:T(8,128)(2,1)S(1)} %get-tuple-element.53), channel_id=1, source_target_pairs={{0,24},{4,28},{8,16},{12,20},{16,8},{20,12},{24,0},{28,4},{1,25},{... | collective-permute-start | bytes 294920 | tf_op jit(solution)/shard_map/chips/ppermute | solution.py:27
  90.7 1.3 %collective-permute-done.29.refs_0_ = bf16[2,16,1536]{2,1,0:T(8,128)(2,1)S(1)} collective-permute-done((bf16[2,16,1536]{2,1,0:T(8,128)(2,1)S(1)}, bf16[2,16,1536]{2,1,0:T(8,128)(2,1)S(1)}, u32[]{:S(2)}, u32[]{:S(2)}) %collective-permute-start.29) | collective-permute-done | bytes 98336 | tf_op jit(solution)/shard_map/chips/ppermute | solution.py:27
  92.1 3.3 %collective-permute-done.30.refs_1_ = bf16[2,16,1536]{2,1,0:T(8,128)(2,1)S(1)} collective-permute-done((bf16[2,16,1536]{2,1,0:T(8,128)(2,1)S(1)}, bf16[2,16,1536]{2,1,0:T(8,128)(2,1)S(1)}, u32[]{:S(2)}, u32[]{:S(2)}) %collective-permute-start.30) | collective-permute-done | bytes 98336 | tf_op jit(solution)/shard_map/chips/ppermute | solution.py:27
  95.4 0.7 finish.1
  (46 shorter events, 0.3 us)
Async XLA Ops:
  0.6 11.3 %collective-permute-start = (bf16[16,1536]{1,0:T(8,128)(2,1)}, bf16[16,1536]{1,0:T(8,128)(2,1)S(1)}, u32[]{:S(2)}, u32[]{:S(2)}) collective-permute-start(bf16[16,1536]{1,0:T(8,128)(2,1)} %param.8), channel_id=1, source_target_pairs={{0,1},{1,0},{2,3},{3,2},{4,5},{5,4},{6,7},{7,6},{8,9},{9,8},{10,11... | collective-permute-start | bytes 147464 | tf_op jit(solution)/shard_map/gather_tokens/ppermute | solution.py:27
  3.7 11.9 %collective-permute-start.3 = (bf16[16,1536]{1,0:T(8,128)(2,1)}, bf16[16,1536]{1,0:T(8,128)(2,1)S(1)}, u32[]{:S(2)}, u32[]{:S(2)}) collective-permute-start(bf16[16,1536]{1,0:T(8,128)(2,1)} %param.8), channel_id=1, source_target_pairs={{0,3},{1,2},{2,1},{3,0},{4,7},{5,6},{6,5},{7,4},{8,11},{9,10},{10,... | collective-permute-start | bytes 147464 | tf_op jit(solution)/shard_map/gather_tokens/ppermute | solution.py:27
  6.2 9.4 %collective-permute-start.2 = (bf16[16,1536]{1,0:T(8,128)(2,1)}, bf16[16,1536]{1,0:T(8,128)(2,1)S(1)}, u32[]{:S(2)}, u32[]{:S(2)}) collective-permute-start(bf16[16,1536]{1,0:T(8,128)(2,1)} %param.8), channel_id=1, source_target_pairs={{0,2},{1,3},{2,0},{3,1},{4,6},{5,7},{6,4},{7,5},{8,10},{9,11},{10,... | collective-permute-start | bytes 147464 | tf_op jit(solution)/shard_map/gather_tokens/ppermute | solution.py:27
  6.4 5.3 %copy-start.2 = (s32[16,2]{0,1:T(2,128)S(1)}, s32[16,2]{0,1:T(2,128)}, u32[]{:S(2)}) copy-start(s32[16,2]{0,1:T(2,128)} %param.9) | copy-start | bytes 388
  6.4 5.3 %copy-start.3 = (s32[16,2]{0,1:T(2,128)S(1)}, s32[16,2]{0,1:T(2,128)}, u32[]{:S(2)}) copy-start(s32[16,2]{0,1:T(2,128)} %param.10) | copy-start | bytes 388
  6.4 5.6 %copy-start.4 = (bf16[16,1536]{1,0:T(8,128)(2,1)S(1)}, bf16[16,1536]{1,0:T(8,128)(2,1)}, u32[]{:S(2)}) copy-start(bf16[16,1536]{1,0:T(8,128)(2,1)} %param.8) | copy-start | bytes 147460
  12.0 10.0 %collective-permute-start.4 = (bf16[16,3200]{1,0:T(8,128)(2,1)S(1)}, bf16[16,3200]{1,0:T(8,128)(2,1)S(1)}, u32[]{:S(2)}, u32[]{:S(2)}) collective-permute-start(bf16[16,3200]{1,0:T(8,128)(2,1)S(1)} %get-tuple-element.54), channel_id=1, source_target_pairs={{0,16},{4,20},{8,24},{12,28},{16,0},{20,4},{24,8},{28,12},{1,17},{... | collective-permute-start | bytes 307208 | tf_op jit(solution)/shard_map/gather_tokens/ppermute | solution.py:27
  13.6 4.9 %collective-permute-start.1 = (bf16[16,3200]{1,0:T(8,128)(2,1)S(1)}, bf16[16,3200]{1,0:T(8,128)(2,1)S(1)}, u32[]{:S(2)}, u32[]{:S(2)}) collective-permute-start(bf16[16,3200]{1,0:T(8,128)(2,1)S(1)} %get-tuple-element.54), channel_id=1, source_target_pairs={{0,8},{4,12},{8,0},{12,4},{16,24},{20,28},{24,16},{28,20},{1,9},{5... | collective-permute-start | bytes 307208 | tf_op jit(solution)/shard_map/gather_tokens/ppermute | solution.py:27
  15.1 7.0 %collective-permute-start.5 = (bf16[16,3200]{1,0:T(8,128)(2,1)S(1)}, bf16[16,3200]{1,0:T(8,128)(2,1)S(1)}, u32[]{:S(2)}, u32[]{:S(2)}) collective-permute-start(bf16[16,3200]{1,0:T(8,128)(2,1)S(1)} %get-tuple-element.54), channel_id=1, source_target_pairs={{0,24},{4,28},{8,16},{12,20},{16,8},{20,12},{24,0},{28,4},{1,25},{... | collective-permute-start | bytes 307208 | tf_op jit(solution)/shard_map/gather_tokens/ppermute | solution.py:27
  18.5 9.0 %collective-permute-start.9 = (bf16[16,3072]{1,0:T(8,128)(2,1)S(1)}, bf16[16,3072]{1,0:T(8,128)(2,1)S(1)}, u32[]{:S(2)}, u32[]{:S(2)}) collective-permute-start(bf16[16,3072]{1,0:T(8,128)(2,1)S(1)} %pad_maximum_fusion.3), channel_id=1, source_target_pairs={{0,24},{4,28},{8,16},{12,20},{16,8},{20,12},{24,0},{28,4},{1,25},{... | collective-permute-start | bytes 294920 | tf_op jit(solution)/shard_map/gather_tokens/ppermute | solution.py:27
  20.0 7.5 %collective-permute-start.8 = (bf16[16,3072]{1,0:T(8,128)(2,1)S(1)}, bf16[16,3072]{1,0:T(8,128)(2,1)S(1)}, u32[]{:S(2)}, u32[]{:S(2)}) collective-permute-start(bf16[16,3072]{1,0:T(8,128)(2,1)S(1)} %pad_maximum_fusion.3), channel_id=1, source_target_pairs={{0,16},{4,20},{8,24},{12,28},{16,0},{20,4},{24,8},{28,12},{1,17},{... | collective-permute-start | bytes 294920 | tf_op jit(solution)/shard_map/gather_tokens/ppermute | solution.py:27
  21.5 6.1 %collective-permute-start.7 = (bf16[16,3072]{1,0:T(8,128)(2,1)S(1)}, bf16[16,3072]{1,0:T(8,128)(2,1)S(1)}, u32[]{:S(2)}, u32[]{:S(2)}) collective-permute-start(bf16[16,3072]{1,0:T(8,128)(2,1)S(1)} %pad_maximum_fusion.3), channel_id=1, source_target_pairs={{0,8},{4,12},{8,0},{12,4},{16,24},{20,28},{24,16},{28,20},{1,9},{5... | collective-permute-start | bytes 294920 | tf_op jit(solution)/shard_map/gather_tokens/ppermute | solution.py:27
  22.1 6.1 %collective-permute-start.6 = (bf16[64,3200]{1,0:T(8,128)(2,1)S(1)}, bf16[64,3200]{1,0:T(8,128)(2,1)S(1)}, u32[]{:S(2)}, u32[]{:S(2)}) collective-permute-start(bf16[64,3200]{1,0:T(8,128)(2,1)S(1)} %pad_maximum_fusion.refs_2_), channel_id=1, source_target_pairs={{0,4},{4,0},{8,12},{12,8},{16,20},{20,16},{24,28},{28,24},{1,5},{5... | collective-permute-start | bytes 1228808 | tf_op jit(solution)/shard_map/gather_tokens/ppermute | solution.py:27
  27.6 4.7 %collective-permute-start.10 = (bf16[64,3072]{1,0:T(8,128)(2,1)S(1)}, bf16[64,3072]{1,0:T(8,128)(2,1)S(1)}, u32[]{:S(2)}, u32[]{:S(2)}) collective-permute-start(bf16[64,3072]{1,0:T(8,128)(2,1)S(1)} %pad_maximum_fusion.1), channel_id=1, source_target_pairs={{0,4},{4,0},{8,12},{12,8},{16,20},{20,16},{24,28},{28,24},{1,5},{5... | collective-permute-start | bytes 1179656 | tf_op jit(solution)/shard_map/gather_tokens/ppermute | solution.py:27
  32.3 16.5 %copy-start = (s32[4]{0:T(128)S(1)}, s32[4]{0:T(128)}, u32[]{:S(2)}) copy-start(s32[4]{0:T(128)} %labels.7) | copy-start | bytes 52
  32.4 16.4 %copy-start.1 = (s32[4]{0:T(128)S(1)}, s32[4]{0:T(128)}, u32[]{:S(2)}) copy-start(s32[4]{0:T(128)} %freq.3) | copy-start | bytes 52
  32.4 45.3 %slice-start = ((s8[12582912]{0:T(1024)(128)(4,1)}), s8[4194304]{0:T(1024)(128)(4,1)S(1)}, s32[]{:S(2)}) async-start(s8[12582912]{0:T(1024)(128)(4,1)} %bitcast.4), calls=%async_computation | async-start | bytes 8388608
  32.4 45.3 %slice-start.1 = ((s8[12582912]{0:T(1024)(128)(4,1)}), s8[4194304]{0:T(1024)(128)(4,1)S(1)}, s32[]{:S(2)}) async-start(s8[12582912]{0:T(1024)(128)(4,1)} %bitcast.4), calls=%async_computation.1 | async-start | bytes 8388608
  36.3 41.4 %slice-start.2 = ((s8[12582912]{0:T(1024)(128)(4,1)}), s8[4194304]{0:T(1024)(128)(4,1)S(1)}, s32[]{:S(2)}) async-start(s8[12582912]{0:T(1024)(128)(4,1)} %bitcast.4), calls=%async_computation.2 | async-start | bytes 8388608
  38.0 6.9 %collective-permute-start.11 = (bf16[96,1024]{1,0:T(8,128)(2,1)S(1)}, bf16[96,1024]{1,0:T(8,128)(2,1)S(1)}, u32[]{:S(2)}, u32[]{:S(2)}) collective-permute-start(bf16[96,1024]{1,0:T(8,128)(2,1)S(1)} %get-tuple-element.35.refs_1_), channel_id=1, source_target_pairs={{0,1},{1,0},{2,3},{3,2},{4,5},{5,4},{6,7},{7,6},{8,9},{9,8},{10,11... | collective-permute-start | bytes 589832 | tf_op jit(solution)/shard_map/spread_first/ppermute | solution.py:27
  39.7 6.6 %collective-permute-start.14 = (bf16[2,256,128]{2,1,0:T(8,128)(2,1)S(1)}, bf16[2,256,128]{2,1,0:T(8,128)(2,1)S(1)}, u32[]{:S(2)}, u32[]{:S(2)}) collective-permute-start(bf16[2,256,128]{2,1,0:T(8,128)(2,1)S(1)} %get-tuple-element.37), channel_id=1, source_target_pairs={{0,8},{4,12},{8,0},{12,4},{16,24},{20,28},{24,16},{28,20},{1,9},{5... | collective-permute-start | bytes 393224 | tf_op jit(solution)/shard_map/peers/ppermute | solution.py:27
  41.1 7.7 %collective-permute-start.15 = (bf16[2,256,128]{2,1,0:T(8,128)(2,1)S(1)}, bf16[2,256,128]{2,1,0:T(8,128)(2,1)S(1)}, u32[]{:S(2)}, u32[]{:S(2)}) collective-permute-start(bf16[2,256,128]{2,1,0:T(8,128)(2,1)S(1)} %get-tuple-element.38), channel_id=1, source_target_pairs={{0,16},{4,20},{8,24},{12,28},{16,0},{20,4},{24,8},{28,12},{1,17},{... | collective-permute-start | bytes 393224 | tf_op jit(solution)/shard_map/peers/ppermute | solution.py:27
  41.7 7.1 %collective-permute-start.16 = (bf16[2,256,128]{2,1,0:T(8,128)(2,1)S(1)}, bf16[2,256,128]{2,1,0:T(8,128)(2,1)S(1)}, u32[]{:S(2)}, u32[]{:S(2)}) collective-permute-start(bf16[2,256,128]{2,1,0:T(8,128)(2,1)S(1)} %get-tuple-element.39), channel_id=1, source_target_pairs={{0,24},{4,28},{8,16},{12,20},{16,8},{20,12},{24,0},{28,4},{1,25},{... | collective-permute-start | bytes 393224 | tf_op jit(solution)/shard_map/peers/ppermute | solution.py:27
  44.9 12.4 %collective-permute-start.13 = (bf16[96,1024]{1,0:T(8,128)(2,1)S(1)}, bf16[96,1024]{1,0:T(8,128)(2,1)S(1)}, u32[]{:S(2)}, u32[]{:S(2)}) collective-permute-start(bf16[96,1024]{1,0:T(8,128)(2,1)S(1)} %collective-permute-done.11.refs_2_), channel_id=1, source_target_pairs={{1,2},{2,1},{5,6},{6,5},{9,10},{10,9},{13,14},{14,13},{17,18},{18,... | collective-permute-start | bytes 589832 | tf_op jit(solution)/shard_map/spread_first/ppermute | solution.py:439
  45.6 14.4 %collective-permute-start.12 = (bf16[96,1024]{1,0:T(8,128)(2,1)S(1)}, bf16[96,1024]{1,0:T(8,128)(2,1)S(1)}, u32[]{:S(2)}, u32[]{:S(2)}) collective-permute-start(bf16[96,1024]{1,0:T(8,128)(2,1)S(1)} %get-tuple-element.35.refs_1_), channel_id=1, source_target_pairs={{1,2},{2,1},{5,6},{6,5},{9,10},{10,9},{13,14},{14,13},{17,18},{18,... | collective-permute-start | bytes 589832 | tf_op jit(solution)/shard_map/spread_first/ppermute | solution.py:419
  49.8 7.5 %collective-permute-start.17 = (bf16[2,128,256]{2,1,0:T(8,128)(2,1)S(1)}, bf16[2,128,256]{2,1,0:T(8,128)(2,1)S(1)}, u32[]{:S(2)}, u32[]{:S(2)}) collective-permute-start(bf16[2,128,256]{2,1,0:T(8,128)(2,1)S(1)} %merge.1.refs_0_), channel_id=1, source_target_pairs={{0,1},{1,0},{2,3},{3,2},{4,5},{5,4},{6,7},{7,6},{8,9},{9,8},{10,11... | collective-permute-start | bytes 393224 | tf_op jit(solution)/shard_map/spread_second/ppermute | solution.py:27
  53.4 8.8 %collective-permute-start.21 = (bf16[2,128,256]{2,1,0:T(8,128)(2,1)S(1)}, bf16[2,128,256]{2,1,0:T(8,128)(2,1)S(1)}, u32[]{:S(2)}, u32[]{:S(2)}) collective-permute-start(bf16[2,128,256]{2,1,0:T(8,128)(2,1)S(1)} %merge.1.refs_0_), channel_id=1, source_target_pairs={{0,3},{1,2},{2,1},{3,0},{4,7},{5,6},{6,5},{7,4},{8,11},{9,10},{10,... | collective-permute-start | bytes 393224 | tf_op jit(solution)/shard_map/spread_second/ppermute | solution.py:27
  55.9 13.4 %collective-permute-start.20 = (bf16[2,128,256]{2,1,0:T(8,128)(2,1)S(1)}, bf16[2,128,256]{2,1,0:T(8,128)(2,1)S(1)}, u32[]{:S(2)}, u32[]{:S(2)}) collective-permute-start(bf16[2,128,256]{2,1,0:T(8,128)(2,1)S(1)} %merge.1.refs_0_), channel_id=1, source_target_pairs={{0,2},{1,3},{2,0},{3,1},{4,6},{5,7},{6,4},{7,5},{8,10},{9,11},{10,... | collective-permute-start | bytes 393224 | tf_op jit(solution)/shard_map/spread_second/ppermute | solution.py:27
  57.9 12.9 %collective-permute-start.22 = (bf16[1,128,256]{2,1,0:T(8,128)(2,1)S(1)}, bf16[1,128,256]{2,1,0:T(8,128)(2,1)S(1)}, u32[]{:S(2)}, u32[]{:S(2)}) collective-permute-start(bf16[1,128,256]{2,1,0:T(8,128)(2,1)S(1)} %get-tuple-element.42), channel_id=1, source_target_pairs={{0,8},{4,12},{8,0},{12,4},{16,24},{20,28},{24,16},{28,20},{1,9},{5... | collective-permute-start | bytes 196616 | tf_op jit(solution)/shard_map/groups/ppermute | solution.py:27
  59.4 11.4 %collective-permute-start.23 = (bf16[1,128,256]{2,1,0:T(8,128)(2,1)S(1)}, bf16[1,128,256]{2,1,0:T(8,128)(2,1)S(1)}, u32[]{:S(2)}, u32[]{:S(2)}) collective-permute-start(bf16[1,128,256]{2,1,0:T(8,128)(2,1)S(1)} %get-tuple-element.43), channel_id=1, source_target_pairs={{0,16},{4,20},{8,24},{12,28},{16,0},{20,4},{24,8},{28,12},{1,17},{... | collective-permute-start | bytes 196616 | tf_op jit(solution)/shard_map/groups/ppermute | solution.py:27
  60.0 10.8 %collective-permute-start.24 = (bf16[1,128,256]{2,1,0:T(8,128)(2,1)S(1)}, bf16[1,128,256]{2,1,0:T(8,128)(2,1)S(1)}, u32[]{:S(2)}, u32[]{:S(2)}) collective-permute-start(bf16[1,128,256]{2,1,0:T(8,128)(2,1)S(1)} %get-tuple-element.44), channel_id=1, source_target_pairs={{0,24},{4,28},{8,16},{12,20},{16,8},{20,12},{24,0},{28,4},{1,25},{... | collective-permute-start | bytes 196616 | tf_op jit(solution)/shard_map/groups/ppermute | solution.py:27
  62.2 12.8 %collective-permute-start.18 = (bf16[96,1024]{1,0:T(8,128)(2,1)S(1)}, bf16[96,1024]{1,0:T(8,128)(2,1)S(1)}, u32[]{:S(2)}, u32[]{:S(2)}) collective-permute-start(bf16[96,1024]{1,0:T(8,128)(2,1)S(1)} %collective-permute-done.12.refs_3_), channel_id=1, source_target_pairs={{1,0},{2,3},{5,4},{6,7},{9,8},{10,11},{13,12},{14,15},{17,16},{18,... | collective-permute-start | bytes 589832 | tf_op jit(solution)/shard_map/spread_first/ppermute | solution.py:439
  69.4 8.3 %collective-permute-start.19 = (bf16[96,1024]{1,0:T(8,128)(2,1)S(1)}, bf16[96,1024]{1,0:T(8,128)(2,1)S(1)}, u32[]{:S(2)}, u32[]{:S(2)}) collective-permute-start(bf16[96,1024]{1,0:T(8,128)(2,1)S(1)} %collective-permute-done.13.refs_4_), channel_id=1, source_target_pairs={{1,0},{2,3},{5,4},{6,7},{9,8},{10,11},{13,12},{14,15},{17,16},{18,... | collective-permute-start | bytes 589832 | tf_op jit(solution)/shard_map/spread_first/ppermute | solution.py:441
  71.5 9.6 %collective-permute-start.26 = (bf16[3,128,256]{2,1,0:T(8,128)(2,1)S(1)}, bf16[3,128,256]{2,1,0:T(8,128)(2,1)S(1)}, u32[]{:S(2)}, u32[]{:S(2)}) collective-permute-start(bf16[3,128,256]{2,1,0:T(8,128)(2,1)S(1)} %get-tuple-element.46), channel_id=1, source_target_pairs={{0,16},{4,20},{8,24},{12,28},{16,0},{20,4},{24,8},{28,12},{1,17},{... | collective-permute-start | bytes 589832 | tf_op jit(solution)/shard_map/groups/ppermute | solution.py:27
  73.0 8.5 %collective-permute-start.27 = (bf16[3,128,256]{2,1,0:T(8,128)(2,1)S(1)}, bf16[3,128,256]{2,1,0:T(8,128)(2,1)S(1)}, u32[]{:S(2)}, u32[]{:S(2)}) collective-permute-start(bf16[3,128,256]{2,1,0:T(8,128)(2,1)S(1)} %get-tuple-element.47), channel_id=1, source_target_pairs={{0,24},{4,28},{8,16},{12,20},{16,8},{20,12},{24,0},{28,4},{1,25},{... | collective-permute-start | bytes 589832 | tf_op jit(solution)/shard_map/groups/ppermute | solution.py:27
  74.4 8.2 %collective-permute-start.25 = (bf16[3,128,256]{2,1,0:T(8,128)(2,1)S(1)}, bf16[3,128,256]{2,1,0:T(8,128)(2,1)S(1)}, u32[]{:S(2)}, u32[]{:S(2)}) collective-permute-start(bf16[3,128,256]{2,1,0:T(8,128)(2,1)S(1)} %get-tuple-element.45.refs_7_), channel_id=1, source_target_pairs={{0,8},{4,12},{8,0},{12,4},{16,24},{20,28},{24,16},{28,20},{1,9},{5... | collective-permute-start | bytes 589832 | tf_op jit(solution)/shard_map/groups/ppermute | solution.py:27
  85.3 1.8 %collective-permute-start.28 = (bf16[4,2,16,1536]{3,2,1,0:T(8,128)(2,1)S(1)}, bf16[4,2,16,1536]{3,2,1,0:T(8,128)(2,1)S(1)}, u32[]{:S(2)}, u32[]{:S(2)}) collective-permute-start(bf16[4,2,16,1536]{3,2,1,0:T(8,128)(2,1)S(1)} %get-tuple-element.49), channel_id=1, source_target_pairs={{0,4},{4,0},{8,12},{12,8},{16,20},{20,16},{24,28},{28,24},{1,5},{5... | collective-permute-start | bytes 1179656 | tf_op jit(solution)/shard_map/cores/ppermute | solution.py:27
  87.2 4.9 %collective-permute-start.29 = (bf16[2,16,1536]{2,1,0:T(8,128)(2,1)S(1)}, bf16[2,16,1536]{2,1,0:T(8,128)(2,1)S(1)}, u32[]{:S(2)}, u32[]{:S(2)}) collective-permute-start(bf16[2,16,1536]{2,1,0:T(8,128)(2,1)S(1)} %get-tuple-element.51), channel_id=1, source_target_pairs={{0,8},{4,12},{8,0},{12,4},{16,24},{20,28},{24,16},{28,20},{1,9},{5... | collective-permute-start | bytes 294920 | tf_op jit(solution)/shard_map/chips/ppermute | solution.py:27
  88.7 6.7 %collective-permute-start.30 = (bf16[2,16,1536]{2,1,0:T(8,128)(2,1)S(1)}, bf16[2,16,1536]{2,1,0:T(8,128)(2,1)S(1)}, u32[]{:S(2)}, u32[]{:S(2)}) collective-permute-start(bf16[2,16,1536]{2,1,0:T(8,128)(2,1)S(1)} %get-tuple-element.52), channel_id=1, source_target_pairs={{0,16},{4,20},{8,24},{12,28},{16,0},{20,4},{24,8},{28,12},{1,17},{... | collective-permute-start | bytes 294920 | tf_op jit(solution)/shard_map/chips/ppermute | solution.py:27
  89.3 6.1 %collective-permute-start.31 = (bf16[2,16,1536]{2,1,0:T(8,128)(2,1)S(1)}, bf16[2,16,1536]{2,1,0:T(8,128)(2,1)S(1)}, u32[]{:S(2)}, u32[]{:S(2)}) collective-permute-start(bf16[2,16,1536]{2,1,0:T(8,128)(2,1)S(1)} %get-tuple-element.53), channel_id=1, source_target_pairs={{0,24},{4,28},{8,16},{12,20},{16,8},{20,12},{24,0},{28,4},{1,25},{... | collective-permute-start | bytes 294920 | tf_op jit(solution)/shard_map/chips/ppermute | solution.py:27

commit v3 on v2

--- a/solution.py
+++ b/solution.py
@@ -72,19 +72,19 @@
     notes[...] = lax.dot_general(same, table, NT, preferred_element_type=F32).astype(BF16)
 
 
-def load_kernel(place, *refs, ks):
-    weights, (blocks, done, sems) = refs[:2], refs[-3:]
+def load_kernel(place, gate_w, up_w, *refs, ks):
+    blocks, done, sems = refs[-3:]
     rows = blocks.shape[2] // LOADS
     depth = blocks.shape[3]
     copies = []
     for i, k in enumerate(ks):
         columns = pl.ds(pl.multiple_of((place[0] ^ k) * depth, LANES), depth)
-        for w, weight in enumerate(weights):
+        for w, weight in enumerate((gate_w, up_w)):
             for p in range(LOADS):
                 part = pl.ds(p * rows, rows)
                 copies.append(
                     pltpu.make_async_copy(
-                        weight.at[part, columns], blocks.at[w, i, part], sems.at[w, i, p]
+                        weight.at[part, columns], blocks.at[w, k, part], sems.at[w, i, p]
                     )
                 )
     for copy in copies:
@@ -94,6 +94,20 @@
     done[...] = jnp.zeros(done.shape, F32)
 
 
+def load_down_kernel(weight, *refs):
+    held, done, sems = refs[-3:]
+    rows = weight.shape[0] // (4 * LOADS)
+    copies = []
+    for p in range(4 * LOADS):
+        part = pl.ds(p * rows, rows)
+        copies.append(pltpu.make_async_copy(weight.at[part], held.at[part], sems.at[p]))
+    for copy in copies:
+        copy.start()
+    for copy in copies:
+        copy.wait()
+    done[...] = jnp.zeros(done.shape, F32)
+
+
 def product(place, blocks, x, j, w):
     size = blocks.shape[2] // EXPERTS
     depth = blocks.shape[3]
@@ -101,21 +115,14 @@
     total = None
     for i in range(blocks.shape[1]):
         part = lax.dot_general(
-            blocks[w, i, rows], x[:, i * depth:(i + 1) * depth], NT, preferred_element_type=F32
+            blocks[w, i, rows], x[:, LANES + i * depth:LANES + (i + 1) * depth], NT, preferred_element_type=F32
         )
         total = part if total is None else total + part
     return total
 
 
-def project_first_kernel(place, x, blocks, *refs):
-    sums = refs[-1]
-    for j in range(EXPERTS):
-        for w in range(2):
-            sums[j, w] = product(place, blocks, x, j, w)
-
-
 def picks(notes, expert, rows, shard):
-    table = notes[...].astype(F32).T
+    table = notes.astype(F32).T
     slot = jnp.sum(jnp.where(iota(table.shape, 0) == expert, table, 0.0), axis=0, keepdims=True)
     tokens = slot.shape[1]
     first = (iota((1, tokens), 1) // shard) * CAP
@@ -123,12 +130,12 @@
     return one_hot(iota((rows, tokens), 0) == target)
 
 
-def project_sent_kernel(place, x, notes, sums, blocks, slots, *sent, shard):
+def project_sent_kernel(place, x, blocks, slots, *sent, shard):
     size = blocks.shape[2] // EXPERTS
-    pick = picks(notes, place[1], slots.shape[0], shard)
+    pick = picks(x[:, :LANES], place[1], slots.shape[0], shard)
     for j in range(1, EXPERTS):
-        gate = product(place, blocks, x, j, 0) + sums[j, 0]
-        upper = product(place, blocks, x, j, 1) + sums[j, 1]
+        gate = product(place, blocks, x, j, 0)
+        upper = product(place, blocks, x, j, 1)
         sent[j - 1][0] = gate.astype(BF16)
         sent[j - 1][1] = upper.astype(BF16)
         hidden = (silu(gate) * upper).T.astype(BF16)
@@ -137,11 +144,11 @@
         ).astype(BF16)
 
 
-def project_own_kernel(place, x, notes, sums, blocks, others, slots, own, *, shard):
+def project_own_kernel(place, x, blocks, others, slots, own, *, shard):
     size = blocks.shape[2] // EXPERTS
-    pick = picks(notes, place[1], slots.shape[0], shard)
-    gate = product(place, blocks, x, 0, 0) + sums[0, 0]
-    upper = product(place, blocks, x, 0, 1) + sums[0, 1]
+    pick = picks(x[:, :LANES], place[1], slots.shape[0], shard)
+    gate = product(place, blocks, x, 0, 0)
+    upper = product(place, blocks, x, 0, 1)
     own[0] = gate
     own[1] = upper
     hidden = (silu(gate) * upper).T.astype(BF16)
@@ -201,19 +208,10 @@
         store(n, step, total * factor)
 
 
-def first_down_kernel(place, notes, *refs, shard, n_exp, line):
-    weight, *pieces = refs[:-2]
-    out, hidden = refs[-2:]
-    z, expert = place[0], place[1]
+def first_down_kernel(place, notes, weight, *refs, shard, n_exp):
+    pieces, (out, hidden) = refs[:n_exp], refs[-2:]
+    expert = place[1]
     depth = weight.shape[0] // n_exp
-    ks = list(range(n_exp))
-    inner = None
-    if line:
-        inner = jnp.logical_or(z == 1, z == 2)
-        ks = [0, 1, jnp.where(inner, 3, 2), jnp.where(inner, 2, 3)]
-        pieces = [[pieces[0]], [pieces[1]], [pieces[2], pieces[4]], [pieces[3], pieces[5]]]
-    else:
-        pieces = [[piece] for piece in pieces[:n_exp]]
     table = notes[...].astype(F32)
     tokens = table.shape[0]
     lane = iota(table.shape, 1)
@@ -221,19 +219,16 @@
     factor = jnp.sum(jnp.where(lane == EXPERTS + expert, table, 0.0), axis=1, keepdims=True)
     first = (iota((tokens, 1), 0) // shard) * CAP
     target = jnp.where(slot < 0.0, -1, first + slot.astype(jnp.int32))
-    spread = one_hot(iota((tokens, pieces[0][0].shape[0]), 1) == target)
-    for i, found in enumerate(pieces):
-        piece = found[0][...]
-        if len(found) > 1:
-            piece = jnp.where(inner, piece, found[1][...])
-        hidden[:, i * depth:(i + 1) * depth] = jnp.dot(
-            spread, piece, preferred_element_type=F32
+    spread = one_hot(iota((tokens, pieces[0].shape[0]), 1) == target)
+    for k, piece in enumerate(pieces):
+        hidden[:, k * depth:(k + 1) * depth] = jnp.dot(
+            spread, piece[...], preferred_element_type=F32
         ).astype(BF16)
 
     def store(n, step, total):
         out[:, n:n + step] = total
 
-    times_weight(place, weight, hidden, ks, n_exp, factor, store)
+    times_weight(place, weight, hidden, range(n_exp), n_exp, factor, store)
 
 
 def second_down_kernel(place, labels, freq, notes, weight, initial, *refs, flips, n_exp, shard):
@@ -309,6 +304,7 @@
     others = range(1, EXPERTS)
     gate_w = pltpu.with_memory_space_constraint(w_gate, pltpu.HBM)
     up_w = pltpu.with_memory_space_constraint(w_up, pltpu.HBM)
+    down_w = pltpu.with_memory_space_constraint(w_down, pltpu.HBM)
     place = jnp.stack([z, expert]).astype(jnp.int32)
     shape = jax.ShapeDtypeStruct
 
@@ -329,70 +325,51 @@
             name=name,
         )(*args)
 
-    def load(ks, *after):
-        return call(
+    def load(ks, before=None, *after):
+        aliased = [] if before is None else [before]
+        blocks = (2, n_exp, units, depth)
+        return pl.pallas_call(
             functools.partial(load_kernel, ks=ks),
-            "load",
-            [pltpu.VMEM((2, len(ks), units, depth), BF16), shape((8, LANES), F32)],
-            place,
-            gate_w,
-            up_w,
-            *after,
-            scratch=[pltpu.SemaphoreType.DMA((2, len(ks), LOADS))],
-            smem=1,
-            hbm=2,
-            unused=len(after),
-            cost=False,
+            in_specs=[IN_SMEM, IN_HBM, IN_HBM]
+            + [IN_VMEM] * len(aliased)
+            + [ANYWHERE] * len(after),
+            out_specs=[IN_VMEM] * 2,
+            out_shape=[pltpu.VMEM(blocks, BF16), shape((8, LANES), F32)],
+            scratch_shapes=[pltpu.SemaphoreType.DMA((2, len(ks), LOADS))],
+            input_output_aliases={3: 0} if aliased else {},
+            compiler_params=pltpu.CompilerParams(vmem_limit_bytes=limit),
+            name="load",
+        )(place, gate_w, up_w, *aliased, *after)
+
+    weights, done = load(range(half))
+    notes = call(
+        notes_kernel,
+        "notes",
+        shape((shard, LANES), BF16),
+        route_ids.T,
+        gate_codes.T,
+        done,
+        unused=1,
+    )
+    with jax.named_scope("gather_tokens"):
+        row = jnp.concatenate(
+            [notes, tokens] + [swapped(tokens, "exp", k) for k in range(1, n_exp)], axis=1
         )
-
-    near_w, near_done = load(range(half))
-    notes = call(
-        notes_kernel, "notes", shape((shard, LANES), BF16), route_ids.T, gate_codes.T, near_done, unused=1
-    )
-
-    with jax.named_scope("gather_tokens"):
-        rows = [tokens] + [swapped(tokens, "exp", k) for k in range(1, n_exp)]
-        near = jnp.concatenate([notes] + rows[:half], axis=1)
-        far = jnp.concatenate(rows[half:], axis=1)
-
-        def chips(row):
-            return [row] + [swapped(row, "tok", j) for j in range(2, n_tok, 2)]
-
-        def cores(parts):
-            rows = jnp.concatenate(parts, axis=0)
-            return jnp.concatenate([rows, swapped(rows, "tok", 1)], axis=0), rows
-
-        near = chips(near)
-        near[1], far = lax.optimization_barrier((near[1], far))
-        far = chips(far)
-        near, near_rows = cores(near)
-        far_w, far_done = load(range(half, n_exp), near_rows)
-        far, _ = cores(far)
-        table = near[:, :LANES]
-        near = near[:, LANES:]
-
-    sums = call(
-        project_first_kernel,
-        "project_first",
-        shape((EXPERTS, 2, size, all_tokens), F32),
-        place,
-        near,
-        near_w,
-        far_done,
-        smem=1,
-        unused=1,
-        cost=False,
-    )
+        weights, _ = load(range(half, n_exp), weights, row)
+        chips = jnp.concatenate(
+            [row] + [swapped(row, "tok", j) for j in range(2, n_tok, 2)], axis=0
+        )
+        x = jnp.concatenate([chips, swapped(chips, "tok", 1)], axis=0)
+        table = x[:, :LANES]
+
     others_slots, *sent = call(
         functools.partial(project_sent_kernel, shard=shard),
         "project_sent",
         [shape((n_tok * CAP, units - size), BF16)]
         + [shape((2, size, all_tokens), BF16) for _ in others],
         place,
-        far,
-        table,
-        sums,
-        far_w,
+        x,
+        weights,
         smem=1,
         cost=False,
     )
@@ -403,22 +380,15 @@
         "project_own",
         [shape((n_tok * CAP, units), BF16), shape((2, size, all_tokens), F32)],
         place,
-        far,
-        table,
-        sums,
-        far_w,
+        x,
+        weights,
         others_slots,
         smem=1,
         cost=False,
     )
-    line = n_exp == 4
-    middle = ((1, 2), (2, 1))
-    ends = ((1, 0), (2, 3))
+    early = n_exp // 2
     with jax.named_scope("spread_first"):
-        if line:
-            early = [swapped(slots, "exp", 1), lax.ppermute(slots, "exp", middle)]
-        else:
-            early = [swapped(slots, "exp", k) for k in range(1, n_exp)]
+        sooner = swapped(slots, "exp", early)
     merged = call(
         functools.partial(merge_kernel, flips=flips),
         "merge",
@@ -428,18 +398,12 @@
         freq_counts,
         own,
         *peers,
+        sooner,
         smem=3,
+        unused=1,
     )
     with jax.named_scope("spread_second"):
         second = [merged] + [swapped(merged, "exp", k) for k in range(1, n_exp)]
-    with jax.named_scope("spread_first"):
-        first = [slots] + early
-        later = []
-        if line:
-            later = [lax.ppermute(early[0], "exp", middle), lax.ppermute(early[1], "exp", ends)]
-            later[0], second[1] = lax.optimization_barrier((later[0], second[1]))
-            first += later + [lax.ppermute(later[0], "exp", ends)]
-
     def grouped(pieces, *after):
         out = call(
             functools.partial(route_kernel, count=len(pieces)),
@@ -454,15 +418,31 @@
         with jax.named_scope("groups"):
             return out, [swapped(out[j - 1], "tok", j * span) for j in others]
 
-    own_out, groups = grouped(second[:1], second[1])
+    down_v, down_done = call(
+        load_down_kernel,
+        "load_down",
+        [pltpu.VMEM(w_down.shape, BF16), shape((8, LANES), F32)],
+        down_w,
+        second[1],
+        scratch=[pltpu.SemaphoreType.DMA((4 * LOADS,))],
+        hbm=1,
+        unused=1,
+        cost=False,
+    )
+    own_out, groups = grouped(second[:1], down_done)
+    waiting, _ = lax.optimization_barrier((slots, down_done))
+    with jax.named_scope("spread_first"):
+        first = [slots] + [
+            sooner if k == early else swapped(waiting, "exp", k) for k in range(1, n_exp)
+        ]
     far_out, more = grouped(second[1:], *groups)
     initial = call(
-        functools.partial(first_down_kernel, shard=shard, n_exp=n_exp, line=line),
+        functools.partial(first_down_kernel, shard=shard, n_exp=n_exp),
         "first_down",
         shape((all_tokens, width), F32),
         place,
         table,
-        w_down,
+        down_v,
         *first,
         far_out[0],
         scratch=[pltpu.VMEM((all_tokens, n_exp * units), BF16)],
@@ -479,7 +459,7 @@
         merge_labels,
         freq_counts,
         table,
-        w_down,
+        down_v,
         initial,
         *second,
         *groups,

time: 96.3 us -> 91.2 us (0.947)
  starting transfers between devices: 39.4 us -> 34 us
  Pallas kernels: 28.7 us -> 33.2 us
  waiting for transfers between devices: 26.5 us -> 22.6 us
    pallas_call x0 -> x2, Pallas kernels: none -> 11.2 us  [load(): pl.pallas_call(functools.partial(load_kernel, ks=ks), in_specs=[IN_SMEM,...]
    pallas_call x13 -> x11, Pallas kernels: 28.7 us -> 22 us  [call(): pl.pallas_call(kernel, in_specs=specs, out_specs=[IN_VMEM] * len(out_shap...]
    ppermute x4 -> x0, starting transfers between devices: 4.08 us -> none  [the longest x1 1.46 us: local(): first += later + [lax.ppermute(later[0], 'exp', ends)]]
    ppermute x4 -> x0, waiting for transfers between devices: 2.67 us -> none  [the longest x1 2.66 us: local(): first += later + [lax.ppermute(later[0], 'exp', ends)]]
    ppermute x28 -> x26, starting transfers between devices: 35.3 us -> 34 us  [swapped(): return lax.ppermute(value, axis, [(i, i ^ by) for i in range(devices)])]
    ppermute x28 -> x26, waiting for transfers between devices: 23.8 us -> 22.6 us  [swapped(): return lax.ppermute(value, axis, [(i, i ^ by) for i in range(devices)])]
  transfers between devices with their start and end apart: 32 -> 26, of which waited for: 13 -> 14; matrix products, arithmetic and copies ran while one was open for 0% -> 0% of each run, Pallas kernels for 20% -> 22%
where the time goes in v3:
time: 91.2 us; the launch traced here: 91 us
  starting transfers between devices  34 us (37%)
  Pallas kernels  33.2 us (36%)
  waiting for transfers between devices  22.6 us (25%)
    ppermute x26, starting transfers between devices, swapped(): return lax.ppermute(value, axis, [(i, i ^ by) for i in range(devices)])  34 us
    ppermute x26, waiting for transfers between devices, swapped(): return lax.ppermute(value, axis, [(i, i ^ by) for i in range(devices)])  22.6 us
    pallas_call x11, Pallas kernels, call(): pl.pallas_call(kernel, in_specs=specs, out_specs=[IN_VMEM] * len(out_shap...  22 us
    pallas_call x2, Pallas kernels, load(): pl.pallas_call(functools.partial(load_kernel, ks=ks), in_specs=[IN_SMEM,...  11.2 us
  transfers between devices with their start and end apart: 26, of which 14 were waited for; matrix products, arithmetic and copies ran while one was open for 0% of the time, Pallas kernels for 22%

profile of v3, /device:TPU:0, one launch (start us, length us, event | category | flops | bytes accessed | tf_op | source)
XLA Modules:
  0.0 91.0 jit_solution(6538925942160826614)
XLA Ops:
  0.6 4.1 %collective-permute-start.1 = (bf16[16,1536]{1,0:T(8,128)(2,1)}, bf16[16,1536]{1,0:T(8,128)(2,1)S(1)}, u32[]{:S(2)}, u32[]{:S(2)}) collective-permute-start(bf16[16,1536]{1,0:T(8,128)(2,1)} %param.8), channel_id=1, source_target_pairs={{0,2},{1,3},{2,0},{3,1},{4,6},{5,7},{6,4},{7,5},{8,10},{9,11},{10,... | collective-permute-start | bytes 147464 | tf_op jit(solution)/shard_map/gather_tokens/ppermute | solution.py:27
  4.7 1.6 %collective-permute-start = (bf16[16,1536]{1,0:T(8,128)(2,1)}, bf16[16,1536]{1,0:T(8,128)(2,1)S(1)}, u32[]{:S(2)}, u32[]{:S(2)}) collective-permute-start(bf16[16,1536]{1,0:T(8,128)(2,1)} %param.8), channel_id=1, source_target_pairs={{0,1},{1,0},{2,3},{3,2},{4,5},{5,4},{6,7},{7,6},{8,9},{9,8},{10,11... | collective-permute-start | bytes 147464 | tf_op jit(solution)/shard_map/gather_tokens/ppermute | solution.py:27
  6.3 0.1 pad_add_fusion.place
  6.4 5.3 %load.2 = (bf16[2,4,1024,1536]{3,2,1,0:T(8,128)(2,1)S(1)}, f32[8,128]{1,0:T(8,128)S(1)}) custom-call(s32[2]{0:T(128)S(1)} %pad_add_fusion.place, bf16[1024,6144]{1,0:T(8,128)(2,1)} %gate_w.3, bf16[1024,6144]{1,0:T(8,128)(2,1)} %up_w.3), custom_call_target="tpu_custom_call" | custom-call | tf_op jit(solution)/shard_map/load/pallas_call | solution.py:331
  11.7 0.2 notes.1
  12.0 0.0 collective-permute-done.1
  12.1 0.3 collective-permute-done.2
  12.4 2.5 %collective-permute-start.5 = (bf16[16,6272]{1,0:T(8,128)(2,1)S(1)}, bf16[16,6272]{1,0:T(8,128)(2,1)S(1)}, u32[]{:S(2)}, u32[]{:S(2)}) collective-permute-start(bf16[16,6272]{1,0:T(8,128)(2,1)S(1)} %get-tuple-element.50.refs_1_), channel_id=1, source_target_pairs={{0,24},{4,28},{8,16},{12,20},{16,8},{20,12},{24,0},{28,4},{1,25},{... | collective-permute-start | bytes 602120 | tf_op jit(solution)/shard_map/gather_tokens/ppermute | solution.py:27
  14.9 0.5 collective-permute-start.4
  15.4 0.5 collective-permute-start.3
  16.0 5.9 %load.3 = (bf16[2,4,1024,1536]{3,2,1,0:T(8,128)(2,1)S(1)}, f32[8,128]{1,0:T(8,128)}) custom-call(s32[2]{0:T(128)S(1)} %pad_add_fusion.place, bf16[1024,6144]{1,0:T(8,128)(2,1)} %gate_w.3, bf16[1024,6144]{1,0:T(8,128)(2,1)} %up_w.3, bf16[2,4,1024,1536]{3,2,1,0:T(8,128)(2,1)S(1)} %get-tuple-element.27.refs_0_, ...), custom_call_target="tpu_custom_call", output_to_operand_aliasing={{0}: (3, {})} | custom-call | tf_op jit(solution)/shard_map/gather_tokens/load/pallas_call | solution.py:331
  21.9 1.6 %collective-permute-done.4 = bf16[16,6272]{1,0:T(8,128)(2,1)S(1)} collective-permute-done((bf16[16,6272]{1,0:T(8,128)(2,1)S(1)}, bf16[16,6272]{1,0:T(8,128)(2,1)S(1)}, u32[]{:S(2)}, u32[]{:S(2)}) %collective-permute-start.4) | collective-permute-done | bytes 200736 | tf_op jit(solution)/shard_map/gather_tokens/ppermute | solution.py:27
  23.5 0.1 collective-permute-done.3
  23.6 0.1 pad_maximum_fusion
  23.7 0.1 collective-permute-start.6
  23.8 2.2 %collective-permute-done.6 = bf16[64,6272]{1,0:T(8,128)(2,1)S(1)} collective-permute-done((bf16[64,6272]{1,0:T(8,128)(2,1)S(1)}, bf16[64,6272]{1,0:T(8,128)(2,1)S(1)}, u32[]{:S(2)}, u32[]{:S(2)}) %collective-permute-start.6) | collective-permute-done | bytes 802848 | tf_op jit(solution)/shard_map/gather_tokens/ppermute | solution.py:27
  26.1 0.1 constant_dynamic-update-slice_fusion.5.x
  26.2 6.2 %project_sent.1 = (bf16[96,768]{1,0:T(8,128)(2,1)S(1)}, bf16[2,256,128]{2,1,0:T(8,128)(2,1)S(1)}, bf16[2,256,128]{2,1,0:T(8,128)(2,1)S(1)}, bf16[2,256,128]{2,1,0:T(8,128)(2,1)S(1)}) custom-call(s32[2]{0:T(128)S(1)} %pad_add_fusion.place, bf16[128,6272]{1,0:T(8,128)(2,1)S(1)} %constant_dynamic-update-slice_fusion.5.x, ...), custom_call_target="tpu_custom_call" | custom-call | tf_op jit(solution)/shard_map/project_sent/pallas_call | solution.py:317
  32.4 0.0 copy-start
  32.4 0.0 copy-start.1
  32.4 2.5 %project_own.1 = (bf16[96,1024]{1,0:T(8,128)(2,1)S(1)}, f32[2,256,128]{2,1,0:T(8,128)S(1)}) custom-call(s32[2]{0:T(128)S(1)} %pad_add_fusion.place, bf16[128,6272]{1,0:T(8,128)(2,1)S(1)} %constant_dynamic-update-slice_fusion.5.x, bf16[2,4,1024,1536]{3,2,1,0:T(8,128)(2,1)S(1)} %get-tuple-element.28.blocks, bf16[96,768]{1,0:T(8,128)(2,1)S(1)} %get-tuple-element.29.others), custom_call_target="tpu_custom_call" | custom-call | tf_op jit(solution)/shard_map/project_own/pallas_call | solution.py:317
  35.0 1.7 %collective-permute-start.10 = (bf16[96,1024]{1,0:T(8,128)(2,1)S(1)}, bf16[96,1024]{1,0:T(8,128)(2,1)S(1)}, u32[]{:S(2)}, u32[]{:S(2)}) collective-permute-start(bf16[96,1024]{1,0:T(8,128)(2,1)S(1)} %get-tuple-element.37.refs_0_), channel_id=1, source_target_pairs={{0,2},{1,3},{2,0},{3,1},{4,6},{5,7},{6,4},{7,5},{8,10},{9,11},{10,... | collective-permute-start | bytes 589832 | tf_op jit(solution)/shard_map/spread_first/ppermute | solution.py:27
  36.7 1.5 %collective-permute-start.7 = (bf16[2,256,128]{2,1,0:T(8,128)(2,1)S(1)}, bf16[2,256,128]{2,1,0:T(8,128)(2,1)S(1)}, u32[]{:S(2)}, u32[]{:S(2)}) collective-permute-start(bf16[2,256,128]{2,1,0:T(8,128)(2,1)S(1)} %get-tuple-element.31), channel_id=1, source_target_pairs={{0,8},{4,12},{8,0},{12,4},{16,24},{20,28},{24,16},{28,20},{1,9},{5... | collective-permute-start | bytes 393224 | tf_op jit(solution)/shard_map/peers/ppermute | solution.py:27
  38.2 0.7 collective-permute-start.8
  38.9 1.3 %collective-permute-start.9 = (bf16[2,256,128]{2,1,0:T(8,128)(2,1)S(1)}, bf16[2,256,128]{2,1,0:T(8,128)(2,1)S(1)}, u32[]{:S(2)}, u32[]{:S(2)}) collective-permute-start(bf16[2,256,128]{2,1,0:T(8,128)(2,1)S(1)} %get-tuple-element.33), channel_id=1, source_target_pairs={{0,24},{4,28},{8,16},{12,20},{16,8},{20,12},{24,0},{28,4},{1,25},{... | collective-permute-start | bytes 393224 | tf_op jit(solution)/shard_map/peers/ppermute | solution.py:27
  40.1 2.1 %collective-permute-done.7.refs_0_ = bf16[2,256,128]{2,1,0:T(8,128)(2,1)S(1)} collective-permute-done((bf16[2,256,128]{2,1,0:T(8,128)(2,1)S(1)}, bf16[2,256,128]{2,1,0:T(8,128)(2,1)S(1)}, u32[]{:S(2)}, u32[]{:S(2)}) %collective-permute-start.7) | collective-permute-done | bytes 131104 | tf_op jit(solution)/shard_map/peers/ppermute | solution.py:27
  42.3 3.6 %collective-permute-done.8.refs_1_ = bf16[2,256,128]{2,1,0:T(8,128)(2,1)S(1)} collective-permute-done((bf16[2,256,128]{2,1,0:T(8,128)(2,1)S(1)}, bf16[2,256,128]{2,1,0:T(8,128)(2,1)S(1)}, u32[]{:S(2)}, u32[]{:S(2)}) %collective-permute-start.8) | collective-permute-done | bytes 131104 | tf_op jit(solution)/shard_map/peers/ppermute | solution.py:27
  45.9 0.0 collective-permute-done.9.refs_2_
  45.9 1.1 %collective-permute-done.10.refs_3_.refs_2_ = bf16[96,1024]{1,0:T(8,128)(2,1)S(1)} collective-permute-done((bf16[96,1024]{1,0:T(8,128)(2,1)S(1)}, bf16[96,1024]{1,0:T(8,128)(2,1)S(1)}, u32[]{:S(2)}, u32[]{:S(2)}) %collective-permute-start.10) | collective-permute-done | bytes 196640 | tf_op jit(solution)/shard_map/spread_first/ppermute | solution.py:27
  47.1 1.0 %merge.1.refs_0_ = bf16[2,128,256]{2,1,0:T(8,128)(2,1)S(1)} custom-call(s32[2]{0:T(128)S(1)} %pad_add_fusion.place, s32[4]{0:T(128)S(1)} %copy-done, s32[4]{0:T(128)S(1)} %copy-done.1, f32[2,256,128]{2,1,0:T(8,128)S(1)} %get-tuple-element.30.own, bf16[2,256,128]{2,1,0:T(8,128)(2,1)S(1)} %collective-permute-done.7.refs_0_, ...), custom_call_target="tpu_custom_call" | custom-call | flops 1 | bytes 1 | tf_op jit(solution)/shard_map/merge/pallas_call | solution.py:317
  48.1 1.4 %collective-permute-start.11 = (bf16[2,128,256]{2,1,0:T(8,128)(2,1)S(1)}, bf16[2,128,256]{2,1,0:T(8,128)(2,1)S(1)}, u32[]{:S(2)}, u32[]{:S(2)}) collective-permute-start(bf16[2,128,256]{2,1,0:T(8,128)(2,1)S(1)} %merge.1.refs_0_), channel_id=1, source_target_pairs={{0,1},{1,0},{2,3},{3,2},{4,5},{5,4},{6,7},{7,6},{8,9},{9,8},{10,11... | collective-permute-start | bytes 393224 | tf_op jit(solution)/shard_map/spread_second/ppermute | solution.py:27
  49.5 1.3 %collective-permute-start.15 = (bf16[2,128,256]{2,1,0:T(8,128)(2,1)S(1)}, bf16[2,128,256]{2,1,0:T(8,128)(2,1)S(1)}, u32[]{:S(2)}, u32[]{:S(2)}) collective-permute-start(bf16[2,128,256]{2,1,0:T(8,128)(2,1)S(1)} %merge.1.refs_0_), channel_id=1, source_target_pairs={{0,3},{1,2},{2,1},{3,0},{4,7},{5,6},{6,5},{7,4},{8,11},{9,10},{10,... | collective-permute-start | bytes 393224 | tf_op jit(solution)/shard_map/spread_second/ppermute | solution.py:27
  50.7 0.9 collective-permute-start.14
  51.6 1.5 %collective-permute-done.11.refs_0_.refs_1_ = bf16[2,128,256]{2,1,0:T(8,128)(2,1)S(1)} collective-permute-done((bf16[2,128,256]{2,1,0:T(8,128)(2,1)S(1)}, bf16[2,128,256]{2,1,0:T(8,128)(2,1)S(1)}, u32[]{:S(2)}, u32[]{:S(2)}) %collective-permute-start.11) | collective-permute-done | bytes 131104 | tf_op jit(solution)/shard_map/spread_second/ppermute | solution.py:27
  53.1 4.7 %load_down.1 = (bf16[4096,1536]{1,0:T(8,128)(2,1)S(1)}, f32[8,128]{1,0:T(8,128)S(1)}) custom-call(bf16[4096,1536]{1,0:T(8,128)(2,1)} %weight.1, bf16[2,128,256]{2,1,0:T(8,128)(2,1)S(1)} %collective-permute-done.11.refs_0_.refs_1_), custom_call_target="tpu_custom_call" | custom-call | tf_op jit(solution)/shard_map/load_down/pallas_call | solution.py:317
  57.8 0.6 route.2
  58.4 1.6 %collective-permute-start.16 = (bf16[1,128,256]{2,1,0:T(8,128)(2,1)S(1)}, bf16[1,128,256]{2,1,0:T(8,128)(2,1)S(1)}, u32[]{:S(2)}, u32[]{:S(2)}) collective-permute-start(bf16[1,128,256]{2,1,0:T(8,128)(2,1)S(1)} %get-tuple-element.38), channel_id=1, source_target_pairs={{0,8},{4,12},{8,0},{12,4},{16,24},{20,28},{24,16},{28,20},{1,9},{5... | collective-permute-start | bytes 196616 | tf_op jit(solution)/shard_map/groups/ppermute | solution.py:27
  60.0 0.7 collective-permute-start.17
  60.7 1.3 %collective-permute-start.18 = (bf16[1,128,256]{2,1,0:T(8,128)(2,1)S(1)}, bf16[1,128,256]{2,1,0:T(8,128)(2,1)S(1)}, u32[]{:S(2)}, u32[]{:S(2)}) collective-permute-start(bf16[1,128,256]{2,1,0:T(8,128)(2,1)S(1)} %get-tuple-element.40), channel_id=1, source_target_pairs={{0,24},{4,28},{8,16},{12,20},{16,8},{20,12},{24,0},{28,4},{1,25},{... | collective-permute-start | bytes 196616 | tf_op jit(solution)/shard_map/groups/ppermute | solution.py:27
  62.0 0.0 collective-permute-done.15.refs_2_.refs_3_
  62.0 5.3 %collective-permute-start.13 = (bf16[96,1024]{1,0:T(8,128)(2,1)S(1)}, bf16[96,1024]{1,0:T(8,128)(2,1)S(1)}, u32[]{:S(2)}, u32[]{:S(2)}) collective-permute-start(bf16[96,1024]{1,0:T(8,128)(2,1)S(1)} %get-tuple-element.37.refs_0_), channel_id=1, source_target_pairs={{0,3},{1,2},{2,1},{3,0},{4,7},{5,6},{6,5},{7,4},{8,11},{9,10},{10,... | collective-permute-start | bytes 589832 | tf_op jit(solution)/shard_map/spread_first/ppermute | solution.py:27
  67.2 0.0 collective-permute-done.14.refs_1_.refs_2_
  67.2 0.0 collective-permute-start.12
  67.2 0.0 collective-permute-done.16.refs_3_.refs_4_
  67.3 0.6 route.3
  67.9 2.0 %collective-permute-start.20 = (bf16[3,128,256]{2,1,0:T(8,128)(2,1)S(1)}, bf16[3,128,256]{2,1,0:T(8,128)(2,1)S(1)}, u32[]{:S(2)}, u32[]{:S(2)}) collective-permute-start(bf16[3,128,256]{2,1,0:T(8,128)(2,1)S(1)} %get-tuple-element.42), channel_id=1, source_target_pairs={{0,16},{4,20},{8,24},{12,28},{16,0},{20,4},{24,8},{28,12},{1,17},{... | collective-permute-start | bytes 589832 | tf_op jit(solution)/shard_map/groups/ppermute | solution.py:27
  69.8 1.5 %collective-permute-start.21 = (bf16[3,128,256]{2,1,0:T(8,128)(2,1)S(1)}, bf16[3,128,256]{2,1,0:T(8,128)(2,1)S(1)}, u32[]{:S(2)}, u32[]{:S(2)}) collective-permute-start(bf16[3,128,256]{2,1,0:T(8,128)(2,1)S(1)} %get-tuple-element.43), channel_id=1, source_target_pairs={{0,24},{4,28},{8,16},{12,20},{16,8},{20,12},{24,0},{28,4},{1,25},{... | collective-permute-start | bytes 589832 | tf_op jit(solution)/shard_map/groups/ppermute | solution.py:27
  71.3 0.1 collective-permute-start.19
  71.4 0.0 collective-permute-done.13.refs_3_
  71.4 1.7 %collective-permute-done.12.refs_1_ = bf16[96,1024]{1,0:T(8,128)(2,1)S(1)} collective-permute-done((bf16[96,1024]{1,0:T(8,128)(2,1)S(1)}, bf16[96,1024]{1,0:T(8,128)(2,1)S(1)}, u32[]{:S(2)}, u32[]{:S(2)}) %collective-permute-start.12) | collective-permute-done | bytes 196640 | tf_op jit(solution)/shard_map/spread_first/ppermute | solution.py:27
  73.1 2.7 %first_down.1.initial = f32[128,1536]{1,0:T(8,128)S(1)} custom-call(s32[2]{0:T(128)S(1)} %pad_add_fusion.place, bf16[128,128]{1,0:T(8,128)(2,1)S(1)} %slice.4.notes, bf16[4096,1536]{1,0:T(8,128)(2,1)S(1)} %get-tuple-element.35.weight, bf16[96,1024]{1,0:T(8,128)(2,1)S(1)} %get-tuple-element.37.refs_0_, bf16[96,1024]{1,0:T(8,128)(2,1)S(1)} %collective-permute-done.12.refs_1_, ...), custom_call_target="tpu_custom_call" | custom-call | tf_op jit(solution)/shard_map/first_down/pallas_call | solution.py:317
  75.8 0.0 collective-permute-done.20.refs_8_
  75.8 0.5 collective-permute-done.21.refs_9_
  76.4 0.8 collective-permute-done.19.refs_7_
  77.2 2.6 %second_down.1 = (f32[4,2,16,1536]{3,2,1,0:T(8,128)S(1)}, bf16[4,2,16,1536]{3,2,1,0:T(8,128)(2,1)S(1)}) custom-call(s32[2]{0:T(128)S(1)} %pad_add_fusion.place, s32[4]{0:T(128)S(1)} %copy-done, s32[4]{0:T(128)S(1)} %copy-done.1, bf16[128,128]{1,0:T(8,128)(2,1)S(1)} %slice.4.notes, bf16[4096,1536]{1,0:T(8,128)(2,1)S(1)} %get-tuple-element.35.weight, ...), custom_call_target="tpu_custom_call" | custom-call | tf_op jit(solution)/shard_map/second_down/pallas_call | solution.py:317
  79.8 0.1 collective-permute-start.22
  79.9 1.7 %collective-permute-done.22.theirs = bf16[4,2,16,1536]{3,2,1,0:T(8,128)(2,1)S(1)} collective-permute-done((bf16[4,2,16,1536]{3,2,1,0:T(8,128)(2,1)S(1)}, bf16[4,2,16,1536]{3,2,1,0:T(8,128)(2,1)S(1)}, u32[]{:S(2)}, u32[]{:S(2)}) %collective-permute-start.22) | collective-permute-done | bytes 393248 | tf_op jit(solution)/shard_map/cores/ppermute | solution.py:27
  81.6 0.1 cores.1
  81.7 2.0 %collective-permute-start.23 = (bf16[2,16,1536]{2,1,0:T(8,128)(2,1)S(1)}, bf16[2,16,1536]{2,1,0:T(8,128)(2,1)S(1)}, u32[]{:S(2)}, u32[]{:S(2)}) collective-permute-start(bf16[2,16,1536]{2,1,0:T(8,128)(2,1)S(1)} %get-tuple-element.47), channel_id=1, source_target_pairs={{0,8},{4,12},{8,0},{12,4},{16,24},{20,28},{24,16},{28,20},{1,9},{5... | collective-permute-start | bytes 294920 | tf_op jit(solution)/shard_map/chips/ppermute | solution.py:27
  83.7 0.1 collective-permute-start.24
  83.8 1.5 %collective-permute-start.25 = (bf16[2,16,1536]{2,1,0:T(8,128)(2,1)S(1)}, bf16[2,16,1536]{2,1,0:T(8,128)(2,1)S(1)}, u32[]{:S(2)}, u32[]{:S(2)}) collective-permute-start(bf16[2,16,1536]{2,1,0:T(8,128)(2,1)S(1)} %get-tuple-element.49), channel_id=1, source_target_pairs={{0,24},{4,28},{8,16},{12,20},{16,8},{20,12},{24,0},{28,4},{1,25},{... | collective-permute-start | bytes 294920 | tf_op jit(solution)/shard_map/chips/ppermute | solution.py:27
  85.3 1.6 %collective-permute-done.23.refs_0_ = bf16[2,16,1536]{2,1,0:T(8,128)(2,1)S(1)} collective-permute-done((bf16[2,16,1536]{2,1,0:T(8,128)(2,1)S(1)}, bf16[2,16,1536]{2,1,0:T(8,128)(2,1)S(1)}, u32[]{:S(2)}, u32[]{:S(2)}) %collective-permute-start.23) | collective-permute-done | bytes 98336 | tf_op jit(solution)/shard_map/chips/ppermute | solution.py:27
  86.8 3.5 %collective-permute-done.24.refs_1_ = bf16[2,16,1536]{2,1,0:T(8,128)(2,1)S(1)} collective-permute-done((bf16[2,16,1536]{2,1,0:T(8,128)(2,1)S(1)}, bf16[2,16,1536]{2,1,0:T(8,128)(2,1)S(1)}, u32[]{:S(2)}, u32[]{:S(2)}) %collective-permute-start.24) | collective-permute-done | bytes 98336 | tf_op jit(solution)/shard_map/chips/ppermute | solution.py:27
  90.3 0.7 finish.1
  (23 shorter events, 0.2 us)
Async XLA Ops:
  0.6 11.4 %collective-permute-start.1 = (bf16[16,1536]{1,0:T(8,128)(2,1)}, bf16[16,1536]{1,0:T(8,128)(2,1)S(1)}, u32[]{:S(2)}, u32[]{:S(2)}) collective-permute-start(bf16[16,1536]{1,0:T(8,128)(2,1)} %param.8), channel_id=1, source_target_pairs={{0,2},{1,3},{2,0},{3,1},{4,6},{5,7},{6,4},{7,5},{8,10},{9,11},{10,... | collective-permute-start | bytes 147464 | tf_op jit(solution)/shard_map/gather_tokens/ppermute | solution.py:27
  4.7 7.3 %collective-permute-start = (bf16[16,1536]{1,0:T(8,128)(2,1)}, bf16[16,1536]{1,0:T(8,128)(2,1)S(1)}, u32[]{:S(2)}, u32[]{:S(2)}) collective-permute-start(bf16[16,1536]{1,0:T(8,128)(2,1)} %param.8), channel_id=1, source_target_pairs={{0,1},{1,0},{2,3},{3,2},{4,5},{5,4},{6,7},{7,6},{8,9},{9,8},{10,11... | collective-permute-start | bytes 147464 | tf_op jit(solution)/shard_map/gather_tokens/ppermute | solution.py:27
  6.3 6.1 %collective-permute-start.2 = (bf16[16,1536]{1,0:T(8,128)(2,1)}, bf16[16,1536]{1,0:T(8,128)(2,1)S(1)}, u32[]{:S(2)}, u32[]{:S(2)}) collective-permute-start(bf16[16,1536]{1,0:T(8,128)(2,1)} %param.8), channel_id=1, source_target_pairs={{0,3},{1,2},{2,1},{3,0},{4,7},{5,6},{6,5},{7,4},{8,11},{9,10},{10,... | collective-permute-start | bytes 147464 | tf_op jit(solution)/shard_map/gather_tokens/ppermute | solution.py:27
  6.4 5.3 %copy-start.2 = (s32[16,2]{0,1:T(2,128)S(1)}, s32[16,2]{0,1:T(2,128)}, u32[]{:S(2)}) copy-start(s32[16,2]{0,1:T(2,128)} %param.9) | copy-start | bytes 388
  6.4 5.3 %copy-start.3 = (s32[16,2]{0,1:T(2,128)S(1)}, s32[16,2]{0,1:T(2,128)}, u32[]{:S(2)}) copy-start(s32[16,2]{0,1:T(2,128)} %param.10) | copy-start | bytes 388
  6.4 5.6 %copy-start.4 = (bf16[16,1536]{1,0:T(8,128)(2,1)S(1)}, bf16[16,1536]{1,0:T(8,128)(2,1)}, u32[]{:S(2)}) copy-start(bf16[16,1536]{1,0:T(8,128)(2,1)} %param.8) | copy-start | bytes 147460
  12.4 9.5 %collective-permute-start.5 = (bf16[16,6272]{1,0:T(8,128)(2,1)S(1)}, bf16[16,6272]{1,0:T(8,128)(2,1)S(1)}, u32[]{:S(2)}, u32[]{:S(2)}) collective-permute-start(bf16[16,6272]{1,0:T(8,128)(2,1)S(1)} %get-tuple-element.50.refs_1_), channel_id=1, source_target_pairs={{0,24},{4,28},{8,16},{12,20},{16,8},{20,12},{24,0},{28,4},{1,25},{... | collective-permute-start | bytes 602120 | tf_op jit(solution)/shard_map/gather_tokens/ppermute | solution.py:27
  14.9 8.6 %collective-permute-start.4 = (bf16[16,6272]{1,0:T(8,128)(2,1)S(1)}, bf16[16,6272]{1,0:T(8,128)(2,1)S(1)}, u32[]{:S(2)}, u32[]{:S(2)}) collective-permute-start(bf16[16,6272]{1,0:T(8,128)(2,1)S(1)} %get-tuple-element.50.refs_1_), channel_id=1, source_target_pairs={{0,16},{4,20},{8,24},{12,28},{16,0},{20,4},{24,8},{28,12},{1,17},{... | collective-permute-start | bytes 602120 | tf_op jit(solution)/shard_map/gather_tokens/ppermute | solution.py:27
  15.4 8.2 %collective-permute-start.3 = (bf16[16,6272]{1,0:T(8,128)(2,1)S(1)}, bf16[16,6272]{1,0:T(8,128)(2,1)S(1)}, u32[]{:S(2)}, u32[]{:S(2)}) collective-permute-start(bf16[16,6272]{1,0:T(8,128)(2,1)S(1)} %get-tuple-element.50.refs_1_), channel_id=1, source_target_pairs={{0,8},{4,12},{8,0},{12,4},{16,24},{20,28},{24,16},{28,20},{1,9},{5... | collective-permute-start | bytes 602120 | tf_op jit(solution)/shard_map/gather_tokens/ppermute | solution.py:27
  23.7 2.4 %collective-permute-start.6 = (bf16[64,6272]{1,0:T(8,128)(2,1)S(1)}, bf16[64,6272]{1,0:T(8,128)(2,1)S(1)}, u32[]{:S(2)}, u32[]{:S(2)}) collective-permute-start(bf16[64,6272]{1,0:T(8,128)(2,1)S(1)} %pad_maximum_fusion), channel_id=1, source_target_pairs={{0,4},{4,0},{8,12},{12,8},{16,20},{20,16},{24,28},{28,24},{1,5},{5... | collective-permute-start | bytes 2408456 | tf_op jit(solution)/shard_map/gather_tokens/ppermute | solution.py:27
  32.4 14.7 %copy-start = (s32[4]{0:T(128)S(1)}, s32[4]{0:T(128)}, u32[]{:S(2)}) copy-start(s32[4]{0:T(128)} %labels.7) | copy-start | bytes 52
  32.4 14.7 %copy-start.1 = (s32[4]{0:T(128)S(1)}, s32[4]{0:T(128)}, u32[]{:S(2)}) copy-start(s32[4]{0:T(128)} %freq.3) | copy-start | bytes 52
  35.0 12.1 %collective-permute-start.10 = (bf16[96,1024]{1,0:T(8,128)(2,1)S(1)}, bf16[96,1024]{1,0:T(8,128)(2,1)S(1)}, u32[]{:S(2)}, u32[]{:S(2)}) collective-permute-start(bf16[96,1024]{1,0:T(8,128)(2,1)S(1)} %get-tuple-element.37.refs_0_), channel_id=1, source_target_pairs={{0,2},{1,3},{2,0},{3,1},{4,6},{5,7},{6,4},{7,5},{8,10},{9,11},{10,... | collective-permute-start | bytes 589832 | tf_op jit(solution)/shard_map/spread_first/ppermute | solution.py:27
  36.7 5.6 %collective-permute-start.7 = (bf16[2,256,128]{2,1,0:T(8,128)(2,1)S(1)}, bf16[2,256,128]{2,1,0:T(8,128)(2,1)S(1)}, u32[]{:S(2)}, u32[]{:S(2)}) collective-permute-start(bf16[2,256,128]{2,1,0:T(8,128)(2,1)S(1)} %get-tuple-element.31), channel_id=1, source_target_pairs={{0,8},{4,12},{8,0},{12,4},{16,24},{20,28},{24,16},{28,20},{1,9},{5... | collective-permute-start | bytes 393224 | tf_op jit(solution)/shard_map/peers/ppermute | solution.py:27
  38.2 7.8 %collective-permute-start.8 = (bf16[2,256,128]{2,1,0:T(8,128)(2,1)S(1)}, bf16[2,256,128]{2,1,0:T(8,128)(2,1)S(1)}, u32[]{:S(2)}, u32[]{:S(2)}) collective-permute-start(bf16[2,256,128]{2,1,0:T(8,128)(2,1)S(1)} %get-tuple-element.32), channel_id=1, source_target_pairs={{0,16},{4,20},{8,24},{12,28},{16,0},{20,4},{24,8},{28,12},{1,17},{... | collective-permute-start | bytes 393224 | tf_op jit(solution)/shard_map/peers/ppermute | solution.py:27
  38.9 7.1 %collective-permute-start.9 = (bf16[2,256,128]{2,1,0:T(8,128)(2,1)S(1)}, bf16[2,256,128]{2,1,0:T(8,128)(2,1)S(1)}, u32[]{:S(2)}, u32[]{:S(2)}) collective-permute-start(bf16[2,256,128]{2,1,0:T(8,128)(2,1)S(1)} %get-tuple-element.33), channel_id=1, source_target_pairs={{0,24},{4,28},{8,16},{12,20},{16,8},{20,12},{24,0},{28,4},{1,25},{... | collective-permute-start | bytes 393224 | tf_op jit(solution)/shard_map/peers/ppermute | solution.py:27
  48.1 5.0 %collective-permute-start.11 = (bf16[2,128,256]{2,1,0:T(8,128)(2,1)S(1)}, bf16[2,128,256]{2,1,0:T(8,128)(2,1)S(1)}, u32[]{:S(2)}, u32[]{:S(2)}) collective-permute-start(bf16[2,128,256]{2,1,0:T(8,128)(2,1)S(1)} %merge.1.refs_0_), channel_id=1, source_target_pairs={{0,1},{1,0},{2,3},{3,2},{4,5},{5,4},{6,7},{7,6},{8,9},{9,8},{10,11... | collective-permute-start | bytes 393224 | tf_op jit(solution)/shard_map/spread_second/ppermute | solution.py:27
  49.5 12.5 %collective-permute-start.15 = (bf16[2,128,256]{2,1,0:T(8,128)(2,1)S(1)}, bf16[2,128,256]{2,1,0:T(8,128)(2,1)S(1)}, u32[]{:S(2)}, u32[]{:S(2)}) collective-permute-start(bf16[2,128,256]{2,1,0:T(8,128)(2,1)S(1)} %merge.1.refs_0_), channel_id=1, source_target_pairs={{0,3},{1,2},{2,1},{3,0},{4,7},{5,6},{6,5},{7,4},{8,11},{9,10},{10,... | collective-permute-start | bytes 393224 | tf_op jit(solution)/shard_map/spread_second/ppermute | solution.py:27
  50.7 16.5 %collective-permute-start.14 = (bf16[2,128,256]{2,1,0:T(8,128)(2,1)S(1)}, bf16[2,128,256]{2,1,0:T(8,128)(2,1)S(1)}, u32[]{:S(2)}, u32[]{:S(2)}) collective-permute-start(bf16[2,128,256]{2,1,0:T(8,128)(2,1)S(1)} %merge.1.refs_0_), channel_id=1, source_target_pairs={{0,2},{1,3},{2,0},{3,1},{4,6},{5,7},{6,4},{7,5},{8,10},{9,11},{10,... | collective-permute-start | bytes 393224 | tf_op jit(solution)/shard_map/spread_second/ppermute | solution.py:27
  58.4 8.8 %collective-permute-start.16 = (bf16[1,128,256]{2,1,0:T(8,128)(2,1)S(1)}, bf16[1,128,256]{2,1,0:T(8,128)(2,1)S(1)}, u32[]{:S(2)}, u32[]{:S(2)}) collective-permute-start(bf16[1,128,256]{2,1,0:T(8,128)(2,1)S(1)} %get-tuple-element.38), channel_id=1, source_target_pairs={{0,8},{4,12},{8,0},{12,4},{16,24},{20,28},{24,16},{28,20},{1,9},{5... | collective-permute-start | bytes 196616 | tf_op jit(solution)/shard_map/groups/ppermute | solution.py:27
  60.0 7.3 %collective-permute-start.17 = (bf16[1,128,256]{2,1,0:T(8,128)(2,1)S(1)}, bf16[1,128,256]{2,1,0:T(8,128)(2,1)S(1)}, u32[]{:S(2)}, u32[]{:S(2)}) collective-permute-start(bf16[1,128,256]{2,1,0:T(8,128)(2,1)S(1)} %get-tuple-element.39), channel_id=1, source_target_pairs={{0,16},{4,20},{8,24},{12,28},{16,0},{20,4},{24,8},{28,12},{1,17},{... | collective-permute-start | bytes 196616 | tf_op jit(solution)/shard_map/groups/ppermute | solution.py:27
  60.7 6.6 %collective-permute-start.18 = (bf16[1,128,256]{2,1,0:T(8,128)(2,1)S(1)}, bf16[1,128,256]{2,1,0:T(8,128)(2,1)S(1)}, u32[]{:S(2)}, u32[]{:S(2)}) collective-permute-start(bf16[1,128,256]{2,1,0:T(8,128)(2,1)S(1)} %get-tuple-element.40), channel_id=1, source_target_pairs={{0,24},{4,28},{8,16},{12,20},{16,8},{20,12},{24,0},{28,4},{1,25},{... | collective-permute-start | bytes 196616 | tf_op jit(solution)/shard_map/groups/ppermute | solution.py:27
  62.0 9.5 %collective-permute-start.13 = (bf16[96,1024]{1,0:T(8,128)(2,1)S(1)}, bf16[96,1024]{1,0:T(8,128)(2,1)S(1)}, u32[]{:S(2)}, u32[]{:S(2)}) collective-permute-start(bf16[96,1024]{1,0:T(8,128)(2,1)S(1)} %get-tuple-element.37.refs_0_), channel_id=1, source_target_pairs={{0,3},{1,2},{2,1},{3,0},{4,7},{5,6},{6,5},{7,4},{8,11},{9,10},{10,... | collective-permute-start | bytes 589832 | tf_op jit(solution)/shard_map/spread_first/ppermute | solution.py:27
  67.2 5.9 %collective-permute-start.12 = (bf16[96,1024]{1,0:T(8,128)(2,1)S(1)}, bf16[96,1024]{1,0:T(8,128)(2,1)S(1)}, u32[]{:S(2)}, u32[]{:S(2)}) collective-permute-start(bf16[96,1024]{1,0:T(8,128)(2,1)S(1)} %get-tuple-element.37.refs_0_), channel_id=1, source_target_pairs={{0,1},{1,0},{2,3},{3,2},{4,5},{5,4},{6,7},{7,6},{8,9},{9,8},{10,11... | collective-permute-start | bytes 589832 | tf_op jit(solution)/shard_map/spread_first/ppermute | solution.py:27
  67.9 8.0 %collective-permute-start.20 = (bf16[3,128,256]{2,1,0:T(8,128)(2,1)S(1)}, bf16[3,128,256]{2,1,0:T(8,128)(2,1)S(1)}, u32[]{:S(2)}, u32[]{:S(2)}) collective-permute-start(bf16[3,128,256]{2,1,0:T(8,128)(2,1)S(1)} %get-tuple-element.42), channel_id=1, source_target_pairs={{0,16},{4,20},{8,24},{12,28},{16,0},{20,4},{24,8},{28,12},{1,17},{... | collective-permute-start | bytes 589832 | tf_op jit(solution)/shard_map/groups/ppermute | solution.py:27
  69.8 6.6 %collective-permute-start.21 = (bf16[3,128,256]{2,1,0:T(8,128)(2,1)S(1)}, bf16[3,128,256]{2,1,0:T(8,128)(2,1)S(1)}, u32[]{:S(2)}, u32[]{:S(2)}) collective-permute-start(bf16[3,128,256]{2,1,0:T(8,128)(2,1)S(1)} %get-tuple-element.43), channel_id=1, source_target_pairs={{0,24},{4,28},{8,16},{12,20},{16,8},{20,12},{24,0},{28,4},{1,25},{... | collective-permute-start | bytes 589832 | tf_op jit(solution)/shard_map/groups/ppermute | solution.py:27
  71.3 5.9 %collective-permute-start.19 = (bf16[3,128,256]{2,1,0:T(8,128)(2,1)S(1)}, bf16[3,128,256]{2,1,0:T(8,128)(2,1)S(1)}, u32[]{:S(2)}, u32[]{:S(2)}) collective-permute-start(bf16[3,128,256]{2,1,0:T(8,128)(2,1)S(1)} %get-tuple-element.41.refs_4_), channel_id=1, source_target_pairs={{0,8},{4,12},{8,0},{12,4},{16,24},{20,28},{24,16},{28,20},{1,9},{5... | collective-permute-start | bytes 589832 | tf_op jit(solution)/shard_map/groups/ppermute | solution.py:27
  79.8 1.8 %collective-permute-start.22 = (bf16[4,2,16,1536]{3,2,1,0:T(8,128)(2,1)S(1)}, bf16[4,2,16,1536]{3,2,1,0:T(8,128)(2,1)S(1)}, u32[]{:S(2)}, u32[]{:S(2)}) collective-permute-start(bf16[4,2,16,1536]{3,2,1,0:T(8,128)(2,1)S(1)} %get-tuple-element.45), channel_id=1, source_target_pairs={{0,4},{4,0},{8,12},{12,8},{16,20},{20,16},{24,28},{28,24},{1,5},{5... | collective-permute-start | bytes 1179656 | tf_op jit(solution)/shard_map/cores/ppermute | solution.py:27
  81.7 5.1 %collective-permute-start.23 = (bf16[2,16,1536]{2,1,0:T(8,128)(2,1)S(1)}, bf16[2,16,1536]{2,1,0:T(8,128)(2,1)S(1)}, u32[]{:S(2)}, u32[]{:S(2)}) collective-permute-start(bf16[2,16,1536]{2,1,0:T(8,128)(2,1)S(1)} %get-tuple-element.47), channel_id=1, source_target_pairs={{0,8},{4,12},{8,0},{12,4},{16,24},{20,28},{24,16},{28,20},{1,9},{5... | collective-permute-start | bytes 294920 | tf_op jit(solution)/shard_map/chips/ppermute | solution.py:27
  83.7 6.7 %collective-permute-start.24 = (bf16[2,16,1536]{2,1,0:T(8,128)(2,1)S(1)}, bf16[2,16,1536]{2,1,0:T(8,128)(2,1)S(1)}, u32[]{:S(2)}, u32[]{:S(2)}) collective-permute-start(bf16[2,16,1536]{2,1,0:T(8,128)(2,1)S(1)} %get-tuple-element.48), channel_id=1, source_target_pairs={{0,16},{4,20},{8,24},{12,28},{16,0},{20,4},{24,8},{28,12},{1,17},{... | collective-permute-start | bytes 294920 | tf_op jit(solution)/shard_map/chips/ppermute | solution.py:27
  83.8 6.5 %collective-permute-start.25 = (bf16[2,16,1536]{2,1,0:T(8,128)(2,1)S(1)}, bf16[2,16,1536]{2,1,0:T(8,128)(2,1)S(1)}, u32[]{:S(2)}, u32[]{:S(2)}) collective-permute-start(bf16[2,16,1536]{2,1,0:T(8,128)(2,1)S(1)} %get-tuple-element.49), channel_id=1, source_target_pairs={{0,24},{4,28},{8,16},{12,20},{16,8},{20,12},{24,0},{28,4},{1,25},{... | collective-permute-start | bytes 294920 | tf_op jit(solution)/shard_map/chips/ppermute | solution.py:27

commit v4 on v3

--- a/solution.py
+++ b/solution.py
@@ -389,6 +389,17 @@
     early = n_exp // 2
     with jax.named_scope("spread_first"):
         sooner = swapped(slots, "exp", early)
+    down_v, down_done = call(
+        load_down_kernel,
+        "load_down",
+        [pltpu.VMEM(w_down.shape, BF16), shape((8, LANES), F32)],
+        down_w,
+        slots,
+        scratch=[pltpu.SemaphoreType.DMA((4 * LOADS,))],
+        hbm=1,
+        unused=1,
+        cost=False,
+    )
     merged = call(
         functools.partial(merge_kernel, flips=flips),
         "merge",
@@ -399,8 +410,9 @@
         own,
         *peers,
         sooner,
+        down_done,
         smem=3,
-        unused=1,
+        unused=2,
     )
     with jax.named_scope("spread_second"):
         second = [merged] + [swapped(merged, "exp", k) for k in range(1, n_exp)]
@@ -418,24 +430,19 @@
         with jax.named_scope("groups"):
             return out, [swapped(out[j - 1], "tok", j * span) for j in others]
 
-    down_v, down_done = call(
-        load_down_kernel,
-        "load_down",
-        [pltpu.VMEM(w_down.shape, BF16), shape((8, LANES), F32)],
-        down_w,
-        second[1],
-        scratch=[pltpu.SemaphoreType.DMA((4 * LOADS,))],
-        hbm=1,
-        unused=1,
-        cost=False,
-    )
-    own_out, groups = grouped(second[:1], down_done)
-    waiting, _ = lax.optimization_barrier((slots, down_done))
+    own_out, groups = grouped(second[:n_exp // 2])
+    beside, _ = lax.optimization_barrier((slots, own_out[0]))
+    waiting, *_ = lax.optimization_barrier((slots, second[n_exp // 2]))
     with jax.named_scope("spread_first"):
-        first = [slots] + [
-            sooner if k == early else swapped(waiting, "exp", k) for k in range(1, n_exp)
-        ]
-    far_out, more = grouped(second[1:], *groups)
+        first = [slots]
+        for k in range(1, n_exp):
+            if k == n_exp // 2:
+                first.append(sooner)
+            elif k < n_exp // 2:
+                first.append(swapped(beside, "exp", k))
+            else:
+                first.append(swapped(waiting, "exp", k))
+    far_out, more = grouped(second[n_exp // 2:], *groups)
     initial = call(
         functools.partial(first_down_kernel, shard=shard, n_exp=n_exp),
         "first_down",

time: 91.2 us -> 89.2 us (0.978)
  waiting for transfers between devices: 22.6 us -> 21.6 us
    ppermute x26, waiting for transfers between devices: 22.6 us -> 21.6 us  [swapped(): return lax.ppermute(value, axis, [(i, i ^ by) for i in range(devices)])]
    ppermute x26, starting transfers between devices: 34 us -> 33.1 us  [swapped(): return lax.ppermute(value, axis, [(i, i ^ by) for i in range(devices)])]
  transfers between devices with their start and end apart: 26 -> 26, of which waited for: 14 -> 13; matrix products, arithmetic and copies ran while one was open for 0% -> 0% of each run, Pallas kernels for 22% -> 23%
where the time goes in v4:
time: 89.2 us; the launch traced here: 89.1 us
  Pallas kernels  33.2 us (37%)
  starting transfers between devices  33.1 us (37%)
  waiting for transfers between devices  21.6 us (24%)
    ppermute x26, starting transfers between devices, swapped(): return lax.ppermute(value, axis, [(i, i ^ by) for i in range(devices)])  33.1 us
    pallas_call x11, Pallas kernels, call(): pl.pallas_call(kernel, in_specs=specs, out_specs=[IN_VMEM] * len(out_shap...  22 us
    ppermute x26, waiting for transfers between devices, swapped(): return lax.ppermute(value, axis, [(i, i ^ by) for i in range(devices)])  21.6 us
    pallas_call x2, Pallas kernels, load(): pl.pallas_call(functools.partial(load_kernel, ks=ks), in_specs=[IN_SMEM,...  11.2 us
  transfers between devices with their start and end apart: 26, of which 13 were waited for; matrix products, arithmetic and copies ran while one was open for 0% of the time, Pallas kernels for 23%

profile of v4, /device:TPU:0, one launch (start us, length us, event | category | flops | bytes accessed | tf_op | source)
XLA Modules:
  0.0 89.1 jit_solution(14227239218930618080)
XLA Ops:
  0.6 4.1 %collective-permute-start.1 = (bf16[16,1536]{1,0:T(8,128)(2,1)}, bf16[16,1536]{1,0:T(8,128)(2,1)S(1)}, u32[]{:S(2)}, u32[]{:S(2)}) collective-permute-start(bf16[16,1536]{1,0:T(8,128)(2,1)} %param.8), channel_id=1, source_target_pairs={{0,2},{1,3},{2,0},{3,1},{4,6},{5,7},{6,4},{7,5},{8,10},{9,11},{10,... | collective-permute-start | bytes 147464 | tf_op jit(solution)/shard_map/gather_tokens/ppermute | solution.py:27
  4.7 1.6 %collective-permute-start = (bf16[16,1536]{1,0:T(8,128)(2,1)}, bf16[16,1536]{1,0:T(8,128)(2,1)S(1)}, u32[]{:S(2)}, u32[]{:S(2)}) collective-permute-start(bf16[16,1536]{1,0:T(8,128)(2,1)} %param.8), channel_id=1, source_target_pairs={{0,1},{1,0},{2,3},{3,2},{4,5},{5,4},{6,7},{7,6},{8,9},{9,8},{10,11... | collective-permute-start | bytes 147464 | tf_op jit(solution)/shard_map/gather_tokens/ppermute | solution.py:27
  6.3 0.0 collective-permute-start.2
  6.3 0.1 pad_add_fusion.place
  6.4 5.3 %load.2 = (bf16[2,4,1024,1536]{3,2,1,0:T(8,128)(2,1)S(1)}, f32[8,128]{1,0:T(8,128)S(1)}) custom-call(s32[2]{0:T(128)S(1)} %pad_add_fusion.place, bf16[1024,6144]{1,0:T(8,128)(2,1)} %gate_w.3, bf16[1024,6144]{1,0:T(8,128)(2,1)} %up_w.3), custom_call_target="tpu_custom_call" | custom-call | tf_op jit(solution)/shard_map/load/pallas_call | solution.py:331
  11.7 0.2 notes.1
  12.0 0.0 collective-permute-done
  12.0 0.0 collective-permute-done.1
  12.1 0.3 collective-permute-done.2
  12.4 2.5 %collective-permute-start.5 = (bf16[16,6272]{1,0:T(8,128)(2,1)S(1)}, bf16[16,6272]{1,0:T(8,128)(2,1)S(1)}, u32[]{:S(2)}, u32[]{:S(2)}) collective-permute-start(bf16[16,6272]{1,0:T(8,128)(2,1)S(1)} %get-tuple-element.52.refs_1_), channel_id=1, source_target_pairs={{0,24},{4,28},{8,16},{12,20},{16,8},{20,12},{24,0},{28,4},{1,25},{... | collective-permute-start | bytes 602120 | tf_op jit(solution)/shard_map/gather_tokens/ppermute | solution.py:27
  14.9 0.5 collective-permute-start.4
  15.4 0.5 collective-permute-start.3
  16.0 5.9 %load.3 = (bf16[2,4,1024,1536]{3,2,1,0:T(8,128)(2,1)S(1)}, f32[8,128]{1,0:T(8,128)}) custom-call(s32[2]{0:T(128)S(1)} %pad_add_fusion.place, bf16[1024,6144]{1,0:T(8,128)(2,1)} %gate_w.3, bf16[1024,6144]{1,0:T(8,128)(2,1)} %up_w.3, bf16[2,4,1024,1536]{3,2,1,0:T(8,128)(2,1)S(1)} %get-tuple-element.28.refs_0_, ...), custom_call_target="tpu_custom_call", output_to_operand_aliasing={{0}: (3, {})} | custom-call | tf_op jit(solution)/shard_map/gather_tokens/load/pallas_call | solution.py:331
  21.9 1.6 %collective-permute-done.4 = bf16[16,6272]{1,0:T(8,128)(2,1)S(1)} collective-permute-done((bf16[16,6272]{1,0:T(8,128)(2,1)S(1)}, bf16[16,6272]{1,0:T(8,128)(2,1)S(1)}, u32[]{:S(2)}, u32[]{:S(2)}) %collective-permute-start.4) | collective-permute-done | bytes 200736 | tf_op jit(solution)/shard_map/gather_tokens/ppermute | solution.py:27
  23.5 0.1 collective-permute-done.3
  23.6 0.1 pad_maximum_fusion
  23.7 0.1 collective-permute-start.6
  23.8 2.2 %collective-permute-done.6 = bf16[64,6272]{1,0:T(8,128)(2,1)S(1)} collective-permute-done((bf16[64,6272]{1,0:T(8,128)(2,1)S(1)}, bf16[64,6272]{1,0:T(8,128)(2,1)S(1)}, u32[]{:S(2)}, u32[]{:S(2)}) %collective-permute-start.6) | collective-permute-done | bytes 802848 | tf_op jit(solution)/shard_map/gather_tokens/ppermute | solution.py:27
  26.1 0.1 constant_dynamic-update-slice_fusion.5.x
  26.2 6.2 %project_sent.1 = (bf16[96,768]{1,0:T(8,128)(2,1)S(1)}, bf16[2,256,128]{2,1,0:T(8,128)(2,1)S(1)}, bf16[2,256,128]{2,1,0:T(8,128)(2,1)S(1)}, bf16[2,256,128]{2,1,0:T(8,128)(2,1)S(1)}) custom-call(s32[2]{0:T(128)S(1)} %pad_add_fusion.place, bf16[128,6272]{1,0:T(8,128)(2,1)S(1)} %constant_dynamic-update-slice_fusion.5.x, ...), custom_call_target="tpu_custom_call" | custom-call | tf_op jit(solution)/shard_map/project_sent/pallas_call | solution.py:317
  32.4 2.5 %project_own.1 = (bf16[96,1024]{1,0:T(8,128)(2,1)S(1)}, f32[2,256,128]{2,1,0:T(8,128)S(1)}) custom-call(s32[2]{0:T(128)S(1)} %pad_add_fusion.place, bf16[128,6272]{1,0:T(8,128)(2,1)S(1)} %constant_dynamic-update-slice_fusion.5.x, bf16[2,4,1024,1536]{3,2,1,0:T(8,128)(2,1)S(1)} %get-tuple-element.29.blocks, bf16[96,768]{1,0:T(8,128)(2,1)S(1)} %get-tuple-element.30.others), custom_call_target="tpu_custom_call" | custom-call | tf_op jit(solution)/shard_map/project_own/pallas_call | solution.py:317
  34.9 1.7 %collective-permute-start.10 = (bf16[96,1024]{1,0:T(8,128)(2,1)S(1)}, bf16[96,1024]{1,0:T(8,128)(2,1)S(1)}, u32[]{:S(2)}, u32[]{:S(2)}) collective-permute-start(bf16[96,1024]{1,0:T(8,128)(2,1)S(1)} %get-tuple-element.40.refs_0_), channel_id=1, source_target_pairs={{0,2},{1,3},{2,0},{3,1},{4,6},{5,7},{6,4},{7,5},{8,10},{9,11},{10,... | collective-permute-start | bytes 589832 | tf_op jit(solution)/shard_map/spread_first/ppermute | solution.py:27
  36.6 1.5 %collective-permute-start.7 = (bf16[2,256,128]{2,1,0:T(8,128)(2,1)S(1)}, bf16[2,256,128]{2,1,0:T(8,128)(2,1)S(1)}, u32[]{:S(2)}, u32[]{:S(2)}) collective-permute-start(bf16[2,256,128]{2,1,0:T(8,128)(2,1)S(1)} %get-tuple-element.34), channel_id=1, source_target_pairs={{0,8},{4,12},{8,0},{12,4},{16,24},{20,28},{24,16},{28,20},{1,9},{5... | collective-permute-start | bytes 393224 | tf_op jit(solution)/shard_map/peers/ppermute | solution.py:27
  38.1 0.7 collective-permute-start.8
  38.9 1.3 %collective-permute-start.9 = (bf16[2,256,128]{2,1,0:T(8,128)(2,1)S(1)}, bf16[2,256,128]{2,1,0:T(8,128)(2,1)S(1)}, u32[]{:S(2)}, u32[]{:S(2)}) collective-permute-start(bf16[2,256,128]{2,1,0:T(8,128)(2,1)S(1)} %get-tuple-element.36), channel_id=1, source_target_pairs={{0,24},{4,28},{8,16},{12,20},{16,8},{20,12},{24,0},{28,4},{1,25},{... | collective-permute-start | bytes 393224 | tf_op jit(solution)/shard_map/peers/ppermute | solution.py:27
  40.1 4.7 %load_down.1 = (bf16[4096,1536]{1,0:T(8,128)(2,1)S(1)}, f32[8,128]{1,0:T(8,128)S(1)}) custom-call(bf16[4096,1536]{1,0:T(8,128)(2,1)} %weight.1, bf16[96,1024]{1,0:T(8,128)(2,1)S(1)} %get-tuple-element.40.refs_0_), custom_call_target="tpu_custom_call" | custom-call | tf_op jit(solution)/shard_map/load_down/pallas_call | solution.py:317
  44.9 0.0 collective-permute-done.7.refs_0_
  44.9 1.0 %collective-permute-done.8.refs_1_ = bf16[2,256,128]{2,1,0:T(8,128)(2,1)S(1)} collective-permute-done((bf16[2,256,128]{2,1,0:T(8,128)(2,1)S(1)}, bf16[2,256,128]{2,1,0:T(8,128)(2,1)S(1)}, u32[]{:S(2)}, u32[]{:S(2)}) %collective-permute-start.8) | collective-permute-done | bytes 131104 | tf_op jit(solution)/shard_map/peers/ppermute | solution.py:27
  45.9 0.0 collective-permute-done.9.refs_2_
  45.9 1.1 %collective-permute-done.10.refs_3_.refs_2_ = bf16[96,1024]{1,0:T(8,128)(2,1)S(1)} collective-permute-done((bf16[96,1024]{1,0:T(8,128)(2,1)S(1)}, bf16[96,1024]{1,0:T(8,128)(2,1)S(1)}, u32[]{:S(2)}, u32[]{:S(2)}) %collective-permute-start.10) | collective-permute-done | bytes 196640 | tf_op jit(solution)/shard_map/spread_first/ppermute | solution.py:27
  47.1 1.0 %merge.1.refs_0_ = bf16[2,128,256]{2,1,0:T(8,128)(2,1)S(1)} custom-call(s32[2]{0:T(128)S(1)} %pad_add_fusion.place, s32[4]{0:T(128)S(1)} %copy-done, s32[4]{0:T(128)S(1)} %copy-done.1, f32[2,256,128]{2,1,0:T(8,128)S(1)} %get-tuple-element.33.own, bf16[2,256,128]{2,1,0:T(8,128)(2,1)S(1)} %collective-permute-done.7.refs_0_, ...), custom_call_target="tpu_custom_call" | custom-call | flops 1 | bytes 1 | tf_op jit(solution)/shard_map/merge/pallas_call | solution.py:317
  48.0 1.4 %collective-permute-start.11 = (bf16[2,128,256]{2,1,0:T(8,128)(2,1)S(1)}, bf16[2,128,256]{2,1,0:T(8,128)(2,1)S(1)}, u32[]{:S(2)}, u32[]{:S(2)}) collective-permute-start(bf16[2,128,256]{2,1,0:T(8,128)(2,1)S(1)} %merge.1.refs_0_), channel_id=1, source_target_pairs={{0,1},{1,0},{2,3},{3,2},{4,5},{5,4},{6,7},{7,6},{8,9},{9,8},{10,11... | collective-permute-start | bytes 393224 | tf_op jit(solution)/shard_map/spread_second/ppermute | solution.py:27
  49.5 1.7 %collective-permute-start.13 = (bf16[2,128,256]{2,1,0:T(8,128)(2,1)S(1)}, bf16[2,128,256]{2,1,0:T(8,128)(2,1)S(1)}, u32[]{:S(2)}, u32[]{:S(2)}) collective-permute-start(bf16[2,128,256]{2,1,0:T(8,128)(2,1)S(1)} %merge.1.refs_0_), channel_id=1, source_target_pairs={{0,2},{1,3},{2,0},{3,1},{4,6},{5,7},{6,4},{7,5},{8,10},{9,11},{10,... | collective-permute-start | bytes 393224 | tf_op jit(solution)/shard_map/spread_second/ppermute | solution.py:27
  51.2 1.3 %collective-permute-start.15 = (bf16[2,128,256]{2,1,0:T(8,128)(2,1)S(1)}, bf16[2,128,256]{2,1,0:T(8,128)(2,1)S(1)}, u32[]{:S(2)}, u32[]{:S(2)}) collective-permute-start(bf16[2,128,256]{2,1,0:T(8,128)(2,1)S(1)} %merge.1.refs_0_), channel_id=1, source_target_pairs={{0,3},{1,2},{2,1},{3,0},{4,7},{5,6},{6,5},{7,4},{8,11},{9,10},{10,... | collective-permute-start | bytes 393224 | tf_op jit(solution)/shard_map/spread_second/ppermute | solution.py:27
  52.5 2.1 %collective-permute-done.11.refs_1_ = bf16[2,128,256]{2,1,0:T(8,128)(2,1)S(1)} collective-permute-done((bf16[2,128,256]{2,1,0:T(8,128)(2,1)S(1)}, bf16[2,128,256]{2,1,0:T(8,128)(2,1)S(1)}, u32[]{:S(2)}, u32[]{:S(2)}) %collective-permute-start.11) | collective-permute-done | bytes 131104 | tf_op jit(solution)/shard_map/spread_second/ppermute | solution.py:27
  54.6 0.6 route.2
  55.2 1.9 %collective-permute-start.17 = (bf16[2,128,256]{2,1,0:T(8,128)(2,1)S(1)}, bf16[2,128,256]{2,1,0:T(8,128)(2,1)S(1)}, u32[]{:S(2)}, u32[]{:S(2)}) collective-permute-start(bf16[2,128,256]{2,1,0:T(8,128)(2,1)S(1)} %get-tuple-element.41), channel_id=1, source_target_pairs={{0,16},{4,20},{8,24},{12,28},{16,0},{20,4},{24,8},{28,12},{1,17},{... | collective-permute-start | bytes 393224 | tf_op jit(solution)/shard_map/groups/ppermute | solution.py:27
  57.1 1.7 %collective-permute-start.18 = (bf16[2,128,256]{2,1,0:T(8,128)(2,1)S(1)}, bf16[2,128,256]{2,1,0:T(8,128)(2,1)S(1)}, u32[]{:S(2)}, u32[]{:S(2)}) collective-permute-start(bf16[2,128,256]{2,1,0:T(8,128)(2,1)S(1)} %get-tuple-element.42), channel_id=1, source_target_pairs={{0,24},{4,28},{8,16},{12,20},{16,8},{20,12},{24,0},{28,4},{1,25},{... | collective-permute-start | bytes 393224 | tf_op jit(solution)/shard_map/groups/ppermute | solution.py:27
  58.8 5.6 %collective-permute-done.13.refs_0_.refs_2_ = bf16[2,128,256]{2,1,0:T(8,128)(2,1)S(1)} collective-permute-done((bf16[2,128,256]{2,1,0:T(8,128)(2,1)S(1)}, bf16[2,128,256]{2,1,0:T(8,128)(2,1)S(1)}, u32[]{:S(2)}, u32[]{:S(2)}) %collective-permute-start.13) | collective-permute-done | bytes 131104 | tf_op jit(solution)/shard_map/spread_second/ppermute | solution.py:27
  64.4 0.0 collective-permute-start.14
  64.4 0.0 collective-permute-done.15.refs_1_.refs_3_
  64.4 3.4 %collective-permute-start.12 = (bf16[96,1024]{1,0:T(8,128)(2,1)S(1)}, bf16[96,1024]{1,0:T(8,128)(2,1)S(1)}, u32[]{:S(2)}, u32[]{:S(2)}) collective-permute-start(bf16[96,1024]{1,0:T(8,128)(2,1)S(1)} %get-tuple-element.40.refs_0_), channel_id=1, source_target_pairs={{0,1},{1,0},{2,3},{3,2},{4,5},{5,4},{6,7},{7,6},{8,9},{9,8},{10,11... | collective-permute-start | bytes 589832 | tf_op jit(solution)/shard_map/spread_first/ppermute | solution.py:27
  67.8 0.0 collective-permute-done.17.refs_3_.refs_5_
  67.8 0.0 collective-permute-done.18.refs_4_.refs_6_
  67.8 0.0 collective-permute-done.16.refs_2_.refs_4_
  67.8 0.6 route.3
  68.4 0.9 collective-permute-start.20
  69.3 1.2 %collective-permute-start.21 = (bf16[2,128,256]{2,1,0:T(8,128)(2,1)S(1)}, bf16[2,128,256]{2,1,0:T(8,128)(2,1)S(1)}, u32[]{:S(2)}, u32[]{:S(2)}) collective-permute-start(bf16[2,128,256]{2,1,0:T(8,128)(2,1)S(1)} %get-tuple-element.45), channel_id=1, source_target_pairs={{0,24},{4,28},{8,16},{12,20},{16,8},{20,12},{24,0},{28,4},{1,25},{... | collective-permute-start | bytes 393224 | tf_op jit(solution)/shard_map/groups/ppermute | solution.py:27
  70.5 1.4 %collective-permute-start.19 = (bf16[2,128,256]{2,1,0:T(8,128)(2,1)S(1)}, bf16[2,128,256]{2,1,0:T(8,128)(2,1)S(1)}, u32[]{:S(2)}, u32[]{:S(2)}) collective-permute-start(bf16[2,128,256]{2,1,0:T(8,128)(2,1)S(1)} %get-tuple-element.43.refs_4_), channel_id=1, source_target_pairs={{0,8},{4,12},{8,0},{12,4},{16,24},{20,28},{24,16},{28,20},{1,9},{5... | collective-permute-start | bytes 393224 | tf_op jit(solution)/shard_map/groups/ppermute | solution.py:27
  71.9 0.0 collective-permute-done.14.refs_3_
  72.0 1.6 %collective-permute-done.12.refs_1_ = bf16[96,1024]{1,0:T(8,128)(2,1)S(1)} collective-permute-done((bf16[96,1024]{1,0:T(8,128)(2,1)S(1)}, bf16[96,1024]{1,0:T(8,128)(2,1)S(1)}, u32[]{:S(2)}, u32[]{:S(2)}) %collective-permute-start.12) | collective-permute-done | bytes 196640 | tf_op jit(solution)/shard_map/spread_first/ppermute | solution.py:27
  73.5 2.7 %first_down.1.initial = f32[128,1536]{1,0:T(8,128)S(1)} custom-call(s32[2]{0:T(128)S(1)} %pad_add_fusion.place, bf16[128,128]{1,0:T(8,128)(2,1)S(1)} %slice.4.notes, bf16[4096,1536]{1,0:T(8,128)(2,1)S(1)} %get-tuple-element.32.weight, bf16[96,1024]{1,0:T(8,128)(2,1)S(1)} %get-tuple-element.40.refs_0_, bf16[96,1024]{1,0:T(8,128)(2,1)S(1)} %collective-permute-done.12.refs_1_, ...), custom_call_target="tpu_custom_call" | custom-call | tf_op jit(solution)/shard_map/first_down/pallas_call | solution.py:317
  76.3 0.0 collective-permute-done.21.refs_9_
  76.3 2.6 %second_down.1 = (f32[4,2,16,1536]{3,2,1,0:T(8,128)S(1)}, bf16[4,2,16,1536]{3,2,1,0:T(8,128)(2,1)S(1)}) custom-call(s32[2]{0:T(128)S(1)} %pad_add_fusion.place, s32[4]{0:T(128)S(1)} %copy-done, s32[4]{0:T(128)S(1)} %copy-done.1, bf16[128,128]{1,0:T(8,128)(2,1)S(1)} %slice.4.notes, bf16[4096,1536]{1,0:T(8,128)(2,1)S(1)} %get-tuple-element.32.weight, ...), custom_call_target="tpu_custom_call" | custom-call | tf_op jit(solution)/shard_map/second_down/pallas_call | solution.py:317
  79.0 0.1 collective-permute-start.22
  79.0 1.7 %collective-permute-done.22.theirs = bf16[4,2,16,1536]{3,2,1,0:T(8,128)(2,1)S(1)} collective-permute-done((bf16[4,2,16,1536]{3,2,1,0:T(8,128)(2,1)S(1)}, bf16[4,2,16,1536]{3,2,1,0:T(8,128)(2,1)S(1)}, u32[]{:S(2)}, u32[]{:S(2)}) %collective-permute-start.22) | collective-permute-done | bytes 393248 | tf_op jit(solution)/shard_map/cores/ppermute | solution.py:27
  80.7 0.1 cores.1
  80.8 0.6 collective-permute-start.23
  81.5 1.4 %collective-permute-start.24 = (bf16[2,16,1536]{2,1,0:T(8,128)(2,1)S(1)}, bf16[2,16,1536]{2,1,0:T(8,128)(2,1)S(1)}, u32[]{:S(2)}, u32[]{:S(2)}) collective-permute-start(bf16[2,16,1536]{2,1,0:T(8,128)(2,1)S(1)} %get-tuple-element.50), channel_id=1, source_target_pairs={{0,16},{4,20},{8,24},{12,28},{16,0},{20,4},{24,8},{28,12},{1,17},{... | collective-permute-start | bytes 294920 | tf_op jit(solution)/shard_map/chips/ppermute | solution.py:27
  82.9 1.5 %collective-permute-start.25 = (bf16[2,16,1536]{2,1,0:T(8,128)(2,1)S(1)}, bf16[2,16,1536]{2,1,0:T(8,128)(2,1)S(1)}, u32[]{:S(2)}, u32[]{:S(2)}) collective-permute-start(bf16[2,16,1536]{2,1,0:T(8,128)(2,1)S(1)} %get-tuple-element.51), channel_id=1, source_target_pairs={{0,24},{4,28},{8,16},{12,20},{16,8},{20,12},{24,0},{28,4},{1,25},{... | collective-permute-start | bytes 294920 | tf_op jit(solution)/shard_map/chips/ppermute | solution.py:27
  84.4 2.0 %collective-permute-done.23.refs_0_ = bf16[2,16,1536]{2,1,0:T(8,128)(2,1)S(1)} collective-permute-done((bf16[2,16,1536]{2,1,0:T(8,128)(2,1)S(1)}, bf16[2,16,1536]{2,1,0:T(8,128)(2,1)S(1)}, u32[]{:S(2)}, u32[]{:S(2)}) %collective-permute-start.23) | collective-permute-done | bytes 98336 | tf_op jit(solution)/shard_map/chips/ppermute | solution.py:27
  86.4 0.8 collective-permute-done.24.refs_1_
  87.2 1.2 %collective-permute-done.25.refs_2_ = bf16[2,16,1536]{2,1,0:T(8,128)(2,1)S(1)} collective-permute-done((bf16[2,16,1536]{2,1,0:T(8,128)(2,1)S(1)}, bf16[2,16,1536]{2,1,0:T(8,128)(2,1)S(1)}, u32[]{:S(2)}, u32[]{:S(2)}) %collective-permute-start.25) | collective-permute-done | bytes 98336 | tf_op jit(solution)/shard_map/chips/ppermute | solution.py:27
  88.4 0.7 finish.1
  (23 shorter events, 0.2 us)
Async XLA Ops:
  0.6 11.4 %collective-permute-start.1 = (bf16[16,1536]{1,0:T(8,128)(2,1)}, bf16[16,1536]{1,0:T(8,128)(2,1)S(1)}, u32[]{:S(2)}, u32[]{:S(2)}) collective-permute-start(bf16[16,1536]{1,0:T(8,128)(2,1)} %param.8), channel_id=1, source_target_pairs={{0,2},{1,3},{2,0},{3,1},{4,6},{5,7},{6,4},{7,5},{8,10},{9,11},{10,... | collective-permute-start | bytes 147464 | tf_op jit(solution)/shard_map/gather_tokens/ppermute | solution.py:27
  4.7 7.3 %collective-permute-start = (bf16[16,1536]{1,0:T(8,128)(2,1)}, bf16[16,1536]{1,0:T(8,128)(2,1)S(1)}, u32[]{:S(2)}, u32[]{:S(2)}) collective-permute-start(bf16[16,1536]{1,0:T(8,128)(2,1)} %param.8), channel_id=1, source_target_pairs={{0,1},{1,0},{2,3},{3,2},{4,5},{5,4},{6,7},{7,6},{8,9},{9,8},{10,11... | collective-permute-start | bytes 147464 | tf_op jit(solution)/shard_map/gather_tokens/ppermute | solution.py:27
  6.3 6.1 %collective-permute-start.2 = (bf16[16,1536]{1,0:T(8,128)(2,1)}, bf16[16,1536]{1,0:T(8,128)(2,1)S(1)}, u32[]{:S(2)}, u32[]{:S(2)}) collective-permute-start(bf16[16,1536]{1,0:T(8,128)(2,1)} %param.8), channel_id=1, source_target_pairs={{0,3},{1,2},{2,1},{3,0},{4,7},{5,6},{6,5},{7,4},{8,11},{9,10},{10,... | collective-permute-start | bytes 147464 | tf_op jit(solution)/shard_map/gather_tokens/ppermute | solution.py:27
  6.4 5.3 %copy-start.2 = (s32[16,2]{0,1:T(2,128)S(1)}, s32[16,2]{0,1:T(2,128)}, u32[]{:S(2)}) copy-start(s32[16,2]{0,1:T(2,128)} %param.9) | copy-start | bytes 388
  6.4 5.3 %copy-start.3 = (s32[16,2]{0,1:T(2,128)S(1)}, s32[16,2]{0,1:T(2,128)}, u32[]{:S(2)}) copy-start(s32[16,2]{0,1:T(2,128)} %param.10) | copy-start | bytes 388
  6.4 5.6 %copy-start.4 = (bf16[16,1536]{1,0:T(8,128)(2,1)S(1)}, bf16[16,1536]{1,0:T(8,128)(2,1)}, u32[]{:S(2)}) copy-start(bf16[16,1536]{1,0:T(8,128)(2,1)} %param.8) | copy-start | bytes 147460
  12.4 9.5 %collective-permute-start.5 = (bf16[16,6272]{1,0:T(8,128)(2,1)S(1)}, bf16[16,6272]{1,0:T(8,128)(2,1)S(1)}, u32[]{:S(2)}, u32[]{:S(2)}) collective-permute-start(bf16[16,6272]{1,0:T(8,128)(2,1)S(1)} %get-tuple-element.52.refs_1_), channel_id=1, source_target_pairs={{0,24},{4,28},{8,16},{12,20},{16,8},{20,12},{24,0},{28,4},{1,25},{... | collective-permute-start | bytes 602120 | tf_op jit(solution)/shard_map/gather_tokens/ppermute | solution.py:27
  14.9 8.6 %collective-permute-start.4 = (bf16[16,6272]{1,0:T(8,128)(2,1)S(1)}, bf16[16,6272]{1,0:T(8,128)(2,1)S(1)}, u32[]{:S(2)}, u32[]{:S(2)}) collective-permute-start(bf16[16,6272]{1,0:T(8,128)(2,1)S(1)} %get-tuple-element.52.refs_1_), channel_id=1, source_target_pairs={{0,16},{4,20},{8,24},{12,28},{16,0},{20,4},{24,8},{28,12},{1,17},{... | collective-permute-start | bytes 602120 | tf_op jit(solution)/shard_map/gather_tokens/ppermute | solution.py:27
  15.4 8.2 %collective-permute-start.3 = (bf16[16,6272]{1,0:T(8,128)(2,1)S(1)}, bf16[16,6272]{1,0:T(8,128)(2,1)S(1)}, u32[]{:S(2)}, u32[]{:S(2)}) collective-permute-start(bf16[16,6272]{1,0:T(8,128)(2,1)S(1)} %get-tuple-element.52.refs_1_), channel_id=1, source_target_pairs={{0,8},{4,12},{8,0},{12,4},{16,24},{20,28},{24,16},{28,20},{1,9},{5... | collective-permute-start | bytes 602120 | tf_op jit(solution)/shard_map/gather_tokens/ppermute | solution.py:27
  23.7 2.4 %collective-permute-start.6 = (bf16[64,6272]{1,0:T(8,128)(2,1)S(1)}, bf16[64,6272]{1,0:T(8,128)(2,1)S(1)}, u32[]{:S(2)}, u32[]{:S(2)}) collective-permute-start(bf16[64,6272]{1,0:T(8,128)(2,1)S(1)} %pad_maximum_fusion), channel_id=1, source_target_pairs={{0,4},{4,0},{8,12},{12,8},{16,20},{20,16},{24,28},{28,24},{1,5},{5... | collective-permute-start | bytes 2408456 | tf_op jit(solution)/shard_map/gather_tokens/ppermute | solution.py:27
  34.9 12.1 %collective-permute-start.10 = (bf16[96,1024]{1,0:T(8,128)(2,1)S(1)}, bf16[96,1024]{1,0:T(8,128)(2,1)S(1)}, u32[]{:S(2)}, u32[]{:S(2)}) collective-permute-start(bf16[96,1024]{1,0:T(8,128)(2,1)S(1)} %get-tuple-element.40.refs_0_), channel_id=1, source_target_pairs={{0,2},{1,3},{2,0},{3,1},{4,6},{5,7},{6,4},{7,5},{8,10},{9,11},{10,... | collective-permute-start | bytes 589832 | tf_op jit(solution)/shard_map/spread_first/ppermute | solution.py:27
  36.6 8.2 %collective-permute-start.7 = (bf16[2,256,128]{2,1,0:T(8,128)(2,1)S(1)}, bf16[2,256,128]{2,1,0:T(8,128)(2,1)S(1)}, u32[]{:S(2)}, u32[]{:S(2)}) collective-permute-start(bf16[2,256,128]{2,1,0:T(8,128)(2,1)S(1)} %get-tuple-element.34), channel_id=1, source_target_pairs={{0,8},{4,12},{8,0},{12,4},{16,24},{20,28},{24,16},{28,20},{1,9},{5... | collective-permute-start | bytes 393224 | tf_op jit(solution)/shard_map/peers/ppermute | solution.py:27
  38.1 7.8 %collective-permute-start.8 = (bf16[2,256,128]{2,1,0:T(8,128)(2,1)S(1)}, bf16[2,256,128]{2,1,0:T(8,128)(2,1)S(1)}, u32[]{:S(2)}, u32[]{:S(2)}) collective-permute-start(bf16[2,256,128]{2,1,0:T(8,128)(2,1)S(1)} %get-tuple-element.35), channel_id=1, source_target_pairs={{0,16},{4,20},{8,24},{12,28},{16,0},{20,4},{24,8},{28,12},{1,17},{... | collective-permute-start | bytes 393224 | tf_op jit(solution)/shard_map/peers/ppermute | solution.py:27
  38.8 8.2 %copy-start = (s32[4]{0:T(128)S(1)}, s32[4]{0:T(128)}, u32[]{:S(2)}) copy-start(s32[4]{0:T(128)} %labels.7) | copy-start | bytes 52
  38.9 8.2 %copy-start.1 = (s32[4]{0:T(128)S(1)}, s32[4]{0:T(128)}, u32[]{:S(2)}) copy-start(s32[4]{0:T(128)} %freq.3) | copy-start | bytes 52
  38.9 7.1 %collective-permute-start.9 = (bf16[2,256,128]{2,1,0:T(8,128)(2,1)S(1)}, bf16[2,256,128]{2,1,0:T(8,128)(2,1)S(1)}, u32[]{:S(2)}, u32[]{:S(2)}) collective-permute-start(bf16[2,256,128]{2,1,0:T(8,128)(2,1)S(1)} %get-tuple-element.36), channel_id=1, source_target_pairs={{0,24},{4,28},{8,16},{12,20},{16,8},{20,12},{24,0},{28,4},{1,25},{... | collective-permute-start | bytes 393224 | tf_op jit(solution)/shard_map/peers/ppermute | solution.py:27
  48.0 6.6 %collective-permute-start.11 = (bf16[2,128,256]{2,1,0:T(8,128)(2,1)S(1)}, bf16[2,128,256]{2,1,0:T(8,128)(2,1)S(1)}, u32[]{:S(2)}, u32[]{:S(2)}) collective-permute-start(bf16[2,128,256]{2,1,0:T(8,128)(2,1)S(1)} %merge.1.refs_0_), channel_id=1, source_target_pairs={{0,1},{1,0},{2,3},{3,2},{4,5},{5,4},{6,7},{7,6},{8,9},{9,8},{10,11... | collective-permute-start | bytes 393224 | tf_op jit(solution)/shard_map/spread_second/ppermute | solution.py:27
  49.5 15.0 %collective-permute-start.13 = (bf16[2,128,256]{2,1,0:T(8,128)(2,1)S(1)}, bf16[2,128,256]{2,1,0:T(8,128)(2,1)S(1)}, u32[]{:S(2)}, u32[]{:S(2)}) collective-permute-start(bf16[2,128,256]{2,1,0:T(8,128)(2,1)S(1)} %merge.1.refs_0_), channel_id=1, source_target_pairs={{0,2},{1,3},{2,0},{3,1},{4,6},{5,7},{6,4},{7,5},{8,10},{9,11},{10,... | collective-permute-start | bytes 393224 | tf_op jit(solution)/shard_map/spread_second/ppermute | solution.py:27
  51.2 13.2 %collective-permute-start.15 = (bf16[2,128,256]{2,1,0:T(8,128)(2,1)S(1)}, bf16[2,128,256]{2,1,0:T(8,128)(2,1)S(1)}, u32[]{:S(2)}, u32[]{:S(2)}) collective-permute-start(bf16[2,128,256]{2,1,0:T(8,128)(2,1)S(1)} %merge.1.refs_0_), channel_id=1, source_target_pairs={{0,3},{1,2},{2,1},{3,0},{4,7},{5,6},{6,5},{7,4},{8,11},{9,10},{10,... | collective-permute-start | bytes 393224 | tf_op jit(solution)/shard_map/spread_second/ppermute | solution.py:27
  55.2 12.6 %collective-permute-start.17 = (bf16[2,128,256]{2,1,0:T(8,128)(2,1)S(1)}, bf16[2,128,256]{2,1,0:T(8,128)(2,1)S(1)}, u32[]{:S(2)}, u32[]{:S(2)}) collective-permute-start(bf16[2,128,256]{2,1,0:T(8,128)(2,1)S(1)} %get-tuple-element.41), channel_id=1, source_target_pairs={{0,16},{4,20},{8,24},{12,28},{16,0},{20,4},{24,8},{28,12},{1,17},{... | collective-permute-start | bytes 393224 | tf_op jit(solution)/shard_map/groups/ppermute | solution.py:27
  57.1 10.7 %collective-permute-start.18 = (bf16[2,128,256]{2,1,0:T(8,128)(2,1)S(1)}, bf16[2,128,256]{2,1,0:T(8,128)(2,1)S(1)}, u32[]{:S(2)}, u32[]{:S(2)}) collective-permute-start(bf16[2,128,256]{2,1,0:T(8,128)(2,1)S(1)} %get-tuple-element.42), channel_id=1, source_target_pairs={{0,24},{4,28},{8,16},{12,20},{16,8},{20,12},{24,0},{28,4},{1,25},{... | collective-permute-start | bytes 393224 | tf_op jit(solution)/shard_map/groups/ppermute | solution.py:27
  58.8 9.0 %collective-permute-start.16 = (bf16[2,128,256]{2,1,0:T(8,128)(2,1)S(1)}, bf16[2,128,256]{2,1,0:T(8,128)(2,1)S(1)}, u32[]{:S(2)}, u32[]{:S(2)}) collective-permute-start(bf16[2,128,256]{2,1,0:T(8,128)(2,1)S(1)} %get-tuple-element.38), channel_id=1, source_target_pairs={{0,8},{4,12},{8,0},{12,4},{16,24},{20,28},{24,16},{28,20},{1,9},{5... | collective-permute-start | bytes 393224 | tf_op jit(solution)/shard_map/groups/ppermute | solution.py:27
  64.4 7.6 %collective-permute-start.14 = (bf16[96,1024]{1,0:T(8,128)(2,1)S(1)}, bf16[96,1024]{1,0:T(8,128)(2,1)S(1)}, u32[]{:S(2)}, u32[]{:S(2)}) collective-permute-start(bf16[96,1024]{1,0:T(8,128)(2,1)S(1)} %get-tuple-element.40.refs_0_), channel_id=1, source_target_pairs={{0,3},{1,2},{2,1},{3,0},{4,7},{5,6},{6,5},{7,4},{8,11},{9,10},{10,... | collective-permute-start | bytes 589832 | tf_op jit(solution)/shard_map/spread_first/ppermute | solution.py:27
  64.4 9.1 %collective-permute-start.12 = (bf16[96,1024]{1,0:T(8,128)(2,1)S(1)}, bf16[96,1024]{1,0:T(8,128)(2,1)S(1)}, u32[]{:S(2)}, u32[]{:S(2)}) collective-permute-start(bf16[96,1024]{1,0:T(8,128)(2,1)S(1)} %get-tuple-element.40.refs_0_), channel_id=1, source_target_pairs={{0,1},{1,0},{2,3},{3,2},{4,5},{5,4},{6,7},{7,6},{8,9},{9,8},{10,11... | collective-permute-start | bytes 589832 | tf_op jit(solution)/shard_map/spread_first/ppermute | solution.py:27
  68.4 7.9 %collective-permute-start.20 = (bf16[2,128,256]{2,1,0:T(8,128)(2,1)S(1)}, bf16[2,128,256]{2,1,0:T(8,128)(2,1)S(1)}, u32[]{:S(2)}, u32[]{:S(2)}) collective-permute-start(bf16[2,128,256]{2,1,0:T(8,128)(2,1)S(1)} %get-tuple-element.44), channel_id=1, source_target_pairs={{0,16},{4,20},{8,24},{12,28},{16,0},{20,4},{24,8},{28,12},{1,17},{... | collective-permute-start | bytes 393224 | tf_op jit(solution)/shard_map/groups/ppermute | solution.py:27
  69.3 7.0 %collective-permute-start.21 = (bf16[2,128,256]{2,1,0:T(8,128)(2,1)S(1)}, bf16[2,128,256]{2,1,0:T(8,128)(2,1)S(1)}, u32[]{:S(2)}, u32[]{:S(2)}) collective-permute-start(bf16[2,128,256]{2,1,0:T(8,128)(2,1)S(1)} %get-tuple-element.45), channel_id=1, source_target_pairs={{0,24},{4,28},{8,16},{12,20},{16,8},{20,12},{24,0},{28,4},{1,25},{... | collective-permute-start | bytes 393224 | tf_op jit(solution)/shard_map/groups/ppermute | solution.py:27
  70.5 5.8 %collective-permute-start.19 = (bf16[2,128,256]{2,1,0:T(8,128)(2,1)S(1)}, bf16[2,128,256]{2,1,0:T(8,128)(2,1)S(1)}, u32[]{:S(2)}, u32[]{:S(2)}) collective-permute-start(bf16[2,128,256]{2,1,0:T(8,128)(2,1)S(1)} %get-tuple-element.43.refs_4_), channel_id=1, source_target_pairs={{0,8},{4,12},{8,0},{12,4},{16,24},{20,28},{24,16},{28,20},{1,9},{5... | collective-permute-start | bytes 393224 | tf_op jit(solution)/shard_map/groups/ppermute | solution.py:27
  79.0 1.8 %collective-permute-start.22 = (bf16[4,2,16,1536]{3,2,1,0:T(8,128)(2,1)S(1)}, bf16[4,2,16,1536]{3,2,1,0:T(8,128)(2,1)S(1)}, u32[]{:S(2)}, u32[]{:S(2)}) collective-permute-start(bf16[4,2,16,1536]{3,2,1,0:T(8,128)(2,1)S(1)} %get-tuple-element.47), channel_id=1, source_target_pairs={{0,4},{4,0},{8,12},{12,8},{16,20},{20,16},{24,28},{28,24},{1,5},{5... | collective-permute-start | bytes 1179656 | tf_op jit(solution)/shard_map/cores/ppermute | solution.py:27
  80.8 5.6 %collective-permute-start.23 = (bf16[2,16,1536]{2,1,0:T(8,128)(2,1)S(1)}, bf16[2,16,1536]{2,1,0:T(8,128)(2,1)S(1)}, u32[]{:S(2)}, u32[]{:S(2)}) collective-permute-start(bf16[2,16,1536]{2,1,0:T(8,128)(2,1)S(1)} %get-tuple-element.49), channel_id=1, source_target_pairs={{0,8},{4,12},{8,0},{12,4},{16,24},{20,28},{24,16},{28,20},{1,9},{5... | collective-permute-start | bytes 294920 | tf_op jit(solution)/shard_map/chips/ppermute | solution.py:27
  81.5 5.7 %collective-permute-start.24 = (bf16[2,16,1536]{2,1,0:T(8,128)(2,1)S(1)}, bf16[2,16,1536]{2,1,0:T(8,128)(2,1)S(1)}, u32[]{:S(2)}, u32[]{:S(2)}) collective-permute-start(bf16[2,16,1536]{2,1,0:T(8,128)(2,1)S(1)} %get-tuple-element.50), channel_id=1, source_target_pairs={{0,16},{4,20},{8,24},{12,28},{16,0},{20,4},{24,8},{28,12},{1,17},{... | collective-permute-start | bytes 294920 | tf_op jit(solution)/shard_map/chips/ppermute | solution.py:27
  82.9 5.5 %collective-permute-start.25 = (bf16[2,16,1536]{2,1,0:T(8,128)(2,1)S(1)}, bf16[2,16,1536]{2,1,0:T(8,128)(2,1)S(1)}, u32[]{:S(2)}, u32[]{:S(2)}) collective-permute-start(bf16[2,16,1536]{2,1,0:T(8,128)(2,1)S(1)} %get-tuple-element.51), channel_id=1, source_target_pairs={{0,24},{4,28},{8,16},{12,20},{16,8},{20,12},{24,0},{28,4},{1,25},{... | collective-permute-start | bytes 294920 | tf_op jit(solution)/shard_map/chips/ppermute | solution.py:27

commit v5 on v4

--- a/solution.py
+++ b/solution.py
@@ -442,7 +442,7 @@
                 first.append(swapped(beside, "exp", k))
             else:
                 first.append(swapped(waiting, "exp", k))
-    far_out, more = grouped(second[n_exp // 2:], *groups)
+    far_out, more = grouped(second[n_exp // 2:], first[1], *groups)
     initial = call(
         functools.partial(first_down_kernel, shard=shard, n_exp=n_exp),
         "first_down",

time: 89.2 us -> 89.1 us (level)
  starting transfers between devices: 33.1 us -> 31.8 us
  waiting for transfers between devices: 21.6 us -> 22.7 us
    ppermute x26, starting transfers between devices: 33.1 us -> 31.8 us  [swapped(): return lax.ppermute(value, axis, [(i, i ^ by) for i in range(devices)])]
    ppermute x26, waiting for transfers between devices: 21.6 us -> 22.7 us  [swapped(): return lax.ppermute(value, axis, [(i, i ^ by) for i in range(devices)])]
  transfers between devices with their start and end apart: 26 -> 26, of which waited for: 13 -> 14; matrix products, arithmetic and copies ran while one was open for 0% -> 0% of each run, Pallas kernels for 23% -> 23%
where the time goes in v5:
time: 89.1 us; the launch traced here: 88.9 us
  Pallas kernels  33.2 us (37%)
  starting transfers between devices  31.8 us (36%)
  waiting for transfers between devices  22.7 us (25%)
    ppermute x26, starting transfers between devices, swapped(): return lax.ppermute(value, axis, [(i, i ^ by) for i in range(devices)])  31.8 us
    ppermute x26, waiting for transfers between devices, swapped(): return lax.ppermute(value, axis, [(i, i ^ by) for i in range(devices)])  22.7 us
    pallas_call x11, Pallas kernels, call(): pl.pallas_call(kernel, in_specs=specs, out_specs=[IN_VMEM] * len(out_shap...  22 us
    pallas_call x2, Pallas kernels, load(): pl.pallas_call(functools.partial(load_kernel, ks=ks), in_specs=[IN_SMEM,...  11.2 us
  transfers between devices with their start and end apart: 26, of which 14 were waited for; matrix products, arithmetic and copies ran while one was open for 0% of the time, Pallas kernels for 23%

profile of v5, /device:TPU:0, one launch (start us, length us, event | category | flops | bytes accessed | tf_op | source)
XLA Modules:
  0.0 88.9 jit_solution(6194299355352014658)
XLA Ops:
  0.6 4.1 %collective-permute-start.1 = (bf16[16,1536]{1,0:T(8,128)(2,1)}, bf16[16,1536]{1,0:T(8,128)(2,1)S(1)}, u32[]{:S(2)}, u32[]{:S(2)}) collective-permute-start(bf16[16,1536]{1,0:T(8,128)(2,1)} %param.8), channel_id=1, source_target_pairs={{0,2},{1,3},{2,0},{3,1},{4,6},{5,7},{6,4},{7,5},{8,10},{9,11},{10,... | collective-permute-start | bytes 147464 | tf_op jit(solution)/shard_map/gather_tokens/ppermute | solution.py:27
  4.7 1.6 %collective-permute-start = (bf16[16,1536]{1,0:T(8,128)(2,1)}, bf16[16,1536]{1,0:T(8,128)(2,1)S(1)}, u32[]{:S(2)}, u32[]{:S(2)}) collective-permute-start(bf16[16,1536]{1,0:T(8,128)(2,1)} %param.8), channel_id=1, source_target_pairs={{0,1},{1,0},{2,3},{3,2},{4,5},{5,4},{6,7},{7,6},{8,9},{9,8},{10,11... | collective-permute-start | bytes 147464 | tf_op jit(solution)/shard_map/gather_tokens/ppermute | solution.py:27
  6.3 0.0 collective-permute-start.2
  6.3 0.1 pad_add_fusion.place
  6.4 5.3 %load.2 = (bf16[2,4,1024,1536]{3,2,1,0:T(8,128)(2,1)S(1)}, f32[8,128]{1,0:T(8,128)S(1)}) custom-call(s32[2]{0:T(128)S(1)} %pad_add_fusion.place, bf16[1024,6144]{1,0:T(8,128)(2,1)} %gate_w.3, bf16[1024,6144]{1,0:T(8,128)(2,1)} %up_w.3), custom_call_target="tpu_custom_call" | custom-call | tf_op jit(solution)/shard_map/load/pallas_call | solution.py:331
  11.7 0.2 notes.1
  12.0 0.0 collective-permute-done
  12.0 0.0 collective-permute-done.1
  12.1 0.3 collective-permute-done.2
  12.4 2.5 %collective-permute-start.5 = (bf16[16,6272]{1,0:T(8,128)(2,1)S(1)}, bf16[16,6272]{1,0:T(8,128)(2,1)S(1)}, u32[]{:S(2)}, u32[]{:S(2)}) collective-permute-start(bf16[16,6272]{1,0:T(8,128)(2,1)S(1)} %get-tuple-element.52.refs_1_), channel_id=1, source_target_pairs={{0,24},{4,28},{8,16},{12,20},{16,8},{20,12},{24,0},{28,4},{1,25},{... | collective-permute-start | bytes 602120 | tf_op jit(solution)/shard_map/gather_tokens/ppermute | solution.py:27
  14.9 0.5 collective-permute-start.4
  15.4 0.5 collective-permute-start.3
  16.0 5.9 %load.3 = (bf16[2,4,1024,1536]{3,2,1,0:T(8,128)(2,1)S(1)}, f32[8,128]{1,0:T(8,128)}) custom-call(s32[2]{0:T(128)S(1)} %pad_add_fusion.place, bf16[1024,6144]{1,0:T(8,128)(2,1)} %gate_w.3, bf16[1024,6144]{1,0:T(8,128)(2,1)} %up_w.3, bf16[2,4,1024,1536]{3,2,1,0:T(8,128)(2,1)S(1)} %get-tuple-element.28.refs_0_, ...), custom_call_target="tpu_custom_call", output_to_operand_aliasing={{0}: (3, {})} | custom-call | tf_op jit(solution)/shard_map/gather_tokens/load/pallas_call | solution.py:331
  21.9 0.0 collective-permute-done.5
  21.9 1.6 %collective-permute-done.4 = bf16[16,6272]{1,0:T(8,128)(2,1)S(1)} collective-permute-done((bf16[16,6272]{1,0:T(8,128)(2,1)S(1)}, bf16[16,6272]{1,0:T(8,128)(2,1)S(1)}, u32[]{:S(2)}, u32[]{:S(2)}) %collective-permute-start.4) | collective-permute-done | bytes 200736 | tf_op jit(solution)/shard_map/gather_tokens/ppermute | solution.py:27
  23.5 0.1 collective-permute-done.3
  23.6 0.1 pad_maximum_fusion
  23.7 0.1 collective-permute-start.6
  23.8 2.2 %collective-permute-done.6 = bf16[64,6272]{1,0:T(8,128)(2,1)S(1)} collective-permute-done((bf16[64,6272]{1,0:T(8,128)(2,1)S(1)}, bf16[64,6272]{1,0:T(8,128)(2,1)S(1)}, u32[]{:S(2)}, u32[]{:S(2)}) %collective-permute-start.6) | collective-permute-done | bytes 802848 | tf_op jit(solution)/shard_map/gather_tokens/ppermute | solution.py:27
  26.1 0.1 constant_dynamic-update-slice_fusion.5.x
  26.2 6.2 %project_sent.1 = (bf16[96,768]{1,0:T(8,128)(2,1)S(1)}, bf16[2,256,128]{2,1,0:T(8,128)(2,1)S(1)}, bf16[2,256,128]{2,1,0:T(8,128)(2,1)S(1)}, bf16[2,256,128]{2,1,0:T(8,128)(2,1)S(1)}) custom-call(s32[2]{0:T(128)S(1)} %pad_add_fusion.place, bf16[128,6272]{1,0:T(8,128)(2,1)S(1)} %constant_dynamic-update-slice_fusion.5.x, ...), custom_call_target="tpu_custom_call" | custom-call | tf_op jit(solution)/shard_map/project_sent/pallas_call | solution.py:317
  32.4 2.5 %project_own.1 = (bf16[96,1024]{1,0:T(8,128)(2,1)S(1)}, f32[2,256,128]{2,1,0:T(8,128)S(1)}) custom-call(s32[2]{0:T(128)S(1)} %pad_add_fusion.place, bf16[128,6272]{1,0:T(8,128)(2,1)S(1)} %constant_dynamic-update-slice_fusion.5.x, bf16[2,4,1024,1536]{3,2,1,0:T(8,128)(2,1)S(1)} %get-tuple-element.29.blocks, bf16[96,768]{1,0:T(8,128)(2,1)S(1)} %get-tuple-element.30.others), custom_call_target="tpu_custom_call" | custom-call | tf_op jit(solution)/shard_map/project_own/pallas_call | solution.py:317
  34.9 1.7 %collective-permute-start.10 = (bf16[96,1024]{1,0:T(8,128)(2,1)S(1)}, bf16[96,1024]{1,0:T(8,128)(2,1)S(1)}, u32[]{:S(2)}, u32[]{:S(2)}) collective-permute-start(bf16[96,1024]{1,0:T(8,128)(2,1)S(1)} %get-tuple-element.40.refs_0_), channel_id=1, source_target_pairs={{0,2},{1,3},{2,0},{3,1},{4,6},{5,7},{6,4},{7,5},{8,10},{9,11},{10,... | collective-permute-start | bytes 589832 | tf_op jit(solution)/shard_map/spread_first/ppermute | solution.py:27
  36.6 1.5 %collective-permute-start.7 = (bf16[2,256,128]{2,1,0:T(8,128)(2,1)S(1)}, bf16[2,256,128]{2,1,0:T(8,128)(2,1)S(1)}, u32[]{:S(2)}, u32[]{:S(2)}) collective-permute-start(bf16[2,256,128]{2,1,0:T(8,128)(2,1)S(1)} %get-tuple-element.34), channel_id=1, source_target_pairs={{0,8},{4,12},{8,0},{12,4},{16,24},{20,28},{24,16},{28,20},{1,9},{5... | collective-permute-start | bytes 393224 | tf_op jit(solution)/shard_map/peers/ppermute | solution.py:27
  38.1 0.7 collective-permute-start.8
  38.8 1.3 %collective-permute-start.9 = (bf16[2,256,128]{2,1,0:T(8,128)(2,1)S(1)}, bf16[2,256,128]{2,1,0:T(8,128)(2,1)S(1)}, u32[]{:S(2)}, u32[]{:S(2)}) collective-permute-start(bf16[2,256,128]{2,1,0:T(8,128)(2,1)S(1)} %get-tuple-element.36), channel_id=1, source_target_pairs={{0,24},{4,28},{8,16},{12,20},{16,8},{20,12},{24,0},{28,4},{1,25},{... | collective-permute-start | bytes 393224 | tf_op jit(solution)/shard_map/peers/ppermute | solution.py:27
  40.1 4.7 %load_down.1 = (bf16[4096,1536]{1,0:T(8,128)(2,1)S(1)}, f32[8,128]{1,0:T(8,128)S(1)}) custom-call(bf16[4096,1536]{1,0:T(8,128)(2,1)} %weight.1, bf16[96,1024]{1,0:T(8,128)(2,1)S(1)} %get-tuple-element.40.refs_0_), custom_call_target="tpu_custom_call" | custom-call | tf_op jit(solution)/shard_map/load_down/pallas_call | solution.py:317
  44.8 0.0 collective-permute-done.7.refs_0_
  44.9 1.0 %collective-permute-done.8.refs_1_ = bf16[2,256,128]{2,1,0:T(8,128)(2,1)S(1)} collective-permute-done((bf16[2,256,128]{2,1,0:T(8,128)(2,1)S(1)}, bf16[2,256,128]{2,1,0:T(8,128)(2,1)S(1)}, u32[]{:S(2)}, u32[]{:S(2)}) %collective-permute-start.8) | collective-permute-done | bytes 131104 | tf_op jit(solution)/shard_map/peers/ppermute | solution.py:27
  45.9 1.1 %collective-permute-done.10.refs_3_.refs_2_ = bf16[96,1024]{1,0:T(8,128)(2,1)S(1)} collective-permute-done((bf16[96,1024]{1,0:T(8,128)(2,1)S(1)}, bf16[96,1024]{1,0:T(8,128)(2,1)S(1)}, u32[]{:S(2)}, u32[]{:S(2)}) %collective-permute-start.10) | collective-permute-done | bytes 196640 | tf_op jit(solution)/shard_map/spread_first/ppermute | solution.py:27
  47.1 1.0 %merge.1.refs_0_ = bf16[2,128,256]{2,1,0:T(8,128)(2,1)S(1)} custom-call(s32[2]{0:T(128)S(1)} %pad_add_fusion.place, s32[4]{0:T(128)S(1)} %copy-done, s32[4]{0:T(128)S(1)} %copy-done.1, f32[2,256,128]{2,1,0:T(8,128)S(1)} %get-tuple-element.33.own, bf16[2,256,128]{2,1,0:T(8,128)(2,1)S(1)} %collective-permute-done.7.refs_0_, ...), custom_call_target="tpu_custom_call" | custom-call | flops 1 | bytes 1 | tf_op jit(solution)/shard_map/merge/pallas_call | solution.py:317
  48.0 1.4 %collective-permute-start.11 = (bf16[2,128,256]{2,1,0:T(8,128)(2,1)S(1)}, bf16[2,128,256]{2,1,0:T(8,128)(2,1)S(1)}, u32[]{:S(2)}, u32[]{:S(2)}) collective-permute-start(bf16[2,128,256]{2,1,0:T(8,128)(2,1)S(1)} %merge.1.refs_0_), channel_id=1, source_target_pairs={{0,1},{1,0},{2,3},{3,2},{4,5},{5,4},{6,7},{7,6},{8,9},{9,8},{10,11... | collective-permute-start | bytes 393224 | tf_op jit(solution)/shard_map/spread_second/ppermute | solution.py:27
  49.4 1.8 %collective-permute-start.13 = (bf16[2,128,256]{2,1,0:T(8,128)(2,1)S(1)}, bf16[2,128,256]{2,1,0:T(8,128)(2,1)S(1)}, u32[]{:S(2)}, u32[]{:S(2)}) collective-permute-start(bf16[2,128,256]{2,1,0:T(8,128)(2,1)S(1)} %merge.1.refs_0_), channel_id=1, source_target_pairs={{0,2},{1,3},{2,0},{3,1},{4,6},{5,7},{6,4},{7,5},{8,10},{9,11},{10,... | collective-permute-start | bytes 393224 | tf_op jit(solution)/shard_map/spread_second/ppermute | solution.py:27
  51.2 4.1 %collective-permute-done.11.refs_1_ = bf16[2,128,256]{2,1,0:T(8,128)(2,1)S(1)} collective-permute-done((bf16[2,128,256]{2,1,0:T(8,128)(2,1)S(1)}, bf16[2,128,256]{2,1,0:T(8,128)(2,1)S(1)}, u32[]{:S(2)}, u32[]{:S(2)}) %collective-permute-start.11) | collective-permute-done | bytes 131104 | tf_op jit(solution)/shard_map/spread_second/ppermute | solution.py:27
  55.3 0.6 route.2
  55.9 0.1 collective-permute-start.12
  56.0 2.7 %collective-permute-start.15 = (bf16[2,128,256]{2,1,0:T(8,128)(2,1)S(1)}, bf16[2,128,256]{2,1,0:T(8,128)(2,1)S(1)}, u32[]{:S(2)}, u32[]{:S(2)}) collective-permute-start(bf16[2,128,256]{2,1,0:T(8,128)(2,1)S(1)} %merge.1.refs_0_), channel_id=1, source_target_pairs={{0,3},{1,2},{2,1},{3,0},{4,7},{5,6},{6,5},{7,4},{8,11},{9,10},{10,... | collective-permute-start | bytes 393224 | tf_op jit(solution)/shard_map/spread_second/ppermute | solution.py:27
  58.7 0.8 collective-permute-start.17
  59.5 1.5 %collective-permute-start.18 = (bf16[2,128,256]{2,1,0:T(8,128)(2,1)S(1)}, bf16[2,128,256]{2,1,0:T(8,128)(2,1)S(1)}, u32[]{:S(2)}, u32[]{:S(2)}) collective-permute-start(bf16[2,128,256]{2,1,0:T(8,128)(2,1)S(1)} %get-tuple-element.42), channel_id=1, source_target_pairs={{0,24},{4,28},{8,16},{12,20},{16,8},{20,12},{24,0},{28,4},{1,25},{... | collective-permute-start | bytes 393224 | tf_op jit(solution)/shard_map/groups/ppermute | solution.py:27
  61.0 1.2 %collective-permute-start.16 = (bf16[2,128,256]{2,1,0:T(8,128)(2,1)S(1)}, bf16[2,128,256]{2,1,0:T(8,128)(2,1)S(1)}, u32[]{:S(2)}, u32[]{:S(2)}) collective-permute-start(bf16[2,128,256]{2,1,0:T(8,128)(2,1)S(1)} %get-tuple-element.38), channel_id=1, source_target_pairs={{0,8},{4,12},{8,0},{12,4},{16,24},{20,28},{24,16},{28,20},{1,9},{5... | collective-permute-start | bytes 393224 | tf_op jit(solution)/shard_map/groups/ppermute | solution.py:27
  62.2 3.5 %collective-permute-done.15.refs_1_.refs_3_ = bf16[2,128,256]{2,1,0:T(8,128)(2,1)S(1)} collective-permute-done((bf16[2,128,256]{2,1,0:T(8,128)(2,1)S(1)}, bf16[2,128,256]{2,1,0:T(8,128)(2,1)S(1)}, u32[]{:S(2)}, u32[]{:S(2)}) %collective-permute-start.15) | collective-permute-done | bytes 131104 | tf_op jit(solution)/shard_map/spread_second/ppermute | solution.py:27
  65.7 0.7 collective-permute-start.14
  66.4 0.0 collective-permute-done.17.refs_4_.refs_5_
  66.4 0.0 collective-permute-done.18.refs_5_.refs_6_
  66.4 0.5 collective-permute-done.16.refs_3_.refs_4_
  66.9 0.0 collective-permute-done.12.refs_2_.refs_1_
  66.9 0.6 route.3
  67.5 1.3 %collective-permute-start.20 = (bf16[2,128,256]{2,1,0:T(8,128)(2,1)S(1)}, bf16[2,128,256]{2,1,0:T(8,128)(2,1)S(1)}, u32[]{:S(2)}, u32[]{:S(2)}) collective-permute-start(bf16[2,128,256]{2,1,0:T(8,128)(2,1)S(1)} %get-tuple-element.44), channel_id=1, source_target_pairs={{0,16},{4,20},{8,24},{12,28},{16,0},{20,4},{24,8},{28,12},{1,17},{... | collective-permute-start | bytes 393224 | tf_op jit(solution)/shard_map/groups/ppermute | solution.py:27
  68.8 1.4 %collective-permute-start.21 = (bf16[2,128,256]{2,1,0:T(8,128)(2,1)S(1)}, bf16[2,128,256]{2,1,0:T(8,128)(2,1)S(1)}, u32[]{:S(2)}, u32[]{:S(2)}) collective-permute-start(bf16[2,128,256]{2,1,0:T(8,128)(2,1)S(1)} %get-tuple-element.45), channel_id=1, source_target_pairs={{0,24},{4,28},{8,16},{12,20},{16,8},{20,12},{24,0},{28,4},{1,25},{... | collective-permute-start | bytes 393224 | tf_op jit(solution)/shard_map/groups/ppermute | solution.py:27
  70.2 0.9 collective-permute-start.19
  71.1 2.2 %collective-permute-done.14.refs_3_ = bf16[96,1024]{1,0:T(8,128)(2,1)S(1)} collective-permute-done((bf16[96,1024]{1,0:T(8,128)(2,1)S(1)}, bf16[96,1024]{1,0:T(8,128)(2,1)S(1)}, u32[]{:S(2)}, u32[]{:S(2)}) %collective-permute-start.14) | collective-permute-done | bytes 196640 | tf_op jit(solution)/shard_map/spread_first/ppermute | solution.py:27
  73.3 2.7 %first_down.1.initial = f32[128,1536]{1,0:T(8,128)S(1)} custom-call(s32[2]{0:T(128)S(1)} %pad_add_fusion.place, bf16[128,128]{1,0:T(8,128)(2,1)S(1)} %slice.4.notes, bf16[4096,1536]{1,0:T(8,128)(2,1)S(1)} %get-tuple-element.32.weight, bf16[96,1024]{1,0:T(8,128)(2,1)S(1)} %get-tuple-element.40.refs_0_, ...), custom_call_target="tpu_custom_call" | custom-call | tf_op jit(solution)/shard_map/first_down/pallas_call | solution.py:317
  76.1 0.0 collective-permute-done.19.refs_7_
  76.1 2.6 %second_down.1 = (f32[4,2,16,1536]{3,2,1,0:T(8,128)S(1)}, bf16[4,2,16,1536]{3,2,1,0:T(8,128)(2,1)S(1)}) custom-call(s32[2]{0:T(128)S(1)} %pad_add_fusion.place, s32[4]{0:T(128)S(1)} %copy-done, s32[4]{0:T(128)S(1)} %copy-done.1, bf16[128,128]{1,0:T(8,128)(2,1)S(1)} %slice.4.notes, bf16[4096,1536]{1,0:T(8,128)(2,1)S(1)} %get-tuple-element.32.weight, ...), custom_call_target="tpu_custom_call" | custom-call | tf_op jit(solution)/shard_map/second_down/pallas_call | solution.py:317
  78.7 0.1 collective-permute-start.22
  78.8 1.7 %collective-permute-done.22.theirs = bf16[4,2,16,1536]{3,2,1,0:T(8,128)(2,1)S(1)} collective-permute-done((bf16[4,2,16,1536]{3,2,1,0:T(8,128)(2,1)S(1)}, bf16[4,2,16,1536]{3,2,1,0:T(8,128)(2,1)S(1)}, u32[]{:S(2)}, u32[]{:S(2)}) %collective-permute-start.22) | collective-permute-done | bytes 393248 | tf_op jit(solution)/shard_map/cores/ppermute | solution.py:27
  80.5 0.1 cores.1
  80.6 1.0 %collective-permute-start.23 = (bf16[2,16,1536]{2,1,0:T(8,128)(2,1)S(1)}, bf16[2,16,1536]{2,1,0:T(8,128)(2,1)S(1)}, u32[]{:S(2)}, u32[]{:S(2)}) collective-permute-start(bf16[2,16,1536]{2,1,0:T(8,128)(2,1)S(1)} %get-tuple-element.49), channel_id=1, source_target_pairs={{0,8},{4,12},{8,0},{12,4},{16,24},{20,28},{24,16},{28,20},{1,9},{5... | collective-permute-start | bytes 294920 | tf_op jit(solution)/shard_map/chips/ppermute | solution.py:27
  81.5 1.2 %collective-permute-start.24 = (bf16[2,16,1536]{2,1,0:T(8,128)(2,1)S(1)}, bf16[2,16,1536]{2,1,0:T(8,128)(2,1)S(1)}, u32[]{:S(2)}, u32[]{:S(2)}) collective-permute-start(bf16[2,16,1536]{2,1,0:T(8,128)(2,1)S(1)} %get-tuple-element.50), channel_id=1, source_target_pairs={{0,16},{4,20},{8,24},{12,28},{16,0},{20,4},{24,8},{28,12},{1,17},{... | collective-permute-start | bytes 294920 | tf_op jit(solution)/shard_map/chips/ppermute | solution.py:27
  82.7 1.4 %collective-permute-start.25 = (bf16[2,16,1536]{2,1,0:T(8,128)(2,1)S(1)}, bf16[2,16,1536]{2,1,0:T(8,128)(2,1)S(1)}, u32[]{:S(2)}, u32[]{:S(2)}) collective-permute-start(bf16[2,16,1536]{2,1,0:T(8,128)(2,1)S(1)} %get-tuple-element.51), channel_id=1, source_target_pairs={{0,24},{4,28},{8,16},{12,20},{16,8},{20,12},{24,0},{28,4},{1,25},{... | collective-permute-start | bytes 294920 | tf_op jit(solution)/shard_map/chips/ppermute | solution.py:27
  84.1 1.7 %collective-permute-done.23.refs_0_ = bf16[2,16,1536]{2,1,0:T(8,128)(2,1)S(1)} collective-permute-done((bf16[2,16,1536]{2,1,0:T(8,128)(2,1)S(1)}, bf16[2,16,1536]{2,1,0:T(8,128)(2,1)S(1)}, u32[]{:S(2)}, u32[]{:S(2)}) %collective-permute-start.23) | collective-permute-done | bytes 98336 | tf_op jit(solution)/shard_map/chips/ppermute | solution.py:27
  85.8 1.7 %collective-permute-done.24.refs_1_ = bf16[2,16,1536]{2,1,0:T(8,128)(2,1)S(1)} collective-permute-done((bf16[2,16,1536]{2,1,0:T(8,128)(2,1)S(1)}, bf16[2,16,1536]{2,1,0:T(8,128)(2,1)S(1)}, u32[]{:S(2)}, u32[]{:S(2)}) %collective-permute-start.24) | collective-permute-done | bytes 98336 | tf_op jit(solution)/shard_map/chips/ppermute | solution.py:27
  87.6 0.7 collective-permute-done.25.refs_2_
  88.3 0.7 finish.1
  (23 shorter events, 0.2 us)
Async XLA Ops:
  0.6 11.4 %collective-permute-start.1 = (bf16[16,1536]{1,0:T(8,128)(2,1)}, bf16[16,1536]{1,0:T(8,128)(2,1)S(1)}, u32[]{:S(2)}, u32[]{:S(2)}) collective-permute-start(bf16[16,1536]{1,0:T(8,128)(2,1)} %param.8), channel_id=1, source_target_pairs={{0,2},{1,3},{2,0},{3,1},{4,6},{5,7},{6,4},{7,5},{8,10},{9,11},{10,... | collective-permute-start | bytes 147464 | tf_op jit(solution)/shard_map/gather_tokens/ppermute | solution.py:27
  4.7 7.3 %collective-permute-start = (bf16[16,1536]{1,0:T(8,128)(2,1)}, bf16[16,1536]{1,0:T(8,128)(2,1)S(1)}, u32[]{:S(2)}, u32[]{:S(2)}) collective-permute-start(bf16[16,1536]{1,0:T(8,128)(2,1)} %param.8), channel_id=1, source_target_pairs={{0,1},{1,0},{2,3},{3,2},{4,5},{5,4},{6,7},{7,6},{8,9},{9,8},{10,11... | collective-permute-start | bytes 147464 | tf_op jit(solution)/shard_map/gather_tokens/ppermute | solution.py:27
  6.3 6.1 %collective-permute-start.2 = (bf16[16,1536]{1,0:T(8,128)(2,1)}, bf16[16,1536]{1,0:T(8,128)(2,1)S(1)}, u32[]{:S(2)}, u32[]{:S(2)}) collective-permute-start(bf16[16,1536]{1,0:T(8,128)(2,1)} %param.8), channel_id=1, source_target_pairs={{0,3},{1,2},{2,1},{3,0},{4,7},{5,6},{6,5},{7,4},{8,11},{9,10},{10,... | collective-permute-start | bytes 147464 | tf_op jit(solution)/shard_map/gather_tokens/ppermute | solution.py:27
  6.4 5.3 %copy-start.2 = (s32[16,2]{0,1:T(2,128)S(1)}, s32[16,2]{0,1:T(2,128)}, u32[]{:S(2)}) copy-start(s32[16,2]{0,1:T(2,128)} %param.9) | copy-start | bytes 388
  6.4 5.3 %copy-start.3 = (s32[16,2]{0,1:T(2,128)S(1)}, s32[16,2]{0,1:T(2,128)}, u32[]{:S(2)}) copy-start(s32[16,2]{0,1:T(2,128)} %param.10) | copy-start | bytes 388
  6.4 5.6 %copy-start.4 = (bf16[16,1536]{1,0:T(8,128)(2,1)S(1)}, bf16[16,1536]{1,0:T(8,128)(2,1)}, u32[]{:S(2)}) copy-start(bf16[16,1536]{1,0:T(8,128)(2,1)} %param.8) | copy-start | bytes 147460
  12.4 9.5 %collective-permute-start.5 = (bf16[16,6272]{1,0:T(8,128)(2,1)S(1)}, bf16[16,6272]{1,0:T(8,128)(2,1)S(1)}, u32[]{:S(2)}, u32[]{:S(2)}) collective-permute-start(bf16[16,6272]{1,0:T(8,128)(2,1)S(1)} %get-tuple-element.52.refs_1_), channel_id=1, source_target_pairs={{0,24},{4,28},{8,16},{12,20},{16,8},{20,12},{24,0},{28,4},{1,25},{... | collective-permute-start | bytes 602120 | tf_op jit(solution)/shard_map/gather_tokens/ppermute | solution.py:27
  14.9 8.6 %collective-permute-start.4 = (bf16[16,6272]{1,0:T(8,128)(2,1)S(1)}, bf16[16,6272]{1,0:T(8,128)(2,1)S(1)}, u32[]{:S(2)}, u32[]{:S(2)}) collective-permute-start(bf16[16,6272]{1,0:T(8,128)(2,1)S(1)} %get-tuple-element.52.refs_1_), channel_id=1, source_target_pairs={{0,16},{4,20},{8,24},{12,28},{16,0},{20,4},{24,8},{28,12},{1,17},{... | collective-permute-start | bytes 602120 | tf_op jit(solution)/shard_map/gather_tokens/ppermute | solution.py:27
  15.4 8.2 %collective-permute-start.3 = (bf16[16,6272]{1,0:T(8,128)(2,1)S(1)}, bf16[16,6272]{1,0:T(8,128)(2,1)S(1)}, u32[]{:S(2)}, u32[]{:S(2)}) collective-permute-start(bf16[16,6272]{1,0:T(8,128)(2,1)S(1)} %get-tuple-element.52.refs_1_), channel_id=1, source_target_pairs={{0,8},{4,12},{8,0},{12,4},{16,24},{20,28},{24,16},{28,20},{1,9},{5... | collective-permute-start | bytes 602120 | tf_op jit(solution)/shard_map/gather_tokens/ppermute | solution.py:27
  23.7 2.4 %collective-permute-start.6 = (bf16[64,6272]{1,0:T(8,128)(2,1)S(1)}, bf16[64,6272]{1,0:T(8,128)(2,1)S(1)}, u32[]{:S(2)}, u32[]{:S(2)}) collective-permute-start(bf16[64,6272]{1,0:T(8,128)(2,1)S(1)} %pad_maximum_fusion), channel_id=1, source_target_pairs={{0,4},{4,0},{8,12},{12,8},{16,20},{20,16},{24,28},{28,24},{1,5},{5... | collective-permute-start | bytes 2408456 | tf_op jit(solution)/shard_map/gather_tokens/ppermute | solution.py:27
  34.9 12.1 %collective-permute-start.10 = (bf16[96,1024]{1,0:T(8,128)(2,1)S(1)}, bf16[96,1024]{1,0:T(8,128)(2,1)S(1)}, u32[]{:S(2)}, u32[]{:S(2)}) collective-permute-start(bf16[96,1024]{1,0:T(8,128)(2,1)S(1)} %get-tuple-element.40.refs_0_), channel_id=1, source_target_pairs={{0,2},{1,3},{2,0},{3,1},{4,6},{5,7},{6,4},{7,5},{8,10},{9,11},{10,... | collective-permute-start | bytes 589832 | tf_op jit(solution)/shard_map/spread_first/ppermute | solution.py:27
  36.6 8.2 %collective-permute-start.7 = (bf16[2,256,128]{2,1,0:T(8,128)(2,1)S(1)}, bf16[2,256,128]{2,1,0:T(8,128)(2,1)S(1)}, u32[]{:S(2)}, u32[]{:S(2)}) collective-permute-start(bf16[2,256,128]{2,1,0:T(8,128)(2,1)S(1)} %get-tuple-element.34), channel_id=1, source_target_pairs={{0,8},{4,12},{8,0},{12,4},{16,24},{20,28},{24,16},{28,20},{1,9},{5... | collective-permute-start | bytes 393224 | tf_op jit(solution)/shard_map/peers/ppermute | solution.py:27
  38.1 7.8 %collective-permute-start.8 = (bf16[2,256,128]{2,1,0:T(8,128)(2,1)S(1)}, bf16[2,256,128]{2,1,0:T(8,128)(2,1)S(1)}, u32[]{:S(2)}, u32[]{:S(2)}) collective-permute-start(bf16[2,256,128]{2,1,0:T(8,128)(2,1)S(1)} %get-tuple-element.35), channel_id=1, source_target_pairs={{0,16},{4,20},{8,24},{12,28},{16,0},{20,4},{24,8},{28,12},{1,17},{... | collective-permute-start | bytes 393224 | tf_op jit(solution)/shard_map/peers/ppermute | solution.py:27
  38.8 8.2 %copy-start = (s32[4]{0:T(128)S(1)}, s32[4]{0:T(128)}, u32[]{:S(2)}) copy-start(s32[4]{0:T(128)} %labels.7) | copy-start | bytes 52
  38.8 8.2 %copy-start.1 = (s32[4]{0:T(128)S(1)}, s32[4]{0:T(128)}, u32[]{:S(2)}) copy-start(s32[4]{0:T(128)} %freq.3) | copy-start | bytes 52
  38.8 7.1 %collective-permute-start.9 = (bf16[2,256,128]{2,1,0:T(8,128)(2,1)S(1)}, bf16[2,256,128]{2,1,0:T(8,128)(2,1)S(1)}, u32[]{:S(2)}, u32[]{:S(2)}) collective-permute-start(bf16[2,256,128]{2,1,0:T(8,128)(2,1)S(1)} %get-tuple-element.36), channel_id=1, source_target_pairs={{0,24},{4,28},{8,16},{12,20},{16,8},{20,12},{24,0},{28,4},{1,25},{... | collective-permute-start | bytes 393224 | tf_op jit(solution)/shard_map/peers/ppermute | solution.py:27
  48.0 7.3 %collective-permute-start.11 = (bf16[2,128,256]{2,1,0:T(8,128)(2,1)S(1)}, bf16[2,128,256]{2,1,0:T(8,128)(2,1)S(1)}, u32[]{:S(2)}, u32[]{:S(2)}) collective-permute-start(bf16[2,128,256]{2,1,0:T(8,128)(2,1)S(1)} %merge.1.refs_0_), channel_id=1, source_target_pairs={{0,1},{1,0},{2,3},{3,2},{4,5},{5,4},{6,7},{7,6},{8,9},{9,8},{10,11... | collective-permute-start | bytes 393224 | tf_op jit(solution)/shard_map/spread_second/ppermute | solution.py:27
  49.4 11.6 %collective-permute-start.13 = (bf16[2,128,256]{2,1,0:T(8,128)(2,1)S(1)}, bf16[2,128,256]{2,1,0:T(8,128)(2,1)S(1)}, u32[]{:S(2)}, u32[]{:S(2)}) collective-permute-start(bf16[2,128,256]{2,1,0:T(8,128)(2,1)S(1)} %merge.1.refs_0_), channel_id=1, source_target_pairs={{0,2},{1,3},{2,0},{3,1},{4,6},{5,7},{6,4},{7,5},{8,10},{9,11},{10,... | collective-permute-start | bytes 393224 | tf_op jit(solution)/shard_map/spread_second/ppermute | solution.py:27
  55.9 11.1 %collective-permute-start.12 = (bf16[96,1024]{1,0:T(8,128)(2,1)S(1)}, bf16[96,1024]{1,0:T(8,128)(2,1)S(1)}, u32[]{:S(2)}, u32[]{:S(2)}) collective-permute-start(bf16[96,1024]{1,0:T(8,128)(2,1)S(1)} %get-tuple-element.40.refs_0_), channel_id=1, source_target_pairs={{0,1},{1,0},{2,3},{3,2},{4,5},{5,4},{6,7},{7,6},{8,9},{9,8},{10,11... | collective-permute-start | bytes 589832 | tf_op jit(solution)/shard_map/spread_first/ppermute | solution.py:27
  56.0 9.7 %collective-permute-start.15 = (bf16[2,128,256]{2,1,0:T(8,128)(2,1)S(1)}, bf16[2,128,256]{2,1,0:T(8,128)(2,1)S(1)}, u32[]{:S(2)}, u32[]{:S(2)}) collective-permute-start(bf16[2,128,256]{2,1,0:T(8,128)(2,1)S(1)} %merge.1.refs_0_), channel_id=1, source_target_pairs={{0,3},{1,2},{2,1},{3,0},{4,7},{5,6},{6,5},{7,4},{8,11},{9,10},{10,... | collective-permute-start | bytes 393224 | tf_op jit(solution)/shard_map/spread_second/ppermute | solution.py:27
  58.7 7.7 %collective-permute-start.17 = (bf16[2,128,256]{2,1,0:T(8,128)(2,1)S(1)}, bf16[2,128,256]{2,1,0:T(8,128)(2,1)S(1)}, u32[]{:S(2)}, u32[]{:S(2)}) collective-permute-start(bf16[2,128,256]{2,1,0:T(8,128)(2,1)S(1)} %get-tuple-element.41), channel_id=1, source_target_pairs={{0,16},{4,20},{8,24},{12,28},{16,0},{20,4},{24,8},{28,12},{1,17},{... | collective-permute-start | bytes 393224 | tf_op jit(solution)/shard_map/groups/ppermute | solution.py:27
  59.5 6.8 %collective-permute-start.18 = (bf16[2,128,256]{2,1,0:T(8,128)(2,1)S(1)}, bf16[2,128,256]{2,1,0:T(8,128)(2,1)S(1)}, u32[]{:S(2)}, u32[]{:S(2)}) collective-permute-start(bf16[2,128,256]{2,1,0:T(8,128)(2,1)S(1)} %get-tuple-element.42), channel_id=1, source_target_pairs={{0,24},{4,28},{8,16},{12,20},{16,8},{20,12},{24,0},{28,4},{1,25},{... | collective-permute-start | bytes 393224 | tf_op jit(solution)/shard_map/groups/ppermute | solution.py:27
  61.0 5.9 %collective-permute-start.16 = (bf16[2,128,256]{2,1,0:T(8,128)(2,1)S(1)}, bf16[2,128,256]{2,1,0:T(8,128)(2,1)S(1)}, u32[]{:S(2)}, u32[]{:S(2)}) collective-permute-start(bf16[2,128,256]{2,1,0:T(8,128)(2,1)S(1)} %get-tuple-element.38), channel_id=1, source_target_pairs={{0,8},{4,12},{8,0},{12,4},{16,24},{20,28},{24,16},{28,20},{1,9},{5... | collective-permute-start | bytes 393224 | tf_op jit(solution)/shard_map/groups/ppermute | solution.py:27
  65.7 7.6 %collective-permute-start.14 = (bf16[96,1024]{1,0:T(8,128)(2,1)S(1)}, bf16[96,1024]{1,0:T(8,128)(2,1)S(1)}, u32[]{:S(2)}, u32[]{:S(2)}) collective-permute-start(bf16[96,1024]{1,0:T(8,128)(2,1)S(1)} %get-tuple-element.40.refs_0_), channel_id=1, source_target_pairs={{0,3},{1,2},{2,1},{3,0},{4,7},{5,6},{6,5},{7,4},{8,11},{9,10},{10,... | collective-permute-start | bytes 589832 | tf_op jit(solution)/shard_map/spread_first/ppermute | solution.py:27
  67.5 8.5 %collective-permute-start.20 = (bf16[2,128,256]{2,1,0:T(8,128)(2,1)S(1)}, bf16[2,128,256]{2,1,0:T(8,128)(2,1)S(1)}, u32[]{:S(2)}, u32[]{:S(2)}) collective-permute-start(bf16[2,128,256]{2,1,0:T(8,128)(2,1)S(1)} %get-tuple-element.44), channel_id=1, source_target_pairs={{0,16},{4,20},{8,24},{12,28},{16,0},{20,4},{24,8},{28,12},{1,17},{... | collective-permute-start | bytes 393224 | tf_op jit(solution)/shard_map/groups/ppermute | solution.py:27
  68.8 7.2 %collective-permute-start.21 = (bf16[2,128,256]{2,1,0:T(8,128)(2,1)S(1)}, bf16[2,128,256]{2,1,0:T(8,128)(2,1)S(1)}, u32[]{:S(2)}, u32[]{:S(2)}) collective-permute-start(bf16[2,128,256]{2,1,0:T(8,128)(2,1)S(1)} %get-tuple-element.45), channel_id=1, source_target_pairs={{0,24},{4,28},{8,16},{12,20},{16,8},{20,12},{24,0},{28,4},{1,25},{... | collective-permute-start | bytes 393224 | tf_op jit(solution)/shard_map/groups/ppermute | solution.py:27
  70.2 5.9 %collective-permute-start.19 = (bf16[2,128,256]{2,1,0:T(8,128)(2,1)S(1)}, bf16[2,128,256]{2,1,0:T(8,128)(2,1)S(1)}, u32[]{:S(2)}, u32[]{:S(2)}) collective-permute-start(bf16[2,128,256]{2,1,0:T(8,128)(2,1)S(1)} %get-tuple-element.43.refs_4_), channel_id=1, source_target_pairs={{0,8},{4,12},{8,0},{12,4},{16,24},{20,28},{24,16},{28,20},{1,9},{5... | collective-permute-start | bytes 393224 | tf_op jit(solution)/shard_map/groups/ppermute | solution.py:27
  78.7 1.8 %collective-permute-start.22 = (bf16[4,2,16,1536]{3,2,1,0:T(8,128)(2,1)S(1)}, bf16[4,2,16,1536]{3,2,1,0:T(8,128)(2,1)S(1)}, u32[]{:S(2)}, u32[]{:S(2)}) collective-permute-start(bf16[4,2,16,1536]{3,2,1,0:T(8,128)(2,1)S(1)} %get-tuple-element.47), channel_id=1, source_target_pairs={{0,4},{4,0},{8,12},{12,8},{16,20},{20,16},{24,28},{28,24},{1,5},{5... | collective-permute-start | bytes 1179656 | tf_op jit(solution)/shard_map/cores/ppermute | solution.py:27
  80.6 5.2 %collective-permute-start.23 = (bf16[2,16,1536]{2,1,0:T(8,128)(2,1)S(1)}, bf16[2,16,1536]{2,1,0:T(8,128)(2,1)S(1)}, u32[]{:S(2)}, u32[]{:S(2)}) collective-permute-start(bf16[2,16,1536]{2,1,0:T(8,128)(2,1)S(1)} %get-tuple-element.49), channel_id=1, source_target_pairs={{0,8},{4,12},{8,0},{12,4},{16,24},{20,28},{24,16},{28,20},{1,9},{5... | collective-permute-start | bytes 294920 | tf_op jit(solution)/shard_map/chips/ppermute | solution.py:27
  81.5 6.0 %collective-permute-start.24 = (bf16[2,16,1536]{2,1,0:T(8,128)(2,1)S(1)}, bf16[2,16,1536]{2,1,0:T(8,128)(2,1)S(1)}, u32[]{:S(2)}, u32[]{:S(2)}) collective-permute-start(bf16[2,16,1536]{2,1,0:T(8,128)(2,1)S(1)} %get-tuple-element.50), channel_id=1, source_target_pairs={{0,16},{4,20},{8,24},{12,28},{16,0},{20,4},{24,8},{28,12},{1,17},{... | collective-permute-start | bytes 294920 | tf_op jit(solution)/shard_map/chips/ppermute | solution.py:27
  82.7 5.6 %collective-permute-start.25 = (bf16[2,16,1536]{2,1,0:T(8,128)(2,1)S(1)}, bf16[2,16,1536]{2,1,0:T(8,128)(2,1)S(1)}, u32[]{:S(2)}, u32[]{:S(2)}) collective-permute-start(bf16[2,16,1536]{2,1,0:T(8,128)(2,1)S(1)} %get-tuple-element.51), channel_id=1, source_target_pairs={{0,24},{4,28},{8,16},{12,20},{16,8},{20,12},{24,0},{28,4},{1,25},{... | collective-permute-start | bytes 294920 | tf_op jit(solution)/shard_map/chips/ppermute | solution.py:27
